TPU v7x, 32 devices: a whole 2x2x4 slice. The times are simulated.
32 devices in a mesh: seq: 4 (over y, x), fsdp: 8 (over z, core).
Axes of the slice: x: 2, y: 2, z: 4, core: 2. Of those that a mesh axis runs over, the one named last changes fastest.
Arguments:
- token_ids: int32 [2, 8, 1024], P(None, 'fsdp', 'seq'), may hold values from 0 to 32127
- lengths: int32 [2, 8], P(None, 'fsdp'), may hold values from 683 to 1024, as said below
- routes: int32 [2, 8, 1024, 1], P(None, 'fsdp', 'seq'), may hold values from 0 to 3; in each aligned block of 256 rows (0 to 255, 256 to 511, ..., all dimensions but the last counted through in order) at most 96 rows name the same one
- positions: int32 [2, 8, 128], P(None, 'fsdp', 'seq'), may hold values from 0 to 255
- targets: int32 [2, 8, 128], P(None, 'fsdp', 'seq'), may hold values from 0 to 32127
- teacher_index: int32 [2, 8, 128, 64], P(None, 'fsdp', 'seq'), may hold values from 0 to 32127, as said below
- teacher_weight: float32 [2, 8, 128, 64], P(None, 'fsdp', 'seq'), may hold values from 0.001 to 1
- buckets: int32 [2047], replicated, may hold values from 0 to 31
- embed_weight: float32 [32128, 768], P('fsdp'), may hold values from -6 to 6
- embed_mean: float32 [32128, 768], P('fsdp'), may hold values from -7.6293945e-05 to 7.6293945e-05
- embed_square: float32 [32128, 768], P('fsdp'), may hold values from 1.4891505e-11 to 5.956602e-11
- attend_weight: float32 [2, 768, 2304], P(None, 'fsdp'), may hold values from -0.21875 to 0.21875
- attend_mean: float32 [2, 768, 2304], P(None, 'fsdp'), may hold values from -7.6293945e-05 to 7.6293945e-05
- attend_square: float32 [2, 768, 2304], P(None, 'fsdp'), may hold values from 1.4891505e-11 to 5.956602e-11
- output_weight: float32 [2, 768, 768], P(None, 'fsdp'), may hold values from -2.5 to 2.5
- output_mean: float32 [2, 768, 768], P(None, 'fsdp'), may hold values from -7.6293945e-05 to 7.6293945e-05
- output_square: float32 [2, 768, 768], P(None, 'fsdp'), may hold values from 1.4891505e-11 to 5.956602e-11
- upward_weight: float32 [2, 4, 768, 3072], P(None, None, 'fsdp'), may hold values from -0.21875 to 0.21875
- upward_mean: float32 [2, 4, 768, 3072], P(None, None, 'fsdp'), may hold values from -7.6293945e-05 to 7.6293945e-05
- upward_square: float32 [2, 4, 768, 3072], P(None, None, 'fsdp'), may hold values from 3.722876e-12 to 1.4891505e-11
- downward_weight: float32 [2, 4, 3072, 768], P(None, None, 'fsdp'), may hold values from -0.3125 to 0.3125
- downward_mean: float32 [2, 4, 3072, 768], P(None, None, 'fsdp'), may hold values from -7.6293945e-05 to 7.6293945e-05
- downward_square: float32 [2, 4, 3072, 768], P(None, None, 'fsdp'), may hold values from 3.722876e-12 to 1.4891505e-11
- router_weight: float32 [2, 768, 4], P(None, 'fsdp'), may hold values from -0.15625 to 0.15625
- router_mean: float32 [2, 768, 4], P(None, 'fsdp'), may hold values from -7.6293945e-05 to 7.6293945e-05
- router_square: float32 [2, 768, 4], P(None, 'fsdp'), may hold values from 1.4891505e-11 to 5.956602e-11
- gains_weight: float32 [5, 768], P(None, 'fsdp'), may hold values from 0.5 to 1.5
- gains_mean: float32 [5, 768], P(None, 'fsdp'), may hold values from -7.6293945e-05 to 7.6293945e-05
- gains_square: float32 [5, 768], P(None, 'fsdp'), may hold values from 1.4891504e-09 to 5.9566014e-09
- bias_weight: float32 [2, 384], P(None, 'fsdp'), may hold values from -6 to 6
- bias_mean: float32 [2, 384], P(None, 'fsdp'), may hold values from -7.6293945e-05 to 7.6293945e-05
- bias_square: float32 [2, 384], P(None, 'fsdp'), may hold values from 1.4891505e-11 to 5.956602e-11
Outputs:
- loss_sum: float32 [], replicated
- loss_count: float32 [], replicated
- grad_norm: float32 [], replicated
- embed_weight_next: float32 [32128, 768], P('fsdp')
- embed_mean_next: float32 [32128, 768], P('fsdp')
- embed_square_next: float32 [32128, 768], P('fsdp')
- attend_weight_next: float32 [2, 768, 2304], P(None, 'fsdp')
- attend_mean_next: float32 [2, 768, 2304], P(None, 'fsdp')
- attend_square_next: float32 [2, 768, 2304], P(None, 'fsdp')
- output_weight_next: float32 [2, 768, 768], P(None, 'fsdp')
- output_mean_next: float32 [2, 768, 768], P(None, 'fsdp')
- output_square_next: float32 [2, 768, 768], P(None, 'fsdp')
- upward_weight_next: float32 [2, 4, 768, 3072], P(None, None, 'fsdp')
- upward_mean_next: float32 [2, 4, 768, 3072], P(None, None, 'fsdp')
- upward_square_next: float32 [2, 4, 768, 3072], P(None, None, 'fsdp')
- downward_weight_next: float32 [2, 4, 3072, 768], P(None, None, 'fsdp')
- downward_mean_next: float32 [2, 4, 3072, 768], P(None, None, 'fsdp')
- downward_square_next: float32 [2, 4, 3072, 768], P(None, None, 'fsdp')
- router_weight_next: float32 [2, 768, 4], P(None, 'fsdp')
- router_mean_next: float32 [2, 768, 4], P(None, 'fsdp')
- router_square_next: float32 [2, 768, 4], P(None, 'fsdp')
- gains_weight_next: float32 [5, 768], P(None, 'fsdp')
- gains_mean_next: float32 [5, 768], P(None, 'fsdp')
- gains_square_next: float32 [5, 768], P(None, 'fsdp')
- bias_weight_next: float32 [2, 384], P(None, 'fsdp')
- bias_mean_next: float32 [2, 384], P(None, 'fsdp')
- bias_square_next: float32 [2, 384], P(None, 'fsdp')
Inputs may be any that keep to these rules, and one draw needn't show every extreme that they name: `lengths`: in every micro-batch one sequence has length 1024. `routes`: in every aligned block of 256 rows (the rows of one device) no expert is named more than 96 times. `positions`: entries j * 32 to j * 32 + 31 of a row index block j of 256 tokens. `teacher_index`: the 64 entries of a row differ.
All inputs are finite; a program needn't handle non-finite values.
Results may differ from a plain program's by a relative error of at most 0.018.
The roundings to bfloat16 on the way count: a program that leaves them out, or rounds other values in their place, can miss the bound.
Values may be sent and summed in bfloat16 or wider, within the bound.
No kernel may reach another device: no remote copies, remote signals or barrier semaphores. Data moves between devices by JAX's collectives and lax.ppermute only.
A program may use at most 1.125 GiB of HBM per device.

v0:
```python
import jax
import jax.numpy as jnp
from jax import lax
from jax.sharding import PartitionSpec as P

H = 12
HD = 64
STEP_COUNT = 10


EPSILON = 1e-06
ADAM_EPSILON = 1e-08
BETA_ONE = 0.9
BETA_TWO = 0.999
WEIGHT_DECAY = 0.01
CLIP_NORM = 1.0
STEP_RATES = (0.5, 0.03, 0.3, 0.03, 0.04, 0.02, 0.9, 0.5)
HIGHEST_PRECISION = lax.Precision.HIGHEST


def matmul(left_side, right_side):
    return jnp.dot(left_side, right_side, preferred_element_type=jnp.float32)


def rms_norm(hidden, gain):
    norm_scale = lax.rsqrt(jnp.mean(hidden * hidden, -1, keepdims=True) + EPSILON)
    return (hidden * norm_scale * gain, norm_scale)


def rms_back(hidden, norm_scale, gain, upstream):
    normed = hidden * norm_scale
    grad_normed = upstream * gain
    grad_gain = jnp.sum(upstream * normed, 0)
    grad_hidden = norm_scale * (
        grad_normed - normed * jnp.mean(grad_normed * normed, -1, keepdims=True)
    )
    return (grad_hidden, grad_gain)


def split_heads(matrix):
    return matrix.reshape(matrix.shape[0], -1, HD).transpose(1, 0, 2)


def join_heads(tensor):
    return tensor.transpose(1, 0, 2).reshape(tensor.shape[1], -1)


def relative_rows(buckets, table):
    onehot = (buckets[:, None] == jnp.arange(table.shape[0])[None, :]).astype(jnp.float32)
    return (jnp.dot(onehot, table, precision=HIGHEST_PRECISION).T, onehot)


def skew_bias(relative, block_start, block_size, total_rows):
    head_count = relative.shape[0]
    width = total_rows + block_size
    window = lax.dynamic_slice_in_dim(relative, total_rows - block_start - block_size, width - 1, 1)
    padded = jnp.concatenate([window, jnp.zeros((head_count, 1), relative.dtype)], 1)
    tiled = jnp.tile(padded, (1, block_size + 1))[:, : block_size * (width + 1)]
    rows = tiled.reshape(head_count, block_size, width + 1)[:, :, :total_rows]
    return rows[:, ::-1, :]


def skew_sum(grad_scores, block_start, grad_relative):
    head_count, block_size, total_rows = grad_scores.shape
    width = total_rows + block_size
    flipped = grad_scores[:, ::-1, :]
    padded = jnp.concatenate(
        [flipped, jnp.zeros((head_count, block_size, width + 1 - total_rows), jnp.float32)], 2
    )
    flat = padded.reshape(head_count, block_size * (width + 1))
    flat = jnp.concatenate(
        [
            flat,
            jnp.zeros(
                (head_count, (block_size + 1) * width - block_size * (width + 1)), jnp.float32
            ),
        ],
        1,
    )
    diagonal = jnp.sum(flat.reshape(head_count, block_size + 1, width), 1)[:, : width - 1]
    window_start = total_rows - block_start - block_size
    current = lax.dynamic_slice_in_dim(grad_relative, window_start, width - 1, 1)
    return lax.dynamic_update_slice_in_dim(grad_relative, current + diagonal, window_start, 1)


def block_scores(query_h, key_h, relative, block_start, block_size, seq_length):
    query_block = lax.dynamic_slice_in_dim(query_h, block_start, block_size, 1)
    raw_scores = jnp.einsum("hqd,hkd->hqk", query_block, key_h, preferred_element_type=jnp.float32)
    total_rows = key_h.shape[1]
    col_ids = jnp.arange(total_rows)
    scores = raw_scores * query_h.shape[2] ** (-0.5) + skew_bias(
        relative, block_start, block_size, total_rows
    )
    scores = jnp.where((col_ids < seq_length)[None, None, :], scores, -1e30)
    return (scores, query_block)


def attend(query_h, key_h, value_h, relative, seq_length):
    head_count, total_rows, head_dim = query_h.shape
    block_size = min(512, total_rows)

    def block_step(block_index):
        scores, query_block = block_scores(
            query_h, key_h, relative, block_index * block_size, block_size, seq_length
        )
        row_peak = jnp.max(scores, -1, keepdims=True)
        exp_scores = jnp.exp(scores - row_peak)
        exp_total = jnp.sum(exp_scores, -1, keepdims=True)
        weights = (exp_scores / exp_total).astype(jnp.bfloat16)
        mixed_block = jnp.einsum(
            "hqk,hkd->hqd", weights, value_h, preferred_element_type=jnp.float32
        )
        return (mixed_block.astype(jnp.bfloat16), (row_peak + jnp.log(exp_total))[..., 0])

    mixed_heads, logsum = lax.map(block_step, jnp.arange(total_rows // block_size))
    mixed_heads = mixed_heads.transpose(1, 0, 2, 3).reshape(head_count, total_rows, head_dim)
    return (mixed_heads, logsum.transpose(1, 0, 2).reshape(head_count, total_rows))


def attend_back(query_h, key_h, value_h, relative, seq_length, logsum, grad_mixed):
    head_count, total_rows, head_dim = query_h.shape
    block_size = min(512, total_rows)
    factor = head_dim ** (-0.5)

    def block_step(carried, block_index):
        grad_key, grad_value, grad_relative = carried
        block_start = block_index * block_size
        scores, query_block = block_scores(
            query_h, key_h, relative, block_start, block_size, seq_length
        )
        kept_sum = lax.dynamic_slice_in_dim(logsum, block_start, block_size, 1)
        weights = jnp.exp(scores - kept_sum[..., None])
        grad_block = lax.dynamic_slice_in_dim(grad_mixed, block_start, block_size, 1)
        grad_weights = jnp.einsum(
            "hqd,hkd->hqk", grad_block, value_h, preferred_element_type=jnp.float32
        )
        grad_scores = (
            weights * (grad_weights - jnp.sum(weights * grad_weights, -1, keepdims=True))
        ).astype(jnp.bfloat16)
        grad_query = (
            jnp.einsum("hqk,hkd->hqd", grad_scores, key_h, preferred_element_type=jnp.float32)
            * factor
        )
        grad_key = (
            grad_key
            + jnp.einsum(
                "hqk,hqd->hkd", grad_scores, query_block, preferred_element_type=jnp.float32
            )
            * factor
        )
        grad_value = grad_value + jnp.einsum(
            "hqk,hqd->hkd",
            weights.astype(jnp.bfloat16),
            grad_block,
            preferred_element_type=jnp.float32,
        )
        grad_relative = skew_sum(grad_scores.astype(jnp.float32), block_start, grad_relative)
        return ((grad_key, grad_value, grad_relative), grad_query)

    start_state = (
        jnp.zeros(key_h.shape, jnp.float32),
        jnp.zeros(value_h.shape, jnp.float32),
        jnp.zeros((head_count, 2 * total_rows - 1), jnp.float32),
    )
    (grad_key, grad_value, grad_relative), grad_query = lax.scan(
        block_step, start_state, jnp.arange(total_rows // block_size)
    )
    grad_query = grad_query.transpose(1, 0, 2, 3).reshape(head_count, total_rows, head_dim)
    return (grad_query, grad_key, grad_value, grad_relative)


def layer_forward(hidden, gathered, gain_one, gain_two, router_w, relative, route_ids, seq_length):
    attend_w, output_w, upward_w, downward_w = gathered
    model_width = hidden.shape[1]
    normed_one, scale_one = rms_norm(hidden, gain_one)
    normed_one = normed_one.astype(jnp.bfloat16)
    projected = matmul(normed_one, attend_w).astype(jnp.bfloat16)
    query_t = projected[:, :model_width]
    key_t = projected[:, model_width : 2 * model_width]
    value_t = projected[:, 2 * model_width :]
    query_s, key_s, value_s = (
        lax.all_to_all(query_t, "seq", split_axis=1, concat_axis=0, tiled=True),
        lax.all_to_all(key_t, "seq", split_axis=1, concat_axis=0, tiled=True),
        lax.all_to_all(value_t, "seq", split_axis=1, concat_axis=0, tiled=True),
    )
    query_h, key_h, value_h = (split_heads(query_s), split_heads(key_s), split_heads(value_s))
    mixed_heads, logsum = attend(query_h, key_h, value_h, relative, seq_length)
    mixed_tok = lax.all_to_all(
        join_heads(mixed_heads), "seq", split_axis=0, concat_axis=1, tiled=True
    )
    after_attn = hidden + matmul(mixed_tok, output_w)
    normed_two, scale_two = rms_norm(after_attn, gain_two)
    normed_two = normed_two.astype(jnp.bfloat16)
    router_probs = jax.nn.softmax(matmul(normed_two, router_w), -1)
    experts = router_w.shape[1]
    onehot = (route_ids[:, None] == jnp.arange(experts)[None, :]).astype(jnp.float32)
    gate_value = jnp.sum(router_probs * onehot, -1)
    capacity = hidden.shape[0] * 3 // 8
    slot_ranks = jnp.sum((jnp.cumsum(onehot, 0) - 1.0) * onehot, -1).astype(jnp.int32)
    slot_index = route_ids * capacity + slot_ranks
    dispatch = (slot_index[None, :] == jnp.arange(experts * capacity)[:, None]).astype(jnp.bfloat16)
    expert_rows = (
        matmul(dispatch, normed_two).astype(jnp.bfloat16).reshape(experts, capacity, model_width)
    )
    upward = jnp.einsum("ecd,edf->ecf", expert_rows, upward_w, preferred_element_type=jnp.float32)
    activated = jax.nn.gelu(upward).astype(jnp.bfloat16)
    expert_out = jnp.einsum(
        "ecf,efd->ecd", activated, downward_w, preferred_element_type=jnp.float32
    )
    token_out = expert_out.reshape(experts * capacity, model_width)[slot_index]
    result = after_attn + gate_value[:, None] * token_out
    kept_state = (
        hidden,
        scale_one,
        normed_one,
        query_h,
        key_h,
        value_h,
        logsum,
        mixed_tok,
        after_attn,
        scale_two,
        normed_two,
        router_probs,
        onehot,
        gate_value,
        slot_index,
        dispatch,
        expert_rows,
        upward,
        activated,
        token_out,
    )
    return (result, kept_state)


def layer_backward(
    grad_out,
    kept_state,
    gathered,
    gain_one,
    gain_two,
    router_w,
    relative,
    onehot_buckets,
    seq_length,
):
    (
        hidden,
        scale_one,
        normed_one,
        query_h,
        key_h,
        value_h,
        logsum,
        mixed_tok,
        after_attn,
        scale_two,
        normed_two,
        router_probs,
        onehot,
        gate_value,
        slot_index,
        dispatch,
        expert_rows,
        upward,
        activated,
        token_out,
    ) = kept_state
    attend_w, output_w, upward_w, downward_w = gathered
    experts, capacity, model_width = expert_rows.shape
    grad_gate = jnp.sum(grad_out * token_out, -1)
    grad_token = (gate_value[:, None] * grad_out).astype(jnp.bfloat16)
    grad_expert = (
        matmul(dispatch, grad_token).astype(jnp.bfloat16).reshape(experts, capacity, model_width)
    )
    grad_downward = jnp.einsum(
        "ecf,ecd->efd", activated, grad_expert, preferred_element_type=jnp.float32
    )
    grad_activated = jnp.einsum(
        "ecd,efd->ecf", grad_expert, downward_w, preferred_element_type=jnp.float32
    )
    grad_upward = jax.vjp(jax.nn.gelu, upward)[1](grad_activated)[0].astype(jnp.bfloat16)
    grad_upweight = jnp.einsum(
        "ecd,ecf->edf", expert_rows, grad_upward, preferred_element_type=jnp.float32
    )
    grad_rows = jnp.einsum(
        "ecf,edf->ecd", grad_upward, upward_w, preferred_element_type=jnp.float32
    )
    grad_normed = grad_rows.reshape(experts * capacity, model_width)[slot_index]
    grad_probs = onehot * grad_gate[:, None]
    grad_logits = (
        router_probs * (grad_probs - jnp.sum(grad_probs * router_probs, -1, keepdims=True))
    ).astype(jnp.bfloat16)
    grad_router = matmul(normed_two.T, grad_logits)
    grad_normed = grad_normed + matmul(grad_logits, router_w.T)
    grad_mid, grad_gain_two = rms_back(after_attn, scale_two, gain_two, grad_normed)
    grad_mid = grad_mid + grad_out
    grad_attn = grad_mid.astype(jnp.bfloat16)
    grad_output = matmul(mixed_tok.T, grad_attn)
    grad_mixed = matmul(grad_attn, output_w.T).astype(jnp.bfloat16)
    grad_heads_in = lax.all_to_all(grad_mixed, "seq", split_axis=1, concat_axis=0, tiled=True)
    grad_query, grad_key, grad_value, grad_relative = attend_back(
        query_h, key_h, value_h, relative, seq_length, logsum, split_heads(grad_heads_in)
    )
    grad_parts = (
        lax.all_to_all(
            join_heads(grad_query).astype(jnp.bfloat16),
            "seq",
            split_axis=0,
            concat_axis=1,
            tiled=True,
        ),
        lax.all_to_all(
            join_heads(grad_key).astype(jnp.bfloat16),
            "seq",
            split_axis=0,
            concat_axis=1,
            tiled=True,
        ),
        lax.all_to_all(
            join_heads(grad_value).astype(jnp.bfloat16),
            "seq",
            split_axis=0,
            concat_axis=1,
            tiled=True,
        ),
    )
    grad_projected = jnp.concatenate(grad_parts, 1)
    grad_attend = matmul(normed_one.T, grad_projected)
    grad_first, grad_gain_one = rms_back(
        hidden, scale_one, gain_one, matmul(grad_projected, attend_w.T)
    )
    grad_table = jnp.dot(onehot_buckets.T, grad_relative.T, precision=HIGHEST_PRECISION)
    return (
        grad_mid + grad_first,
        (grad_attend, grad_output, grad_upweight, grad_downward),
        grad_gain_one,
        grad_gain_two,
        grad_router,
        grad_table,
    )


def adam_update(weight, grad, first, second, rate):
    first = BETA_ONE * first + (1.0 - BETA_ONE) * grad
    second = BETA_TWO * second + (1.0 - BETA_TWO) * grad * grad
    mean_hat = first / (1.0 - BETA_ONE**STEP_COUNT)
    square_hat = second / (1.0 - BETA_TWO**STEP_COUNT)
    weight = weight - rate * (
        mean_hat / (jnp.sqrt(square_hat) + ADAM_EPSILON) + WEIGHT_DECAY * weight
    )
    return (weight, first, second)


def per_device(
    token_ids,
    lengths,
    routes,
    positions,
    targets,
    teacher_index,
    teacher_weight,
    buckets,
    embed_weight,
    embed_mean,
    embed_square,
    attend_weight,
    attend_mean,
    attend_square,
    output_weight,
    output_mean,
    output_square,
    upward_weight,
    upward_mean,
    upward_square,
    downward_weight,
    downward_mean,
    downward_square,
    router_weight,
    router_mean,
    router_square,
    gains_weight,
    gains_mean,
    gains_square,
    bias_weight,
    bias_mean,
    bias_square,
):
    embed_all, gains_all, bias_all, router_all = (
        lax.all_gather(embed_weight.astype(jnp.bfloat16), "fsdp", axis=0, tiled=True),
        lax.all_gather(gains_weight.astype(jnp.bfloat16), "fsdp", axis=1, tiled=True),
        lax.all_gather(bias_weight.astype(jnp.bfloat16), "fsdp", axis=1, tiled=True),
        lax.all_gather(router_weight.astype(jnp.bfloat16), "fsdp", axis=1, tiled=True),
    )
    seq_index = lax.axis_index("seq")
    layers = attend_weight.shape[0]
    model_width = embed_weight.shape[1]
    head_local = H // lax.axis_size("seq")
    gains_full = gains_all.astype(jnp.float32)
    bias_full = bias_all.astype(jnp.float32).reshape(layers, -1, H)
    local_tables = lax.dynamic_slice_in_dim(bias_full, seq_index * head_local, head_local, 2)
    relatives = [relative_rows(buckets, local_tables[layer_index]) for layer_index in range(layers)]
    factor = model_width ** (-0.5)
    layer_grads = [
        (
            jnp.zeros(attend_weight.shape[1:], jnp.float32),
            jnp.zeros(output_weight.shape[1:], jnp.float32),
            jnp.zeros(upward_weight.shape[1:], jnp.float32),
            jnp.zeros(downward_weight.shape[1:], jnp.float32),
        )
        for layer_index in range(layers)
    ]
    gain_grads = jnp.zeros((2 * layers + 1, model_width), jnp.float32)
    router_grads = jnp.zeros((layers, model_width, router_all.shape[2]), jnp.float32)
    table_grads = jnp.zeros(local_tables.shape, jnp.float32)
    embed_grad = jnp.zeros(embed_weight.shape, jnp.float32)
    loss_total = jnp.zeros((), jnp.float32)
    count_total = jnp.zeros((), jnp.float32)
    for batch_index in range(token_ids.shape[0]):
        route_ids = routes[batch_index, 0, :, 0]
        seq_length = lengths[batch_index, 0]
        hidden = embed_all[token_ids[batch_index, 0]].astype(jnp.float32)
        kept_states, gathered_all = ([], [])
        for layer_index in range(layers):
            gathered = (
                lax.all_gather(
                    attend_weight[layer_index].astype(jnp.bfloat16), "fsdp", axis=0, tiled=True
                ),
                lax.all_gather(
                    output_weight[layer_index].astype(jnp.bfloat16), "fsdp", axis=0, tiled=True
                ),
                lax.all_gather(
                    upward_weight[layer_index].astype(jnp.bfloat16), "fsdp", axis=1, tiled=True
                ),
                lax.all_gather(
                    downward_weight[layer_index].astype(jnp.bfloat16), "fsdp", axis=1, tiled=True
                ),
            )
            hidden, kept_state = layer_forward(
                hidden,
                gathered,
                gains_full[2 * layer_index],
                gains_full[2 * layer_index + 1],
                router_all[layer_index],
                relatives[layer_index][0],
                route_ids,
                seq_length,
            )
            kept_states.append(kept_state)
            gathered_all.append(gathered)
        final, scale_final = rms_norm(hidden, gains_full[2 * layers])
        pos_ids = positions[batch_index, 0]
        picked = final[pos_ids].astype(jnp.bfloat16)
        logits = (
            jnp.einsum("pd,vd->pv", picked, embed_all, preferred_element_type=jnp.float32) * factor
        )
        log_probs = logits - jax.nn.logsumexp(logits, -1, keepdims=True)
        teacher = teacher_weight[batch_index, 0] / jnp.sum(
            teacher_weight[batch_index, 0], -1, keepdims=True
        )
        index_rows = teacher_index[batch_index, 0]
        taken = jnp.take_along_axis(log_probs, index_rows, 1)
        row_ids = jnp.arange(pos_ids.shape[0])
        target_ids = targets[batch_index, 0]
        valid = (seq_index * hidden.shape[0] + pos_ids < seq_length).astype(jnp.float32)
        per_row = jnp.sum(teacher * (jnp.log(teacher) - taken), -1) - log_probs[row_ids, target_ids]
        loss_total = loss_total + jnp.sum(valid * per_row)
        count_total = count_total + jnp.sum(valid)
        grad_logits = (jnp.sum(teacher, -1, keepdims=True) + 1.0) * jnp.exp(log_probs)
        grad_logits = grad_logits.at[row_ids[:, None], index_rows].add(-teacher)
        grad_logits = grad_logits.at[row_ids, target_ids].add(-1.0)
        grad_logits = (grad_logits * valid[:, None]).astype(jnp.bfloat16)
        grad_picked = matmul(grad_logits, embed_all) * factor
        grad_final = jnp.zeros_like(final).at[pos_ids].add(grad_picked)
        grad_hidden, grad_gain_final = rms_back(
            hidden, scale_final, gains_full[2 * layers], grad_final
        )
        gain_grads = gain_grads.at[2 * layers].add(grad_gain_final)
        for layer_index in reversed(range(layers)):
            grad_hidden, weight_grads, grad_one, grad_two, grad_router, grad_table = layer_backward(
                grad_hidden,
                kept_states[layer_index],
                gathered_all[layer_index],
                gains_full[2 * layer_index],
                gains_full[2 * layer_index + 1],
                router_all[layer_index],
                relatives[layer_index][0],
                relatives[layer_index][1],
                seq_length,
            )
            reduced = (
                lax.psum_scatter(weight_grads[0], "fsdp", scatter_dimension=0, tiled=True),
                lax.psum_scatter(weight_grads[1], "fsdp", scatter_dimension=0, tiled=True),
                lax.psum_scatter(weight_grads[2], "fsdp", scatter_dimension=1, tiled=True),
                lax.psum_scatter(weight_grads[3], "fsdp", scatter_dimension=1, tiled=True),
            )
            layer_grads[layer_index] = tuple(
                (total + piece for total, piece in zip(layer_grads[layer_index], reduced))
            )
            gain_grads = (
                gain_grads.at[2 * layer_index].add(grad_one).at[2 * layer_index + 1].add(grad_two)
            )
            router_grads = router_grads.at[layer_index].add(grad_router)
            table_grads = table_grads.at[layer_index].add(grad_table)
        id_rows = token_ids[batch_index, 0]
        row_count = embed_weight.shape[0] * lax.axis_size("fsdp")
        part_sum = (
            jnp.einsum("pv,pd->vd", grad_logits, picked, preferred_element_type=jnp.float32)
            * factor
        )
        inside = (id_rows >= 0) & (id_rows < row_count)
        lookup = jax.ops.segment_sum(
            grad_hidden, jnp.where(inside, id_rows, row_count), num_segments=row_count + 1
        )
        embed_grad = embed_grad + lax.psum_scatter(
            part_sum + lookup[:row_count], "fsdp", scatter_dimension=0, tiled=True
        )
    table_full = lax.dynamic_update_slice(
        jnp.zeros(bias_full.shape, jnp.float32), table_grads, (0, 0, seq_index * head_local)
    ).reshape(layers, -1)
    gains_red, table_red, router_red = (
        lax.psum_scatter(gain_grads, "fsdp", scatter_dimension=1, tiled=True),
        lax.psum_scatter(table_full, "fsdp", scatter_dimension=1, tiled=True),
        lax.psum_scatter(router_grads, "fsdp", scatter_dimension=1, tiled=True),
    )
    grads = (
        lax.psum(embed_grad.astype(jnp.bfloat16), "seq").astype(jnp.float32),
        lax.psum(jnp.stack([item[0] for item in layer_grads]).astype(jnp.bfloat16), "seq").astype(
            jnp.float32
        ),
        lax.psum(jnp.stack([item[1] for item in layer_grads]).astype(jnp.bfloat16), "seq").astype(
            jnp.float32
        ),
        lax.psum(jnp.stack([item[2] for item in layer_grads]).astype(jnp.bfloat16), "seq").astype(
            jnp.float32
        ),
        lax.psum(jnp.stack([item[3] for item in layer_grads]).astype(jnp.bfloat16), "seq").astype(
            jnp.float32
        ),
        lax.psum(router_red.astype(jnp.bfloat16), "seq").astype(jnp.float32),
        lax.psum(gains_red.astype(jnp.bfloat16), "seq").astype(jnp.float32),
        lax.psum(table_red.astype(jnp.bfloat16), "seq").astype(jnp.float32),
    )
    squares_local = sum((jnp.sum(item * item) for item in grads))
    grad_norm = jnp.sqrt(lax.psum(squares_local, "fsdp"))
    loss_value, loss_count = lax.psum((loss_total, count_total), ("seq", "fsdp"))
    clip_factor = jnp.minimum(1.0, CLIP_NORM / (grad_norm + 1e-06))
    params = (
        embed_weight,
        attend_weight,
        output_weight,
        upward_weight,
        downward_weight,
        router_weight,
        gains_weight,
        bias_weight,
    )
    means = (
        embed_mean,
        attend_mean,
        output_mean,
        upward_mean,
        downward_mean,
        router_mean,
        gains_mean,
        bias_mean,
    )
    squares = (
        embed_square,
        attend_square,
        output_square,
        upward_square,
        downward_square,
        router_square,
        gains_square,
        bias_square,
    )
    results = [loss_value, loss_count, grad_norm]
    for weight, grad, first, second, rate in zip(params, grads, means, squares, STEP_RATES):
        results.extend(adam_update(weight, grad * clip_factor, first, second, rate))
    return tuple(results)


def solution(mesh):
    return jax.shard_map(
        per_device,
        mesh=mesh,
        in_specs=(
            P(None, "fsdp", "seq"),
            P(None, "fsdp"),
            P(None, "fsdp", "seq", None),
            P(None, "fsdp", "seq"),
            P(None, "fsdp", "seq"),
            P(None, "fsdp", "seq", None),
            P(None, "fsdp", "seq", None),
            P(),
            P("fsdp", None),
            P("fsdp", None),
            P("fsdp", None),
            P(None, "fsdp", None),
            P(None, "fsdp", None),
            P(None, "fsdp", None),
            P(None, "fsdp", None),
            P(None, "fsdp", None),
            P(None, "fsdp", None),
            P(None, None, "fsdp", None),
            P(None, None, "fsdp", None),
            P(None, None, "fsdp", None),
            P(None, None, "fsdp", None),
            P(None, None, "fsdp", None),
            P(None, None, "fsdp", None),
            P(None, "fsdp", None),
            P(None, "fsdp", None),
            P(None, "fsdp", None),
            P(None, "fsdp"),
            P(None, "fsdp"),
            P(None, "fsdp"),
            P(None, "fsdp"),
            P(None, "fsdp"),
            P(None, "fsdp"),
        ),
        out_specs=(
            P(),
            P(),
            P(),
            P("fsdp", None),
            P("fsdp", None),
            P("fsdp", None),
            P(None, "fsdp", None),
            P(None, "fsdp", None),
            P(None, "fsdp", None),
            P(None, "fsdp", None),
            P(None, "fsdp", None),
            P(None, "fsdp", None),
            P(None, None, "fsdp", None),
            P(None, None, "fsdp", None),
            P(None, None, "fsdp", None),
            P(None, None, "fsdp", None),
            P(None, None, "fsdp", None),
            P(None, None, "fsdp", None),
            P(None, "fsdp", None),
            P(None, "fsdp", None),
            P(None, "fsdp", None),
            P(None, "fsdp"),
            P(None, "fsdp"),
            P(None, "fsdp"),
            P(None, "fsdp"),
            P(None, "fsdp"),
            P(None, "fsdp"),
        ),
        check_vma=False,
    )
```

profile of v0, /device:TPU:0, one launch (start us, length us, event | category | flops | bytes accessed | tf_op | source)
XLA Modules:
  0.0 7317.0 jit_solution(2882574754350492165)
XLA Ops:
  38.7 32.9 all-gather.8
  117.4 323.3 %all-gather.20.cloned.1.call-done = bf16[32128,768]{1,0:T(8,128)(2,1)} async-done(((bf16[4016,768]{1,0:T(8,128)(2,1)}), bf16[32128,768]{1,0:T(8,128)(2,1)}) %all-gather.20.cloned.1.call-update) | async-done | bytes 49348624 | tf_op jit(solution)/shard_map/all_gather | solution.py:391
  443.7 38.9 all-gather.22.cloned.1.call-done
  539.6 248.3 %while.166 = (s32[]{:T(128)}, bf16[2,3,512,64]{2,3,1,0:T(8,128)(2,1)S(1)}, f32[2,3,512]{2,1,0:T(4,128)S(1)}, s32[]{:T(128)}, s32[2]{0:T(128)S(1)}, /*index=5*/bf...) while((s32[]{:T(128)}, ...), condition=%wide.region_5.6_spmd, body=%wide.region_2.5_spmd.sunk | while | flops 416906752 | bytes 136691952 | solution.py:115
  606.5 48.2 rev.128
  730.5 48.2 rev.128
  798.8 261.5 %while.168 = (s32[]{:T(128)}, bf16[2,3,512,64]{2,3,1,0:T(8,128)(2,1)S(1)}, f32[2,3,512]{2,1,0:T(4,128)}, s32[]{:T(128)}, s32[2]{0:T(128)S(1)}, /*index=5*/bf16[3...) while((s32[]{:T(128)}, ...), condition=%wide.region_32.34_spmd, body=%wide.region_29.33_spmd.sunk | while | flops 416906752 | bytes 136687856 | solution.py:115
  877.6 48.3 rev.130
  1002.1 48.2 rev.130
  1186.9 247.7 %while.167 = (s32[]{:T(128)}, bf16[2,3,512,64]{2,3,1,0:T(8,128)(2,1)S(1)}, f32[2,3,512]{2,1,0:T(4,128)S(1)}, s32[]{:T(128)}, s32[2]{0:T(128)S(1)}, /*index=5*/bf...) while((s32[]{:T(128)}, ...), condition=%wide.region_17.18_spmd, body=%wide.region_14.17_spmd.sunk | while | flops 416906752 | bytes 136691952 | solution.py:115
  1253.8 48.2 rev.129
  1377.5 48.2 rev.129
  1445.4 260.9 %while.169 = (s32[]{:T(128)}, bf16[2,3,512,64]{2,3,1,0:T(8,128)(2,1)S(1)}, f32[2,3,512]{2,1,0:T(4,128)}, s32[]{:T(128)}, s32[2]{0:T(128)S(1)}, /*index=5*/bf16[3...) while((s32[]{:T(128)}, ...), condition=%wide.region_44.46_spmd, body=%wide.region_41.45_spmd.sunk | while | flops 416906752 | bytes 136687856 | solution.py:115
  1524.0 48.2 rev.131
  1648.2 48.2 rev.131
  2080.3 487.8 %while.170 = (s32[]{:T(128)}, f32[3,1024,64]{1,2,0:T(8,128)}, f32[3,1024,64]{1,2,0:T(8,128)}, f32[3,2047]{1,0:T(4,128)}, bf16[2,3,512,64]{2,3,1,0:T(8,128)(2,1)}...) while((s32[]{:T(128)}, f32[3,1024,64]{1,2,0:T(8,128)}, ...), condition=%wide.region_69.71_spmd.clone, body=%wide.region_66.70_spmd.clone.sunk | while | flops 1025806336 | bytes 329953568 | solution.py:165
  2152.6 48.2 rev.132
  2219.2 31.2 rev.133
  2395.2 48.2 rev.132
  2462.2 31.2 rev.133
  2597.1 490.5 %while.172 = (s32[]{:T(128)}, f32[3,1024,64]{1,2,0:T(8,128)}, f32[3,1024,64]{1,2,0:T(8,128)}, f32[3,2047]{1,0:T(4,128)}, bf16[2,3,512,64]{2,3,1,0:T(8,128)(2,1)}...) while((s32[]{:T(128)}, f32[3,1024,64]{1,2,0:T(8,128)}, ...), condition=%wide.region_92.94_spmd.clone, body=%wide.region_89.93_spmd.clone.sunk | while | flops 1025806336 | bytes 329953568 | solution.py:165
  2669.5 48.2 rev.136
  2736.1 31.2 rev.137
  2912.1 48.2 rev.136
  2979.1 31.2 rev.137
  3213.3 488.2 %while.171 = (s32[]{:T(128)}, f32[3,1024,64]{1,2,0:T(8,128)}, f32[3,1024,64]{1,2,0:T(8,128)}, f32[3,2047]{1,0:T(4,128)}, bf16[2,3,512,64]{2,3,1,0:T(8,128)(2,1)}...) while((s32[]{:T(128)}, f32[3,1024,64]{1,2,0:T(8,128)}, ...), condition=%wide.region_77.79_spmd.clone, body=%wide.region_74.78_spmd.clone.sunk | while | flops 1025806336 | bytes 329953568 | solution.py:165
  3286.4 48.2 rev.134
  3353.0 31.2 rev.135
  3528.7 48.2 rev.134
  3595.7 31.2 rev.135
  3729.7 491.7 %while.173 = (s32[]{:T(128)}, f32[3,1024,64]{1,2,0:T(8,128)}, f32[3,1024,64]{1,2,0:T(8,128)}, f32[3,2047]{1,0:T(4,128)}, bf16[2,3,512,64]{2,3,1,0:T(8,128)(2,1)}...) while((s32[]{:T(128)}, f32[3,1024,64]{1,2,0:T(8,128)}, ...), condition=%wide.region_100.102_spmd.clone, body=%wide.region_97.101_spmd.clone.sunk | while | flops 1025806336 | bytes 329953568 | solution.py:165
  3802.4 48.2 rev.138
  3869.0 31.2 rev.139
  4044.7 48.2 rev.138
  4111.7 31.2 rev.139
  4448.5 36.1 fusion.278
  4491.1 31.8 broadcast.1234.clone
  4522.9 33.3 scatter_fusion.3
  4556.2 31.3 broadcast.1234.clone.1
  4587.5 33.2 scatter_fusion.1
  4620.7 126.9 %fusion.96 = f32[32128,768]{1,0:T(8,128)} fusion(f32[32129,768]{1,0:T(8,128)} %scatter_fusion.3, f32[32129,768]{1,0:T(8,128)} %scatter_fusion.1, f32[32128,768]{1,0:T(8,128)} %fusion.278, bf16[32,768]{1,0:T(8,128)(2,1)S(1)} %copy-done.154, f32[32,32128]{1,0:T(8,128)} %scatter_fusion.2, f32[32]{0:T(128)S(1)} %copy-done.189), kind=kOutput, calls=%fused_computation.181 | convolution fusion | flops 1704583168 | bytes 398950528 | tf_op jit(solution)/shard_map/pv,pd->vd/dot_general | solution.py:509
  4767.7 300.9 %reduce-scatter.35.cloned.1.call-done = f32[4,384,768]{2,1,0:T(8,128)} async-done(((f32[4,3072,768]{2,1,0:T(8,128)}), f32[4,384,768]{2,1,0:T(8,128)}) %reduce-scatter.35.cloned.1.call-update) | async-done | bytes 4718608 | tf_op jit(solution)/shard_map/reduce_scatter | solution.py:496
  5071.2 363.0 %reduce-scatter.29.cloned.1.call-done = f32[4,96,3072]{2,1,0:T(8,128)} async-done(((f32[4,768,3072]{2,1,0:T(8,128)}), f32[4,96,3072]{2,1,0:T(8,128)}) %reduce-scatter.29.cloned.1.call-update) | async-done | bytes 4718608 | tf_op jit(solution)/shard_map/reduce_scatter | solution.py:495
  5439.9 360.0 %reduce-scatter.33.cloned.1.call-done = f32[4,384,768]{2,1,0:T(8,128)} async-done(((f32[4,3072,768]{2,1,0:T(8,128)}), f32[4,384,768]{2,1,0:T(8,128)}) %reduce-scatter.33.cloned.1.call-update) | async-done | bytes 4718608 | tf_op jit(solution)/shard_map/reduce_scatter | solution.py:496
  5805.0 932.3 %reduce-scatter.43.cloned.1.call-done = f32[4016,768]{1,0:T(8,128)} async-done(((f32[32128,768]{1,0:T(8,128)}), f32[4016,768]{1,0:T(8,128)}) %reduce-scatter.43.cloned.1.call-update) | async-done | bytes 12337168
  6801.2 31.0 reduce-scatter.39.cloned.1.call-done
  6844.9 302.1 %all-reduce.23.cloned.1.call-done = (bf16[4016,768]{1,0:T(8,128)(2,1)}, bf16[2,96,2304]{2,1,0:T(8,128)(2,1)}, bf16[2,96,768]{2,1,0:T(8,128)(2,1)}, bf16[2,4,96,3...) async-done(((bf16[4016,768]{1,0:T(8,128)(2,1)}, bf16[2,96,2304]{2,1,0:T(8,128)(2,1)}, bf16[2,96,768]{2,1,0:T(8,128)(2,1)}, bf16[2,4,96,3072]{3,2,1,0:T(8,128)(2,1)}, ...) | async-done | bytes 16785424 | tf_op jit(solution)/shard_map/psum | solution.py:528
  7169.0 40.3 all-reduce.18
  (1456 shorter events, 3194.4 us)
Async XLA Ops:
  7.2 433.4 %all-gather.20.cloned.1.call-start = ((), (), s32[]{:S(2)}) async-start(), calls=%async_computation.44 | async-start | bytes 55517184 | tf_op jit(solution)/shard_map/all_gather | solution.py:391
  15.0 467.5 %all-gather.22.cloned.1.call-start = ((), (), s32[]{:S(2)}) async-start(), calls=%async_computation.45 | async-start | bytes 3981312 | tf_op jit(solution)/shard_map/all_gather | solution.py:427
  17.6 1048.6 %all-gather.24.cloned.1.call-start = ((), (), s32[]{:S(2)}) async-start(), calls=%async_computation.46 | async-start | bytes 1327104 | tf_op jit(solution)/shard_map/all_gather | solution.py:430
  18.4 1058.7 %all-gather.26.cloned.1.call-start = ((), (), s32[]{:S(2)}) async-start(), calls=%async_computation.47 | async-start | bytes 21233664 | tf_op jit(solution)/shard_map/all_gather | solution.py:433
  25.8 1063.5 %all-gather.28.cloned.1.call-start = ((), (), s32[]{:S(2)}) async-start(), calls=%async_computation.48 | async-start | bytes 21233664 | tf_op jit(solution)/shard_map/all_gather | solution.py:436
  35.3 1071.0 %all-gather.30.cloned.1.call-start = ((), (), s32[]{:S(2)}) async-start(), calls=%async_computation.49 | async-start | bytes 3981312 | tf_op jit(solution)/shard_map/all_gather | solution.py:427
  35.8 1676.0 %all-gather.32.cloned.1.call-start = ((), (), s32[]{:S(2)}) async-start(), calls=%async_computation.50 | async-start | bytes 1327104 | tf_op jit(solution)/shard_map/all_gather | solution.py:430
  36.6 1686.1 %all-gather.34.cloned.1.call-start = ((), (), s32[]{:S(2)}) async-start(), calls=%async_computation.51 | async-start | bytes 21233664 | tf_op jit(solution)/shard_map/all_gather | solution.py:433
  37.3 1697.2 %all-gather.36.cloned.1.call-start = ((), (), s32[]{:S(2)}) async-start(), calls=%async_computation.52 | async-start | bytes 21233664 | tf_op jit(solution)/shard_map/all_gather | solution.py:436
  486.7 10.7 all-to-all-start
  497.5 9.7 all-to-all-start.1
  507.2 9.5 all-to-all-start.2
  535.4 256.2 %all-to-all-start.10 = ((bf16[256,4,192]{0,2,1:T(8,128)(2,1)}), bf16[256,4,192]{0,2,1:T(8,128)(2,1)}, u32[]{:S(2)}, u32[]{:S(2)}) async-start(bf16[256,4,192]{0,2,1:T(8,128)(2,1)} %bitcast.90), calls=%async_computation.10 | async-start | bytes 786432 | tf_op jit(solution)/shard_map/all_to_all | solution.py:184
  791.5 269.9 %all-to-all-start.3 = ((bf16[4,256,192]{1,2,0:T(8,128)(2,1)}), bf16[4,256,192]{1,2,0:T(8,128)(2,1)}, u32[]{:S(2)}, u32[]{:S(2)}) async-start(bf16[4,256,192]{1,2,0:T(8,128)(2,1)} %copy.330), calls=%async_computation.3 | async-start | bytes 786432 | tf_op jit(solution)/shard_map/all_to_all | solution.py:188
  1061.5 10.5 all-to-all-start.11
  1111.3 25.2 all-to-all-start.4
  1136.5 10.1 all-to-all-start.5
  1146.6 9.5 all-to-all-start.6
  1156.1 15.7 all-to-all-start.12
  1171.8 10.8 all-to-all-start.13
  1182.6 255.7 %all-to-all-start.14 = ((bf16[256,4,192]{0,2,1:T(8,128)(2,1)}), bf16[256,4,192]{0,2,1:T(8,128)(2,1)}, u32[]{:S(2)}, u32[]{:S(2)}) async-start(bf16[256,4,192]{0,2,1:T(8,128)(2,1)} %bitcast.112), calls=%async_computation.14 | async-start | bytes 786432 | tf_op jit(solution)/shard_map/all_to_all | solution.py:184
  1438.3 269.2 %all-to-all-start.7 = ((bf16[4,256,192]{1,2,0:T(8,128)(2,1)}), bf16[4,256,192]{1,2,0:T(8,128)(2,1)}, u32[]{:S(2)}, u32[]{:S(2)}) async-start(bf16[4,256,192]{1,2,0:T(8,128)(2,1)} %copy.343), calls=%async_computation.7 | async-start | bytes 786432 | tf_op jit(solution)/shard_map/all_to_all | solution.py:188
  1707.5 10.2 all-to-all-start.15
  2063.1 9.8 all-to-all-start.16
  2072.9 497.5 %all-to-all-start.24 = ((bf16[256,4,192]{0,2,1:T(8,128)(2,1)}), bf16[256,4,192]{0,2,1:T(8,128)(2,1)}, u32[]{:S(2)}, u32[]{:S(2)}) async-start(bf16[256,4,192]{0,2,1:T(8,128)(2,1)} %bitcast.170), calls=%async_computation.24 | async-start | bytes 786432 | tf_op jit(solution)/shard_map/all_to_all | solution.py:302
  2570.4 11.1 all-to-all-start.19
  2581.5 10.1 all-to-all-start.18
  2591.5 498.4 %all-to-all-start.17 = ((bf16[4,256,192]{1,2,0:T(8,128)(2,1)}), bf16[4,256,192]{1,2,0:T(8,128)(2,1)}, u32[]{:S(2)}, u32[]{:S(2)}) async-start(bf16[4,256,192]{1,2,0:T(8,128)(2,1)} %copy.366), calls=%async_computation.17 | async-start | bytes 786432 | tf_op jit(solution)/shard_map/all_to_all | solution.py:307
  3089.9 10.0 all-to-all-start.27
  3104.2 1653.1 %reduce-scatter.27.cloned.1.call-start = ((), (), s32[]{:S(2)}) async-start(), calls=%async_computation.56 | async-start | bytes 2654208 | tf_op jit(solution)/shard_map/reduce_scatter | solution.py:494
  3110.7 10.1 all-to-all-start.25
  3114.9 1643.4 %reduce-scatter.25.cloned.1.call-start = ((), (), s32[]{:S(2)}) async-start(), calls=%async_computation.55 | async-start | bytes 2654208 | tf_op jit(solution)/shard_map/reduce_scatter | solution.py:494
  3192.7 13.1 all-to-all-start.20
  3196.2 1563.9 %reduce-scatter.23.cloned.1.call-start = ((), (), s32[]{:S(2)}) async-start(), calls=%async_computation.54 | async-start | bytes 7962624 | tf_op jit(solution)/shard_map/reduce_scatter | solution.py:493
  3205.8 498.1 %all-to-all-start.28 = ((bf16[256,4,192]{0,2,1:T(8,128)(2,1)}), bf16[256,4,192]{0,2,1:T(8,128)(2,1)}, u32[]{:S(2)}, u32[]{:S(2)}) async-start(bf16[256,4,192]{0,2,1:T(8,128)(2,1)} %bitcast.187), calls=%async_computation.28 | async-start | bytes 786432 | tf_op jit(solution)/shard_map/all_to_all | solution.py:302
  3703.8 11.0 all-to-all-start.23
  3724.2 499.6 %all-to-all-start.21 = ((bf16[4,256,192]{1,2,0:T(8,128)(2,1)}), bf16[4,256,192]{1,2,0:T(8,128)(2,1)}, u32[]{:S(2)}, u32[]{:S(2)}) async-start(bf16[4,256,192]{1,2,0:T(8,128)(2,1)} %copy.372), calls=%async_computation.21 | async-start | bytes 786432 | tf_op jit(solution)/shard_map/all_to_all | solution.py:307
  4223.8 10.0 all-to-all-start.31
  4246.6 514.7 %reduce-scatter.21.cloned.1.call-start = ((), (), s32[]{:S(2)}) async-start(), calls=%async_computation.53 | async-start | bytes 7962624 | tf_op jit(solution)/shard_map/reduce_scatter | solution.py:493
  4260.5 503.0 %reduce-scatter.31.cloned.1.call-start = ((), (), s32[]{:S(2)}) async-start(), calls=%async_computation.58 | async-start | bytes 42467328 | tf_op jit(solution)/shard_map/reduce_scatter | solution.py:495
  4306.2 762.5 %reduce-scatter.35.cloned.1.call-start = ((), (), s32[]{:S(2)}) async-start(), calls=%async_computation.60 | async-start | bytes 42467328 | tf_op jit(solution)/shard_map/reduce_scatter | solution.py:496
  4354.4 1079.7 %reduce-scatter.29.cloned.1.call-start = ((), (), s32[]{:S(2)}) async-start(), calls=%async_computation.57 | async-start | bytes 42467328 | tf_op jit(solution)/shard_map/reduce_scatter | solution.py:495
  4399.9 1400.0 %reduce-scatter.33.cloned.1.call-start = ((), (), s32[]{:S(2)}) async-start(), calls=%async_computation.59 | async-start | bytes 42467328 | tf_op jit(solution)/shard_map/reduce_scatter | solution.py:496
  4447.7 2289.6 %reduce-scatter.43.cloned.1.call-start = ((), (), s32[]{:S(2)}) async-start(), calls=%async_computation.64 | async-start | bytes 111034368
  4747.9 2021.4 %reduce-scatter.37.cloned.1.call-start = ((), (), s32[]{:S(2)}) async-start(), calls=%async_computation.61 | async-start | bytes 442368
  4751.9 2048.5 %reduce-scatter.41.cloned.1.call-start = ((), (), s32[]{:S(2)}) async-start(), calls=%async_computation.63 | async-start | bytes 221184
  4755.4 2076.9 %reduce-scatter.39.cloned.1.call-start = ((), (), s32[]{:S(2)}) async-start(), calls=%async_computation.62 | async-start | bytes 442368
  4757.2 2389.7 %all-reduce.23.cloned.1.call-start = ((), (), s32[]{:S(2)}) async-start(), calls=%async_computation.65 | async-start | bytes 33570816 | tf_op jit(solution)/shard_map/psum | solution.py:528
  (297 other events, 6795.4 us)
Sparse Core Ops, SparseCore 0:
  15.2 425.4 all-gather.19
  442.8 39.6 all-gather.21
  484.8 21.5 all-gather.23
  508.4 168.0 all-gather.25
  678.5 166.4 all-gather.27
  847.1 39.6 all-gather.29
  888.5 21.5 all-gather.31
  912.3 168.0 all-gather.33
  1082.5 166.4 all-gather.35
  3108.0 36.7 reduce-scatter.26
  3189.6 35.8 reduce-scatter.24
  3228.2 76.4 reduce-scatter.22
  4260.6 76.7 reduce-scatter.20
  4339.6 363.2 reduce-scatter.30
  4705.3 363.3 reduce-scatter.34
  5070.8 363.2 reduce-scatter.28
  5436.5 363.2 reduce-scatter.32
  5802.1 935.1 reduce-scatter.42
  6740.2 29.0 reduce-scatter.36
  6772.0 28.3 reduce-scatter.40
  6803.3 28.8 reduce-scatter.38
  6837.8 309.1 all-reduce.22
where the time goes:
time: 7400 us; the launch traced here: 7320 us
  local copies, waits for them, and re-layouts  2870 us (39%)
  waiting for transfers between devices  2760 us (37%)
  matrix products  889 us (12%)
  other arithmetic  449 us (6%)
  blocking collectives  137 us (2%)
  starting transfers between devices  126 us (2%)
    unnamed x26, waiting for transfers between devices  1020 us
    rev x16, local copies, waits for them, and re-layouts, skew_bias(): return rows[:, ::-1, :]  771 us
    while x88, local copies, waits for them, and re-layouts  715 us
    reduce_scatter x2, waiting for transfers between devices, per_device(): lax.psum_scatter(weight_grads[3], 'fsdp', scatter_dimension=1, tiled=True)  661 us
    reduce_scatter x2, waiting for transfers between devices, per_device(): lax.psum_scatter(weight_grads[2], 'fsdp', scatter_dimension=1, tiled=True)  363 us
    all_gather x1, waiting for transfers between devices, per_device(): lax.all_gather(embed_weight.astype(jnp.bfloat16), 'fsdp', axis=0, tiled=T...  323 us
    psum x1, waiting for transfers between devices, per_device(): lax.psum(embed_grad.astype(jnp.bfloat16), 'seq').astype(jnp.float32)  302 us
    reshape x16, local copies, waits for them, and re-layouts, skew_bias(): rows = tiled.reshape(head_count, block_size, width + 1)[:, :, :total_rows]  266 us
  transfers between devices with their start and end apart: 54, of which 29 were waited for; matrix products, arithmetic and copies ran while one was open for 51% of the time, Pallas kernels for 0%

commit v1 on v0

v1 whole, which is shorter than its diff:
```python
import functools

import jax
import jax.numpy as jnp
from jax import lax
from jax.experimental import pallas as pl
from jax.experimental.pallas import tpu as pltpu
from jax.sharding import PartitionSpec as P

H = 12
HD = 64
STEP_COUNT = 10

EPSILON = 1e-06
ADAM_EPSILON = 1e-08
BETA_ONE = 0.9
BETA_TWO = 0.999
WEIGHT_DECAY = 0.01
CLIP_NORM = 1.0
STEP_RATES = (0.5, 0.03, 0.3, 0.03, 0.04, 0.02, 0.9, 0.5)
HIGHEST_PRECISION = lax.Precision.HIGHEST
VMEM_LIMIT = 48 * 1024 * 1024
BF16 = jnp.bfloat16
F32 = jnp.float32


def matmul(left_side, right_side):
    return jnp.dot(left_side, right_side, preferred_element_type=F32)


def contract(left_side, right_side, left_dim, right_dim):
    return lax.dot_general(
        left_side,
        right_side,
        (((left_dim,), (right_dim,)), ((), ())),
        preferred_element_type=F32,
    )


def rms_norm(hidden, gain):
    norm_scale = lax.rsqrt(jnp.mean(hidden * hidden, -1, keepdims=True) + EPSILON)
    return (hidden * norm_scale * gain, norm_scale)


def rms_back(hidden, norm_scale, gain, upstream):
    normed = hidden * norm_scale
    grad_normed = upstream * gain
    grad_gain = jnp.sum(upstream * normed, 0)
    grad_hidden = norm_scale * (
        grad_normed - normed * jnp.mean(grad_normed * normed, -1, keepdims=True)
    )
    return (grad_hidden, grad_gain)


def bias_tile_kernel(rel_ref, tile_ref):
    heads, width, block = tile_ref.shape
    length = rel_ref.shape[2]
    for head in range(heads):
        spread = jnp.broadcast_to(rel_ref[head], (block, length))
        skewed = pltpu.roll(spread, length - (block - 1), 1, stride=1, stride_axis=0)
        tile_ref[head] = skewed[:, :width].T


def bias_tile(relative, block, total):
    heads, length = relative.shape
    width = 2 * total - block
    padded = jnp.pad(relative, ((0, 0), (0, 2 * total - length)))[:, None, :]
    return pl.pallas_call(
        bias_tile_kernel,
        out_shape=jax.ShapeDtypeStruct((heads, width, block), F32),
        compiler_params=pltpu.CompilerParams(vmem_limit_bytes=VMEM_LIMIT),
        name="bias_tile",
    )(padded)


def head_columns(ref, part, heads, head):
    at = (part * heads + head) * HD
    return jnp.concatenate([ref[index, 0, at : at + HD, :] for index in range(ref.shape[0])], 1)


def transposed_scores(length, key, query_t, tile_ref, head, start, total):
    scores = matmul(key, query_t) * HD ** (-0.5) + tile_ref[head, pl.ds(start, total), :]
    key_ids = lax.broadcasted_iota(jnp.int32, scores.shape, 0)
    return jnp.where(key_ids < length, scores, -1e30)


def attend_kernel(length_ref, qkv_ref, tile_ref, out_ref, lse_ref):
    blocks, _, width, block = qkv_ref.shape
    total = blocks * block
    heads = width // (3 * HD)
    length = length_ref[pl.program_id(0)]
    for head in range(heads):
        at = head * HD
        key = head_columns(qkv_ref, 1, heads, head).T
        value_t = head_columns(qkv_ref, 2, heads, head)

        def step(index, carried, head=head, at=at, key=key, value_t=value_t):
            query_t = qkv_ref[index, 0, at : at + HD, :]
            start = pl.multiple_of((blocks - 1 - index) * block, block)
            scores = transposed_scores(length, key, query_t, tile_ref, head, start, total)
            peak = jnp.max(scores, 0, keepdims=True)
            powers = jnp.exp(scores - peak)
            norm = jnp.sum(powers, 0, keepdims=True)
            weights = (powers * (1.0 / norm)).astype(BF16)
            out_ref[index, 0, at : at + HD, :] = matmul(value_t, weights).astype(BF16)
            lse_ref[0, pl.ds(head * blocks + index, 1), :] = peak + jnp.log(norm)
            return carried

        lax.fori_loop(0, blocks, step, 0)


def attend(qkv, tile, lengths):
    blocks, count, width, block = qkv.shape
    heads = width // (3 * HD)
    total = blocks * block
    return pl.pallas_call(
        attend_kernel,
        grid=(count,),
        in_specs=[
            pl.BlockSpec(memory_space=pltpu.SMEM),
            pl.BlockSpec((blocks, 1, width, block), lambda i: (0, i, 0, 0)),
            pl.BlockSpec(tile.shape, lambda i: (0, 0, 0)),
        ],
        out_specs=[
            pl.BlockSpec((blocks, 1, heads * HD, block), lambda i: (0, i, 0, 0)),
            pl.BlockSpec((1, heads * blocks, block), lambda i: (i, 0, 0)),
        ],
        out_shape=[
            jax.ShapeDtypeStruct((blocks, count, heads * HD, block), BF16),
            jax.ShapeDtypeStruct((count, heads * blocks, block), F32),
        ],
        compiler_params=pltpu.CompilerParams(vmem_limit_bytes=VMEM_LIMIT),
        cost_estimate=pl.CostEstimate(
            flops=4 * count * heads * total * total * HD,
            bytes_accessed=2 * qkv.size + 4 * tile.size,
            transcendentals=count * heads * total * total,
        ),
        name="attend",
    )(lengths, qkv, tile)


def attend_back_kernel(
    length_ref, qkv_ref, out_grad_ref, lse_ref, tile_ref, grad_ref, rel_ref, sums_ref, dk_ref, dv_ref
):
    blocks, _, width, block = qkv_ref.shape
    total = blocks * block
    heads = width // (3 * HD)
    count = pl.num_programs(0)
    length = length_ref[pl.program_id(0)]
    scale = HD ** (-0.5)

    @pl.when(pl.program_id(0) == 0)
    def _():
        sums_ref[...] = jnp.zeros_like(sums_ref)

    for head in range(heads):
        at = head * HD
        key_t = head_columns(qkv_ref, 1, heads, head)
        key = key_t.T
        value = head_columns(qkv_ref, 2, heads, head).T
        dk_ref[...] = jnp.zeros_like(dk_ref)
        dv_ref[...] = jnp.zeros_like(dv_ref)

        def step(index, carried, head=head, at=at, key=key, key_t=key_t, value=value):
            query_t = qkv_ref[index, 0, at : at + HD, :]
            upstream_t = out_grad_ref[index, 0, at : at + HD, :]
            start = pl.multiple_of((blocks - 1 - index) * block, block)
            scores = transposed_scores(length, key, query_t, tile_ref, head, start, total)
            weights = jnp.exp(scores - lse_ref[0, pl.ds(head * blocks + index, 1), :])
            grad_weights = matmul(value, upstream_t)
            product = weights * grad_weights
            delta = jnp.sum(product, 0, keepdims=True)
            grad_scores = (product - weights * delta).astype(BF16)
            grad_ref[index, 0, at : at + HD, :] = (matmul(key_t, grad_scores) * scale).astype(BF16)
            dk_ref[...] += contract(query_t, grad_scores, 1, 1)
            dv_ref[...] += contract(upstream_t, weights.astype(BF16), 1, 1)
            sums_ref[head, pl.ds(start, total), :] += grad_scores.astype(F32)
            return carried

        lax.fori_loop(0, blocks, step, 0)
        key_at, value_at = heads * HD + at, 2 * heads * HD + at
        for index in range(blocks):
            columns = slice(index * block, (index + 1) * block)
            grad_ref[index, 0, key_at : key_at + HD, :] = (dk_ref[:, columns] * scale).astype(BF16)
            grad_ref[index, 0, value_at : value_at + HD, :] = dv_ref[:, columns].astype(BF16)

    @pl.when(pl.program_id(0) == count - 1)
    def _():
        length_all = 2 * total
        for head in range(heads):
            rows = jnp.concatenate([jnp.zeros((block, block), F32), sums_ref[head].T], 1)
            half = block // 2
            while half >= 8:
                rows = rows[:half] + pltpu.roll(rows[half:], length_all - half, 1)
                half //= 2
            folded = rows[:1]
            for row in range(1, 8):
                folded = folded + pltpu.roll(rows, length_all - row, 1)[row : row + 1]
            rel_ref[head] = folded


def attend_back(qkv, out_grad, lse, tile, lengths):
    blocks, count, width, block = qkv.shape
    heads = width // (3 * HD)
    total = blocks * block
    grads, rel = pl.pallas_call(
        attend_back_kernel,
        grid=(count,),
        in_specs=[
            pl.BlockSpec(memory_space=pltpu.SMEM),
            pl.BlockSpec((blocks, 1, width, block), lambda i: (0, i, 0, 0)),
            pl.BlockSpec((blocks, 1, heads * HD, block), lambda i: (0, i, 0, 0)),
            pl.BlockSpec((1, heads * blocks, block), lambda i: (i, 0, 0)),
            pl.BlockSpec(tile.shape, lambda i: (0, 0, 0)),
        ],
        out_specs=[
            pl.BlockSpec((blocks, 1, width, block), lambda i: (0, i, 0, 0)),
            pl.BlockSpec((heads, 1, 2 * total), lambda i: (0, 0, 0)),
        ],
        out_shape=[
            jax.ShapeDtypeStruct((blocks, count, width, block), BF16),
            jax.ShapeDtypeStruct((heads, 1, 2 * total), F32),
        ],
        scratch_shapes=[
            pltpu.VMEM(tile.shape, F32),
            pltpu.VMEM((HD, total), F32),
            pltpu.VMEM((HD, total), F32),
        ],
        compiler_params=pltpu.CompilerParams(vmem_limit_bytes=VMEM_LIMIT),
        cost_estimate=pl.CostEstimate(
            flops=10 * count * heads * total * total * HD,
            bytes_accessed=4 * qkv.size + 4 * tile.size,
            transcendentals=count * heads * total * total,
        ),
        name="attend_back",
    )(lengths, qkv, out_grad, lse, tile)
    return (grads, rel[:, 0, 1:])


def project_kernel(hidden_ref, gain_ref, weight_ref, out_ref, normed_ref, scale_ref):
    ways, _, width, _ = out_ref.shape
    normed, scale = rms_norm(hidden_ref[0], gain_ref[...])
    normed = normed.astype(BF16)
    normed_ref[0] = normed
    scale_ref[0] = scale
    for way in range(ways):
        columns = weight_ref[:, way * width : (way + 1) * width]
        out_ref[way, 0] = matmul(normed, columns).astype(BF16).T


def project(hidden, gain, dense, ways):
    count, rows, width = hidden.shape
    part = 3 * width // ways
    return pl.pallas_call(
        project_kernel,
        grid=(count,),
        in_specs=[
            pl.BlockSpec((1, rows, width), lambda i: (i, 0, 0)),
            pl.BlockSpec((1, width), lambda i: (0, 0)),
            pl.BlockSpec((width, 3 * width), lambda i: (0, 0)),
        ],
        out_specs=[
            pl.BlockSpec((ways, 1, part, rows), lambda i: (0, i, 0, 0)),
            pl.BlockSpec((1, rows, width), lambda i: (i, 0, 0)),
            pl.BlockSpec((1, rows, 1), lambda i: (i, 0, 0)),
        ],
        out_shape=[
            jax.ShapeDtypeStruct((ways, count, part, rows), BF16),
            jax.ShapeDtypeStruct((count, rows, width), BF16),
            jax.ShapeDtypeStruct((count, rows, 1), F32),
        ],
        compiler_params=pltpu.CompilerParams(vmem_limit_bytes=VMEM_LIMIT),
        cost_estimate=pl.CostEstimate(
            flops=6 * count * rows * width * width,
            bytes_accessed=12 * count * rows * width + 6 * width * width,
            transcendentals=0,
        ),
        name="project",
    )(hidden, gain[None], dense)


def embed_adam_kernel(rate, clip_ref, grad_ref, weight_ref, first_ref, second_ref, *out_refs):
    grad = jnp.concatenate([grad_ref[way].T for way in range(grad_ref.shape[0])], 1).astype(F32)
    updated = adam_update(
        weight_ref[...], grad * clip_ref[0], first_ref[...], second_ref[...], rate
    )
    for ref, value in zip(out_refs, updated):
        ref[...] = value


def embed_adam(weight, grad, first, second, clip, rate):
    rows, width = weight.shape
    ways, part, _ = grad.shape
    block = min(256, rows)
    state = pl.BlockSpec((block, width), lambda i: (i, 0))
    return pl.pallas_call(
        functools.partial(embed_adam_kernel, rate),
        grid=(pl.cdiv(rows, block),),
        in_specs=[
            pl.BlockSpec(memory_space=pltpu.SMEM),
            pl.BlockSpec((ways, part, block), lambda i: (0, 0, i)),
            state,
            state,
            state,
        ],
        out_specs=[state, state, state],
        out_shape=[jax.ShapeDtypeStruct((rows, width), F32)] * 3,
        compiler_params=pltpu.CompilerParams(vmem_limit_bytes=VMEM_LIMIT),
        cost_estimate=pl.CostEstimate(
            flops=20 * rows * width, bytes_accessed=26 * rows * width, transcendentals=rows * width
        ),
        name="embed_adam",
    )(clip.reshape(1), grad, weight, first, second)


def exchange(parts):
    return lax.all_to_all(parts, "seq", split_axis=0, concat_axis=0, tiled=True)


def share(part):
    ways = lax.axis_size("seq")
    return exchange(jnp.broadcast_to(part[None], (ways,) + part.shape))


def sum_over_seq(parts):
    return jnp.sum(exchange(parts).astype(F32), 0)


def as_rows(flat):
    return jnp.pad(flat, (0, -flat.size % 1024)).reshape(-1, 128)


def sum_everywhere(parts):
    ways, owners = parts.shape[:2]
    size = parts.size // (ways * owners)
    flat = parts.reshape(ways * owners, size)
    flat = jnp.pad(flat, ((0, 0), (0, -size % 1024))).reshape(ways * owners, -1, 128)
    moved = lax.all_to_all(flat, ("seq", "fsdp"), split_axis=0, concat_axis=0, tiled=True)
    return jnp.sum(moved, 0).reshape(-1)[:size]


def after(value, *others):
    return lax.optimization_barrier((value,) + others)


def layer_forward(hidden, weights, gain_one, gain_two, router_w, tile, moe, lengths):
    dense, upward_w, downward_w = weights
    count, rows, width = hidden.shape
    output_w = dense[:, 3 * width :]
    ways = lax.axis_size("seq")
    dispatch, onehot = moe
    slots = dispatch.shape[1]
    projected, normed_one, scale_one = project(hidden, gain_one, dense, ways)
    qkv = exchange(projected)
    mixed, lse = attend(qkv, tile, lengths)
    mixed_t = exchange(mixed).reshape(width, rows)
    after_attn = hidden + contract(mixed_t, output_w, 0, 0).reshape(hidden.shape)
    normed_two, scale_two = rms_norm(after_attn, gain_two)
    normed_two = normed_two.astype(BF16)
    router_probs = jax.nn.softmax(
        matmul(normed_two.reshape(count * rows, width), router_w).reshape(count, rows, -1), -1
    )
    gate = jnp.sum(router_probs * onehot, -1, keepdims=True)
    sent = jnp.einsum("nst,ntd->nsd", dispatch, normed_two, preferred_element_type=F32).astype(BF16)
    sent = sent.reshape(count, ways, slots // ways, width).transpose(1, 0, 2, 3)
    expert_rows = exchange(sent).reshape(count * slots, width)
    upward = matmul(expert_rows, upward_w)
    activated = jax.nn.gelu(upward).astype(BF16)
    expert_out = matmul(activated, downward_w).astype(BF16)
    back = exchange(expert_out.reshape(ways, count, slots // ways, width))
    back = back.transpose(1, 0, 2, 3).reshape(count, slots, width)
    token_out = jnp.einsum("nst,nsd->ntd", dispatch, back, preferred_element_type=F32)
    result = after_attn + gate * token_out
    kept = dict(
        hidden=hidden,
        scale_one=scale_one,
        normed_one=normed_one,
        qkv=qkv,
        lse=lse,
        mixed_t=mixed_t,
        after_attn=after_attn,
        scale_two=scale_two,
        normed_two=normed_two,
        router_probs=router_probs,
        gate=gate,
        expert_rows=expert_rows,
        upward=upward,
        activated=activated,
        token_out=token_out,
    )
    return (result, kept)


def layer_backward(
    grad_out, kept, weights, gain_one, gain_two, router_w, tile, moe, lengths, gates
):
    dense, upward_w, downward_w = weights
    count, rows, width = grad_out.shape
    attend_w, output_w = dense[:, : 3 * width], dense[:, 3 * width :]
    ways = lax.axis_size("seq")
    dispatch, onehot = moe
    slots = dispatch.shape[1]
    flat = (count * rows, width)
    grad_gate = jnp.sum(grad_out * kept["token_out"], -1, keepdims=True)
    grad_token = (kept["gate"] * grad_out).astype(BF16)
    sent = jnp.einsum("nst,ntd->nsd", dispatch, grad_token, preferred_element_type=F32).astype(BF16)
    sent = sent.reshape(count, ways, slots // ways, width).transpose(1, 0, 2, 3)
    grad_expert = exchange(sent).reshape(count * slots, width)
    grad_activated = contract(grad_expert, downward_w, 1, 1)
    grad_upward = jax.vjp(jax.nn.gelu, kept["upward"])[1](grad_activated)[0].astype(BF16)
    grad_rows = contract(grad_upward, upward_w, 1, 1).astype(BF16)
    back = exchange(grad_rows.reshape(ways, count, slots // ways, width))
    back, *first_gate = after(back, *gates[0])
    back = back.transpose(1, 0, 2, 3).reshape(count, slots, width)
    grad_normed = jnp.einsum("nst,nsd->ntd", dispatch, back, preferred_element_type=F32)
    grad_probs = onehot * grad_gate
    router_probs = kept["router_probs"]
    grad_logits = (
        router_probs * (grad_probs - jnp.sum(grad_probs * router_probs, -1, keepdims=True))
    ).astype(BF16)
    grad_logits = grad_logits.reshape(count * rows, -1)
    grad_router = contract(kept["normed_two"].reshape(flat), grad_logits, 0, 0)
    grad_normed = grad_normed.reshape(flat) + contract(grad_logits, router_w, 1, 1)
    grad_mid, grad_gain_two = rms_back(
        kept["after_attn"].reshape(flat), kept["scale_two"].reshape(-1, 1), gain_two, grad_normed
    )
    grad_mid = grad_mid + grad_out.reshape(flat)
    grad_attn = grad_mid.astype(BF16)
    grad_mixed_t = contract(output_w, grad_attn, 1, 1).astype(BF16)
    grad_mixed_t = exchange(grad_mixed_t.reshape(ways, 1, width // ways, rows))
    grad_mixed_t, *second_gate = after(grad_mixed_t, *gates[1])
    grad_qkv, grad_relative = attend_back(kept["qkv"], grad_mixed_t, kept["lse"], tile, lengths)
    grad_projected_t = exchange(grad_qkv).reshape(3 * width, rows)
    grad_first, grad_gain_one = rms_back(
        kept["hidden"].reshape(flat),
        kept["scale_one"].reshape(-1, 1),
        gain_one,
        contract(grad_projected_t, attend_w, 0, 1),
    )
    return (
        (grad_mid + grad_first).reshape(grad_out.shape),
        (
            (kept["expert_rows"], grad_upward),
            (kept["activated"], grad_expert),
            (kept["normed_one"].reshape(flat), grad_projected_t),
            (kept["mixed_t"], grad_attn),
        ),
        (grad_gain_one, grad_gain_two, grad_router, grad_relative),
        (first_gate, second_gate),
    )


def adam_update(weight, grad, first, second, rate):
    first = BETA_ONE * first + (1.0 - BETA_ONE) * grad
    second = BETA_TWO * second + (1.0 - BETA_TWO) * grad * grad
    mean_hat = first / (1.0 - BETA_ONE**STEP_COUNT)
    square_hat = second / (1.0 - BETA_TWO**STEP_COUNT)
    weight = weight - rate * (
        mean_hat / (jnp.sqrt(square_hat) + ADAM_EPSILON) + WEIGHT_DECAY * weight
    )
    return (weight, first, second)


def scatter_owners(item):
    return lax.psum_scatter(item, "fsdp", scatter_dimension=0, tiled=True)


def sum_squares(*arrays):
    return sum(jnp.sum(jnp.square(item.astype(F32))) for item in arrays)


def per_device(
    token_ids,
    lengths,
    routes,
    positions,
    targets,
    teacher_index,
    teacher_weight,
    buckets,
    embed_weight,
    embed_mean,
    embed_square,
    attend_weight,
    attend_mean,
    attend_square,
    output_weight,
    output_mean,
    output_square,
    upward_weight,
    upward_mean,
    upward_square,
    downward_weight,
    downward_mean,
    downward_square,
    router_weight,
    router_mean,
    router_square,
    gains_weight,
    gains_mean,
    gains_square,
    bias_weight,
    bias_mean,
    bias_square,
):
    ways, owners = lax.axis_size("seq"), lax.axis_size("fsdp")
    seq_index, owner_index = lax.axis_index("seq"), lax.axis_index("fsdp")
    layers, experts = upward_weight.shape[0], upward_weight.shape[1]
    vocab_rows, width = embed_weight.shape
    count, rows = token_ids.shape[0], token_ids.shape[2]
    total = rows * ways
    picks = positions.shape[2]
    shard = upward_weight.shape[2]
    part = width // ways
    capacity = rows * 3 // 8
    factor = width ** (-0.5)
    lengths = lengths[:, 0]

    def dense_shard(layer):
        attend_low = attend_weight[layer].reshape(shard, 3, ways, part).transpose(0, 2, 1, 3)
        return jnp.concatenate(
            [attend_low.reshape(shard, 3 * width).astype(BF16), output_weight[layer].astype(BF16)], 1
        )

    def gather_owners(item):
        return lax.all_gather(item, "fsdp", axis=0, tiled=True)

    def gather_expert(item, layer):
        mine = lax.dynamic_index_in_dim(item[layer], seq_index, 0, False)
        return gather_owners(mine.astype(BF16))

    first_dense = dense_shard(0)
    own_ids, first_dense = after(token_ids[:, 0], first_dense)
    first_dense = gather_owners(first_dense)
    group_ids = lax.all_gather(own_ids, "fsdp", axis=0, tiled=False)
    embed_low = embed_weight.astype(BF16)
    vocab_ids = jnp.arange(vocab_rows)
    founds = []
    for batch in range(count):
        local_ids = group_ids[:, batch].reshape(-1) - owner_index * vocab_rows
        founds.append(
            matmul((local_ids[:, None] == vocab_ids[None, :]).astype(BF16), embed_low).astype(BF16)
        )
        if batch == 0:
            founds[0], first_dense = after(founds[0], first_dense)
    later = (attend_weight, output_weight, upward_weight, downward_weight)
    founds[-1], *later = after(founds[-1], *later)
    hiddens = [
        lax.psum_scatter(
            found.reshape(owners, rows, width), "fsdp", scatter_dimension=0, tiled=False
        )
        .astype(F32)
        .reshape(1, rows, width)
        for found in founds
    ]
    weights = []
    for layer in range(layers):
        weights.append(
            (
                gather_owners(dense_shard(layer)) if layer else first_dense,
                gather_expert(later[2], layer),
                gather_expert(later[3], layer),
            )
        )

    valid_own = (seq_index * rows + positions[:, 0] < lengths[:, None]).astype(F32)
    teacher_own = teacher_weight[:, 0] / jnp.sum(teacher_weight[:, 0], -1, keepdims=True)
    small = jnp.concatenate(
        [
            lax.optimization_barrier(item.astype(BF16)).astype(F32).reshape(-1)
            for item in (gains_weight, bias_weight, router_weight)
        ]
        + [item.astype(F32).reshape(-1) for item in (valid_own, targets, teacher_index, teacher_own)]
    )
    small = lax.all_gather(as_rows(small), "fsdp", axis=0, tiled=False).reshape(owners, -1)
    pieces, at = [], 0
    for item in (gains_weight, bias_weight, router_weight, valid_own, targets, teacher_index, teacher_own):
        pieces.append(small[:, at : at + item.size])
        at += item.size
    norms = 2 * layers + 1
    gains_full = pieces[0].reshape(owners, norms, shard).transpose(1, 0, 2).reshape(norms, width)
    bias_full = pieces[1].reshape(owners, layers, -1).transpose(1, 0, 2).reshape(layers, -1, H)
    router_full = (
        pieces[2].reshape(owners, layers, shard, experts).transpose(1, 0, 2, 3).astype(BF16)
    ).reshape(layers, width, experts)
    valid_all = pieces[3].reshape(-1)
    targets_all = pieces[4].astype(jnp.int32).reshape(-1, 1)
    index_all = pieces[5].astype(jnp.int32).reshape(-1, teacher_index.shape[3])
    teacher_all = pieces[6].reshape(-1, teacher_index.shape[3])

    head_local = H // ways
    local_tables = lax.dynamic_slice_in_dim(bias_full, seq_index * head_local, head_local, 2)
    onehot_buckets = (buckets[:, None] == jnp.arange(bias_full.shape[1])[None, :]).astype(F32)
    tiles = [
        bias_tile(
            jnp.dot(onehot_buckets, local_tables[layer], precision=HIGHEST_PRECISION).T, rows, total
        )
        for layer in range(layers)
    ]

    route_ids = routes[:, 0, :, 0]
    onehot = (route_ids[..., None] == jnp.arange(experts)).astype(F32)
    ranks = jnp.sum((jnp.cumsum(onehot, 1) - 1.0) * onehot, -1).astype(jnp.int32)
    slot_index = route_ids * capacity + ranks
    dispatch = (slot_index[:, None, :] == jnp.arange(experts * capacity)[None, :, None]).astype(BF16)

    base = owner_index * vocab_rows
    entry = jnp.concatenate([index_all, targets_all], 1) - base
    mass = jnp.concatenate([teacher_all, jnp.ones_like(teacher_all[:, :1])], 1)
    lanes = 128
    groups = -(-vocab_rows // lanes)
    entry = jnp.where((entry >= 0) & (entry < vocab_rows), entry, groups * lanes)
    high = (entry[..., None] // lanes == jnp.arange(groups)).astype(F32) * mass[..., None]
    low = (entry[..., None] % lanes == jnp.arange(lanes)).astype(F32)
    wanted = jnp.einsum("rkh,rkl->rhl", high, low, precision=HIGHEST_PRECISION)
    wanted = wanted.reshape(-1, groups * lanes)[:, :vocab_rows]
    mass_all = jnp.sum(teacher_all, -1, keepdims=True) + 1.0

    kept_all = [[None] * count for layer in range(layers)]
    moes = [(dispatch[batch : batch + 1], onehot[batch : batch + 1]) for batch in range(count)]
    used = [lengths[batch : batch + 1] for batch in range(count)]
    for layer in range(layers):
        for batch in range(count):
            hiddens[batch], kept_all[layer][batch] = layer_forward(
                hiddens[batch],
                weights[layer],
                gains_full[2 * layer],
                gains_full[2 * layer + 1],
                router_full[layer],
                tiles[layer],
                moes[batch],
                used[batch],
            )
        if layer == 0:
            hiddens[-1], wanted = after(hiddens[-1], wanted)
    hidden = jnp.concatenate(hiddens, 0)

    final, scale_final = rms_norm(hidden, gains_full[2 * layers])
    chosen = (positions[:, 0][..., None] == jnp.arange(rows)).astype(BF16)
    picked = jnp.einsum("npt,ntd->npd", chosen, final.astype(BF16), preferred_element_type=F32)
    picked = lax.all_gather(
        picked.astype(BF16).reshape(count * picks, width), "fsdp", axis=0, tiled=True
    )
    logits = contract(picked, embed_low, 1, 1) * factor
    peak = jnp.max(logits, -1)
    stats = jnp.stack([peak, jnp.sum(jnp.exp(logits - peak[:, None]), -1)])
    stats = lax.all_gather(stats, "fsdp", axis=0, tiled=False)
    peak_all = jnp.max(stats[:, 0], 0)
    lse_all = peak_all + jnp.log(jnp.sum(stats[:, 1] * jnp.exp(stats[:, 0] - peak_all), 0))
    grad_logits = mass_all * jnp.exp(logits - lse_all[:, None]) - wanted
    grad_logits = (grad_logits * valid_all[:, None]).astype(BF16)
    lse_own = lax.dynamic_slice_in_dim(lse_all, owner_index * count * picks, count * picks, 0)
    mass_own = jnp.sum(teacher_own, -1) + 1.0
    own_rows = jnp.sum(teacher_own * jnp.log(teacher_own), -1) + mass_own * lse_own.reshape(count, picks)
    loss_part = jnp.sum(valid_own * own_rows) - jnp.sum(
        valid_all * jnp.sum(wanted * logits, -1)
    )
    grad_picked = lax.psum_scatter(
        matmul(grad_logits, embed_low), "fsdp", scatter_dimension=0, tiled=True
    )
    grad_picked = (grad_picked * factor).reshape(count, picks, width)
    head_grad = (contract(picked, grad_logits, 0, 0) * factor).astype(BF16)
    head_grad = sum_over_seq(head_grad.reshape(ways, part, vocab_rows))
    grad_final = jnp.einsum(
        "npt,npd->ntd", chosen.astype(F32), grad_picked, precision=HIGHEST_PRECISION
    )
    grad_hidden, grad_gain_final = rms_back(
        hidden.reshape(count * rows, width),
        scale_final.reshape(-1, 1),
        gains_full[2 * layers],
        grad_final.reshape(count * rows, width),
    )
    grad_hidden = grad_hidden.reshape(hidden.shape)
    grad_hiddens = [grad_hidden[batch : batch + 1] for batch in range(count)]

    gain_grads = [None] * norms
    gain_grads[2 * layers] = grad_gain_final
    router_grads, table_grads = [None] * layers, [None] * layers
    grad_parts = [None] * layers
    gates = []
    for layer in reversed(range(layers)):
        sides, small_grads = [None] * count, [None] * count
        passed = []
        for batch in range(count):
            held = gates[2 * batch : 2 * batch + 2]
            held = [held[at : at + 1] for at in range(2)]
            grad_hiddens[batch], sides[batch], small_grads[batch], held = layer_backward(
                grad_hiddens[batch],
                kept_all[layer][batch],
                weights[layer],
                gains_full[2 * layer],
                gains_full[2 * layer + 1],
                router_full[layer],
                tiles[layer],
                moes[batch],
                used[batch],
                held,
            )
            passed.extend(held[0] + held[1])
        if passed:
            grad_parts[layer + 1] = passed
        gain_grads[2 * layer], gain_grads[2 * layer + 1], router_grads[layer], grad_relative = (
            sum(items) for items in zip(*small_grads)
        )
        table_grads[layer] = jnp.dot(onehot_buckets.T, grad_relative.T, precision=HIGHEST_PRECISION)
        weight_grads = [
            contract(
                jnp.concatenate([item[0] for item in pairs], left_dim),
                jnp.concatenate([item[1] for item in pairs], right_dim),
                left_dim,
                right_dim,
            ).astype(BF16)
            for pairs, left_dim, right_dim in zip(zip(*sides), (0, 0, 0, 1), (0, 0, 1, 0))
        ]
        grad_parts[layer] = [scatter_owners(item) for item in weight_grads[:2]]
        dense_grad = jnp.concatenate(weight_grads[2:], 1)
        if layer:
            grad_parts[layer].append(scatter_owners(dense_grad))
        gates = grad_parts[layer]
        if layer:
            grad_hiddens[0], dense_grad = after(grad_hiddens[0], dense_grad)

    moved = []
    for batch in range(count):
        if batch < 2:
            grad_hiddens[batch], grad_parts[0][batch] = after(
                grad_hiddens[batch], grad_parts[0][batch]
            )
        columns = grad_hiddens[batch].reshape(rows, width).astype(BF16).T
        columns = exchange(columns.reshape(ways, part, rows))
        columns = lax.all_gather(columns, "fsdp", axis=0, tiled=False)
        moved.append(columns.transpose(2, 0, 1, 3).reshape(part, -1))
    moved[0], dense_grad = after(moved[0], dense_grad)
    grad_parts[0].append(scatter_owners(dense_grad))
    shared = [[None] * 3 for layer in range(layers)]
    shared[-1] = [share(item) for item in grad_parts[-1][:2]]
    moved[-1], *shared[-1] = after(moved[-1], *shared[-1])
    every_id = lax.all_gather(group_ids, "seq", axis=0, tiled=False) - owner_index * vocab_rows
    every_id = every_id.transpose(2, 1, 0, 3).reshape(count, -1)
    embed_part = head_grad
    for batch in range(count):
        embed_part = embed_part + matmul(
            moved[batch], (every_id[batch][:, None] == vocab_ids[None, :]).astype(BF16)
        )
    embed_part = embed_part.astype(BF16)
    for layer in range(layers):
        dense = grad_parts[layer][2]
        dense = jnp.concatenate(
            [
                dense[:, : 3 * width].reshape(shard, ways, 3 * part),
                dense[:, 3 * width :].reshape(shard, ways, part),
            ],
            2,
        )
        grad_parts[layer][2] = sum_over_seq(dense.transpose(1, 0, 2)).astype(BF16)

    tables = lax.dynamic_update_slice(
        jnp.zeros(bias_full.shape, F32), jnp.stack(table_grads), (0, 0, seq_index * head_local)
    )
    bias_shard = bias_weight.shape[1]
    tiny = jnp.concatenate(
        [
            jnp.stack(gain_grads).reshape(norms, owners, shard).transpose(1, 0, 2).reshape(owners, -1),
            tables.reshape(layers, owners, bias_shard).transpose(1, 0, 2).reshape(owners, -1),
            jnp.stack(router_grads)
            .reshape(layers, owners, shard, experts)
            .transpose(1, 0, 2, 3)
            .reshape(owners, -1),
            jnp.broadcast_to(jnp.stack([loss_part, jnp.sum(valid_own)])[None], (owners, 2)),
        ],
        1,
    )
    tiny = sum_everywhere(jnp.broadcast_to(tiny[None], (ways,) + tiny.shape))
    gain_size, bias_size = gains_weight.size, bias_weight.size
    gains_grad = tiny[:gain_size].reshape(gains_weight.shape)
    bias_grad = tiny[gain_size : gain_size + bias_size].reshape(bias_weight.shape)
    router_grad = tiny[gain_size + bias_size : -2].reshape(router_weight.shape)
    loss_value, loss_count = tiny[-2], tiny[-1]

    squares_part = (
        sum_squares(embed_part, *(item for parts in grad_parts for item in parts))
        + sum_squares(gains_grad, bias_grad, router_grad) / ways
    )
    grad_norm = jnp.sqrt(
        sum_everywhere(jnp.broadcast_to(squares_part, (ways, owners, 1)))[0]
    )
    clip_factor = jnp.minimum(1.0, CLIP_NORM / (grad_norm + 1e-06))

    embed_grad = share(embed_part)
    for layer in range(layers):
        shared[layer] = [
            share(item) if done is None else done for item, done in zip(grad_parts[layer], (shared[layer] + [None])[:3])
        ]
    upward_grad = jnp.stack([items[0] for items in shared])
    downward_grad = jnp.stack([items[1] for items in shared])
    dense_grads = [items[2] for items in shared]
    attend_grad = jnp.stack(
        [
            item[:, :, : 3 * part]
            .reshape(ways, shard, 3, part)
            .transpose(1, 2, 0, 3)
            .reshape(shard, 3 * width)
            for item in dense_grads
        ]
    )
    output_grad = jnp.stack(
        [item[:, :, 3 * part :].transpose(1, 0, 2).reshape(shard, width) for item in dense_grads]
    )
    grads = (
        embed_grad,
        attend_grad,
        output_grad,
        upward_grad,
        downward_grad,
        router_grad,
        gains_grad,
        bias_grad,
    )
    params = (
        embed_weight,
        attend_weight,
        output_weight,
        upward_weight,
        downward_weight,
        router_weight,
        gains_weight,
        bias_weight,
    )
    means = (
        embed_mean,
        attend_mean,
        output_mean,
        upward_mean,
        downward_mean,
        router_mean,
        gains_mean,
        bias_mean,
    )
    squares = (
        embed_square,
        attend_square,
        output_square,
        upward_square,
        downward_square,
        router_square,
        gains_square,
        bias_square,
    )
    results = [loss_value, loss_count, grad_norm]
    results.extend(
        embed_adam(embed_weight, embed_grad, embed_mean, embed_square, clip_factor, STEP_RATES[0])
    )
    for weight, grad, first, second, rate in list(
        zip(params, grads, means, squares, STEP_RATES)
    )[1:]:
        results.extend(adam_update(weight, grad.astype(F32) * clip_factor, first, second, rate))
    return tuple(results)


def solution(mesh):
    token = P(None, "fsdp", "seq")
    entry = P(None, "fsdp", "seq", None)
    state = (
        [P("fsdp", None)] * 3
        + [P(None, "fsdp", None)] * 6
        + [P(None, None, "fsdp", None)] * 6
        + [P(None, "fsdp", None)] * 3
        + [P(None, "fsdp")] * 6
    )
    return jax.shard_map(
        per_device,
        mesh=mesh,
        in_specs=tuple([token, P(None, "fsdp"), entry, token, token, entry, entry, P()] + state),
        out_specs=tuple([P(), P(), P()] + state),
        check_vma=False,
    )
```

time: 7400 us -> 1520 us (0.21)
  local copies, waits for them, and re-layouts: 2870 us -> 143 us
  waiting for transfers between devices: 2760 us -> 356 us
  matrix products: 889 us -> 370 us
  other arithmetic: 449 us -> 130 us
  Pallas kernels: 0 us -> 202 us
    rev x24 -> x0, local copies, waits for them, and re-layouts: 1020 us -> none  [the longest x16 771 us: skew_bias(): return rows[:, ::-1, :]]
    unnamed x26 -> x17, waiting for transfers between devices: 1020 us -> 0.28 us
    reduce_scatter x8 -> x9, waiting for transfers between devices: 1020 us -> 68.5 us  [the longest x1 32.1 us: per_device(): lax.psum_scatter(matmul(grad_logits, embed_low), 'fsdp', scatter_dimensio...]
    while x88 -> x0, local copies, waits for them, and re-layouts: 715 us -> none
    dot_general x136 -> x78, matrix products: 889 us -> 370 us  [the longest x17 159 us: matmul(): return jnp.dot(left_side, right_side, preferred_element_type=F32)]
    reshape x54 -> x28, local copies, waits for them, and re-layouts: 508 us -> 23.1 us  [the longest x2 10.1 us: per_device(): moved.append(columns.transpose(2, 0, 1, 3).reshape(part, -1))]
    all_gather x9 -> x8, waiting for transfers between devices: 362 us -> 57 us  [the longest x6 37.1 us: gather_owners(): return lax.all_gather(item, 'fsdp', axis=0, tiled=True)]
    psum x1 -> x0, waiting for transfers between devices: 302 us -> none  [per_device(): lax.psum(embed_grad.astype(jnp.bfloat16), 'seq').astype(jnp.float32)]
  transfers between devices with their start and end apart: 54 -> 60, of which waited for: 29 -> 29; matrix products, arithmetic and copies ran while one was open for 51% -> 35% of each run, Pallas kernels for 0% -> 13%
where the time goes in v1:
time: 1520 us; the launch traced here: 1510 us
  matrix products  370 us (24%)
  waiting for transfers between devices  356 us (23%)
  Pallas kernels  202 us (13%)
  starting transfers between devices  179 us (12%)
  local copies, waits for them, and re-layouts  143 us (9%)
  other arithmetic  130 us (9%)
  blocking collectives  100 us (7%)
  between operations  27.1 us (2%)
    all_to_all x42, waiting for transfers between devices, exchange(): return lax.all_to_all(parts, 'seq', split_axis=0, concat_axis=0, tiled=True)  228 us
    all_to_all x42, starting transfers between devices, exchange(): return lax.all_to_all(parts, 'seq', split_axis=0, concat_axis=0, tiled=True)  174 us
    dot_general x17, matrix products, matmul(): return jnp.dot(left_side, right_side, preferred_element_type=F32)  159 us
    dot_general x38, matrix products, contract(): lax.dot_general(left_side, right_side, (((left_dim,), (right_dim,)), ((),...  156 us
    pallas_call x4, Pallas kernels, attend_back(): pl.pallas_call(attend_back_kernel, grid=(count,), in_specs=[pl.BlockSpec(...  88.4 us
    pallas_call x4, Pallas kernels, attend(): pl.pallas_call(attend_kernel, grid=(count,), in_specs=[pl.BlockSpec(memor...  59.2 us
    sub x7, other arithmetic, adam_update(): weight - rate * (mean_hat / (jnp.sqrt(square_hat) + ADAM_EPSILON) + WEIGH...  54.3 us
    all_gather x6, waiting for transfers between devices, gather_owners(): return lax.all_gather(item, 'fsdp', axis=0, tiled=True)  37.1 us
  transfers between devices with their start and end apart: 60, of which 29 were waited for; matrix products, arithmetic and copies ran while one was open for 35% of the time, Pallas kernels for 13%

profile of v1, /device:TPU:0, one launch (start us, length us, event | category | flops | bytes accessed | tf_op | source)
XLA Modules:
  0.0 1507.2 jit_solution(13438598348043654426)
XLA Ops:
  21.7 14.7 all-gather.9
  37.0 18.4 %fusion.91 = bf16[2048,768]{1,0:T(8,128)(2,1)} fusion(bf16[4016,768]{1,0:T(8,128)(2,1)} %convert_element_type.390, s32[2048]{0:T(1024)S(1)} %bitcast.665), kind=kOutput, calls=%fused_computation.133 | convolution fusion | flops 12643041280 | bytes 9322496 | tf_op jit(solution)/shard_map/dot_general | solution.py:28
  55.7 18.4 %fusion.92 = bf16[2048,768]{1,0:T(8,128)(2,1)} fusion(bf16[4016,768]{1,0:T(8,128)(2,1)} %convert_element_type.390, s32[2048]{0:T(1024)S(1)} %bitcast.664), kind=kOutput, calls=%fused_computation.134 | convolution fusion | flops 12643041280 | bytes 9322496 | tf_op jit(solution)/shard_map/dot_general | solution.py:28
  96.3 16.4 %all_gather.57 = f32[8,80,128]{2,1,0:T(8,128)S(1)} all-gather(f32[1,80,128]{2,1,0:T(8,128)S(1)} %pad_bitcast_fusion.1), channel_id=1, replica_groups=mesh['seq'=4,'fsdp'=8] {'fsdp'}, dimensions={0}, use_global_device_ids=true | all-gather | bytes 368640 | tf_op jit(solution)/shard_map/all_gather | solution.py:575
  128.8 26.4 %reduce-scatter.10.cloned.1.call-done = bf16[1,256,768]{2,1,0:T(8,128)(2,1)} async-done(((bf16[8,256,768]{2,1,0:T(8,128)(2,1)}), bf16[1,256,768]{2,1,0:T(8,128)(2,1)}) %reduce-scatter.10.cloned.1.call-update) | async-done | bytes 393232 | tf_op jit(solution)/shard_map/reduce_scatter | solution.py:549
  173.7 14.7 attend.6
  192.8 14.8 attend.4
  237.5 8.4 multiply_convert_fusion.5
  245.9 14.7 all-gather.26.cloned.1.call-done
  291.0 22.3 %all-gather.22.cloned.1.call-done.weight_ref = bf16[768,3072]{1,0:T(8,128)(2,1)} async-done(((bf16[96,3072]{1,0:T(8,128)(2,1)}), bf16[768,3072]{1,0:T(8,128)(2,1)}) %all-gather.22.cloned.1.call-update) | async-done | bytes 4718608 | tf_op jit(solution)/shard_map/all_gather | solution.py:526
  322.3 18.8 %fusion.6 = f32[512,32,128]{2,1,0:T(8,128)} fusion(s32[512,65]{1,0:T(8,128)} %get-tuple-element.379, f32[512,65]{1,0:T(8,128)} %concatenate.100, s32[512,65]{1,0:T(8,128)} %get-tuple-element.378), kind=kOutput, calls=%fused_computation.11 | convolution fusion | flops 1642168320 | bytes 8787968 | tf_op jit(solution)/shard_map/rkh,rkl->rhl/dot_general | solution.py:615
  341.1 9.9 copy.496
  377.1 14.6 attend.5
  397.5 15.1 %attend.7 = (bf16[4,1,192,256]{3,2,1,0:T(8,128)(2,1)}, f32[1,12,256]{2,1,0:T(8,128)S(1)}) custom-call(s32[1]{0:T(128)} %bitcast.49.length_ref, bf16[4,1,576,256]{3,2,1,0:T(8,128)(2,1)} %all-to-all-done.12.qkv_ref, f32[3,1792,256]{2,1,0:T(8,128)} %copy-done.1), custom_call_target="tpu_custom_call" | custom-call | flops 805306368 | bytes 6684672 | tf_op jit(solution)/shard_map/attend/pallas_call | solution.py:116
  441.3 8.3 multiply_convert_fusion.4
  492.1 15.8 %all_gather.63 = bf16[512,768]{1,0:T(8,128)(2,1)S(1)} all-gather(bf16[64,768]{1,0:T(8,128)(2,1)S(1)} %bitcast.637), channel_id=1, replica_groups=mesh['seq'=4,'fsdp'=8] {'fsdp'}, dimensions={0}, use_global_device_ids=true | all-gather | bytes 884736 | tf_op jit(solution)/shard_map/all_gather | solution.py:641
  519.1 14.0 all-gather.10
  548.8 32.1 %reduce-scatter.14.cloned.1.call-done = f32[64,768]{1,0:T(8,128)} async-done(((f32[512,768]{1,0:T(8,128)}), f32[64,768]{1,0:T(8,128)}) %reduce-scatter.14.cloned.1.call-update) | async-done | bytes 196624 | tf_op jit(solution)/shard_map/reduce_scatter | solution.py:658
  603.5 9.4 fusion.43
  613.0 8.2 fusion.29
  671.8 21.7 %attend_back.5 = (bf16[4,1,576,256]{3,2,1,0:T(8,128)(2,1)S(1)}, f32[3,1,2048]{2,1,0:T(1,128)S(1)}) custom-call(s32[1]{0:T(128)} %bitcast.49.length_ref, bf16[4,1,576,256]{3,2,1,0:T(8,128)(2,1)} %all-to-all-done.12.qkv_ref, bf16[4,1,192,256]{3,2,1,0:T(8,128)(2,1)S(1)} %all-to-all-done.22.out_grad_ref, f32[1,12,256]{2,1,0:T(8,128)S(1)} %copy-done.24, ...), custom_call_target="tpu_custom_call" | custom-call | flops 2013265920 | bytes 7864320 | tf_op jit(solution)/shard_map/attend_back/pallas_call | solution.py:206
  701.3 8.5 all-to-all-done.23
  719.8 9.0 all_to_all.230.out_grad_ref
  728.8 22.2 %attend_back.4 = (bf16[4,1,576,256]{3,2,1,0:T(8,128)(2,1)}, f32[3,1,2048]{2,1,0:T(1,128)S(1)}) custom-call(s32[1]{0:T(128)} %bitcast.length_ref, bf16[4,1,576,256]{3,2,1,0:T(8,128)(2,1)S(1)} %all-to-all-done.4.qkv_ref, bf16[4,1,192,256]{3,2,1,0:T(8,128)(2,1)S(1)} %all_to_all.230.out_grad_ref, f32[1,12,256]{2,1,0:T(8,128)S(1)} %copy-done.22, ...), custom_call_target="tpu_custom_call" | custom-call | flops 2013265920 | bytes 7864320 | tf_op jit(solution)/shard_map/attend_back/pallas_call | solution.py:206
  772.3 8.8 convolution_convert_fusion.3
  801.5 9.5 fusion.36
  811.0 8.1 fusion.22
  882.6 9.9 reduce-scatter.18.cloned.1.call-done
  892.6 22.3 %attend_back.6 = (bf16[4,1,576,256]{3,2,1,0:T(8,128)(2,1)}, f32[3,1,2048]{2,1,0:T(1,128)S(1)}) custom-call(s32[1]{0:T(128)} %bitcast.length_ref, bf16[4,1,576,256]{3,2,1,0:T(8,128)(2,1)S(1)} %copy-done.5, bf16[4,1,192,256]{3,2,1,0:T(8,128)(2,1)S(1)} %all-to-all-done.26.out_grad_ref, f32[1,12,256]{2,1,0:T(8,128)S(1)} %copy-done.20, f32[3,1792,256]{2,1,0:T(8,128)} %copy-done), custom_call_target="tpu_custom_call" | custom-call | flops 2013265920 | bytes 7864320 | tf_op jit(solution)/shard_map/attend_back/pallas_call | solution.py:206
  919.4 22.3 %attend_back.7 = (bf16[4,1,576,256]{3,2,1,0:T(8,128)(2,1)}, f32[3,1,2048]{2,1,0:T(1,128)S(1)}) custom-call(s32[1]{0:T(128)} %bitcast.49.length_ref, bf16[4,1,576,256]{3,2,1,0:T(8,128)(2,1)S(1)} %copy-done.3, bf16[4,1,192,256]{3,2,1,0:T(8,128)(2,1)S(1)} %all-to-all-done.30.out_grad_ref, f32[1,12,256]{2,1,0:T(8,128)S(1)} %get-tuple-element.115.lse_ref, ...), custom_call_target="tpu_custom_call" | custom-call | flops 2013265920 | bytes 7864320 | tf_op jit(solution)/shard_map/attend_back/pallas_call | solution.py:206
  950.7 7.9 all-to-all-done.31
  965.2 9.7 all_to_all.231
  974.9 8.8 convolution_convert_fusion
  993.2 20.0 %all-gather.32.cloned.1.call-done = bf16[32,192,256]{2,1,0:T(8,128)(2,1)} async-done(((bf16[4,192,256]{2,1,0:T(8,128)(2,1)}), bf16[32,192,256]{2,1,0:T(8,128)(2,1)}) %all-gather.32.cloned.1.call-update) | async-done | bytes 3145744 | tf_op jit(solution)/shard_map/all_gather | solution.py:731
  1025.4 8.2 multiply_convert_fusion
  1033.6 8.6 copy.472
  1049.6 68.7 %all-to-all-done.33 = bf16[4,192,4016]{2,1,0:T(8,128)(2,1)} async-done(((bf16[4,192,4016]{2,1,0:T(8,128)(2,1)}), bf16[4,192,4016]{2,1,0:T(8,128)(2,1)}, u32[]{:S(2)}, u32[]{:S(2)}) %all-to-all-start.33) | async-done | bytes 6168608 | tf_op jit(solution)/shard_map/all_to_all | solution.py:317
  1150.6 22.0 %all-to-all-done.36 = bf16[4,96,3072]{2,1,0:T(8,128)(2,1)} async-done(((bf16[4,96,3072]{2,1,0:T(8,128)(2,1)}), bf16[4,96,3072]{2,1,0:T(8,128)(2,1)}, u32[]{:S(2)}, u32[]{:S(2)}) %all-to-all-start.36) | async-done | bytes 2359328 | tf_op jit(solution)/shard_map/all_to_all | solution.py:317
  1187.8 8.7 all-gather.7
  1222.6 10.3 all-to-all-done.37
  1237.3 30.2 %fusion.14 = f32[192,4016]{1,0:T(8,128)} fusion(f32[192,4016]{1,0:T(8,128)} %convert_reduce_fusion, bf16[192,8192]{1,0:T(8,128)(2,1)} %reshape.1180, s32[8192]{0:T(1024)S(1)} %bitcast.649), kind=kOutput, calls=%fused_computation.48 | convolution fusion | flops 12666913792 | bytes 9347072 | tf_op jit(solution)/shard_map/dot_general | solution.py:28
  1282.6 31.0 %multiply_reduce_fusion.2 = (f32[]{:T(128)}, bf16[192,4016]{1,0:T(8,128)(2,1)}) fusion(f32[192,4016]{1,0:T(8,128)} %fusion.14, bf16[192,8192]{1,0:T(8,128)(2,1)} %reshape.1185, s32[8192]{0:T(1024)S(1)} %bitcast.648), kind=kOutput, calls=%fused_computation.135 | convolution fusion | flops 12669998080 | bytes 7804932 | tf_op jit(solution)/shard_map/dot_general | solution.py:28
  1320.1 12.0 all_to_all.232
  1349.5 18.7 %all-to-all-done.45 = bf16[4,384,768]{2,1,0:T(8,128)(2,1)} async-done(((bf16[4,384,768]{2,1,0:T(8,128)(2,1)}), bf16[4,384,768]{2,1,0:T(8,128)(2,1)}, u32[]{:S(2)}, u32[]{:S(2)}) %all-to-all-start.45) | async-done | bytes 2359328 | tf_op jit(solution)/shard_map/all_to_all | solution.py:317
  1378.4 24.3 %multiply_subtract_fusion.1 = (f32[2,4,96,3072]{3,2,1,0:T(8,128)}, f32[2,4,96,3072]{3,2,1,0:T(8,128)}, f32[2,4,96,3072]{3,2,1,0:T(8,128)}) fusion(f32[2,4,96,3072]{3,2,1,0:T(8,128)} %param.49, f32[]{:T(128)} %min.3, bf16[1,4,96,3072]{3,2,1,0:T(8,128)(2,1)} %bitcast.169, bf16[1,4,96,3072]{3,2,1,0:T(8,128)(2,1)S(1)} %bitcast.585, ...), kind=kLoop, calls=%fused_computation.23 | loop fusion | flops 42467328 | bytes 61341700 | tf_op jit(solution)/shard_map/sub | solution.py:458
  1402.8 20.1 %multiply_subtract_fusion = (f32[2,4,384,768]{3,2,1,0:T(8,128)}, f32[2,4,384,768]{3,2,1,0:T(8,128)}, f32[2,4,384,768]{3,2,1,0:T(8,128)}) fusion(f32[2,4,384,768]{3,2,1,0:T(8,128)S(1)} %bitcast.583, f32[]{:T(128)} %min.3, bf16[1,4,384,768]{3,2,1,0:T(8,128)(2,1)S(1)} %bitcast.584, bf16[1,4,384,768]{3,2,1,0:T(8,128)(2,1)} %bitcast.170, ...), kind=kLoop, calls=%fused_computation.20 | loop fusion | flops 42467328 | bytes 61341700 | tf_op jit(solution)/shard_map/sub | solution.py:458
  1422.9 25.4 %all-to-all-done.41.grad_ref = bf16[4,192,4016]{2,1,0:T(8,128)(2,1)} async-done(((bf16[4,192,4016]{2,1,0:T(8,128)(2,1)}), bf16[4,192,4016]{2,1,0:T(8,128)(2,1)}, u32[]{:S(2)}, u32[]{:S(2)}) %all-to-all-start.41) | async-done | bytes 6168608 | tf_op jit(solution)/shard_map/all_to_all | solution.py:317
  1452.9 33.9 %embed_adam.1 = (f32[4016,768]{1,0:T(8,128)}, f32[4016,768]{1,0:T(8,128)}, f32[4016,768]{1,0:T(8,128)}) custom-call(f32[1]{0:T(128)} %bitcast.161.clip_ref, bf16[4,192,4016]{2,1,0:T(8,128)(2,1)} %all-to-all-done.41.grad_ref, f32[4016,768]{1,0:T(8,128)} %weight_ref.1, f32[4016,768]{1,0:T(8,128)} %first_ref.1, f32[4016,768]{1,0:T(8,128)} %second_ref.1), custom_call_target="tpu_custom_call" | custom-call | flops 61685760 | bytes 80191488 | tf_op jit(solution)/shard_map/embed_adam/pallas_call | solution.py:296
  (862 shorter events, 654.3 us)
Async XLA Ops:
  7.2 66.9 %all-gather.20.cloned.1.call-start = ((), (), s32[]{:S(2)}) async-start(), calls=%async_computation.55 | async-start | bytes 5308416 | tf_op jit(solution)/shard_map/all_gather | solution.py:526
  13.9 105.2 %reduce-scatter.12.cloned.1.call-start = ((), (), s32[]{:S(2)}) async-start(), calls=%async_computation.58 | async-start | bytes 3538944 | tf_op jit(solution)/shard_map/reduce_scatter | solution.py:549
  55.4 99.8 %reduce-scatter.10.cloned.1.call-start = ((), (), s32[]{:S(2)}) async-start(), calls=%async_computation.56 | async-start | bytes 3538944 | tf_op jit(solution)/shard_map/reduce_scatter | solution.py:549
  74.1 163.4 %all-gather.24.cloned.1.call-start = ((), (), s32[]{:S(2)}) async-start(), calls=%async_computation.66 | async-start | bytes 5308416 | tf_op jit(solution)/shard_map/all_gather | solution.py:526
  79.8 180.9 %all-gather.26.cloned.1.call-start = ((), (), s32[]{:S(2)}) async-start(), calls=%async_computation.67 | async-start | bytes 5308416 | tf_op jit(solution)/shard_map/all_gather | solution.py:526
  86.4 226.8 %all-gather.22.cloned.1.call-start = ((), (), s32[]{:S(2)}) async-start(), calls=%async_computation.57 | async-start | bytes 5308416 | tf_op jit(solution)/shard_map/all_gather | solution.py:526
  90.0 351.3 %all-gather.28.cloned.1.call-start = ((), (), s32[]{:S(2)}) async-start(), calls=%async_computation.68 | async-start | bytes 5308416 | tf_op jit(solution)/shard_map/all_gather | solution.py:526
  90.9 358.7 %all-gather.30.cloned.1.call-start = ((), (), s32[]{:S(2)}) async-start(), calls=%async_computation.69 | async-start | bytes 5308416 | tf_op jit(solution)/shard_map/all_gather | solution.py:526
  124.8 36.7 %all-to-all-start.8 = ((bf16[4,1,576,256]{3,2,1,0:T(8,128)(2,1)}), bf16[4,1,576,256]{3,2,1,0:T(8,128)(2,1)S(1)}, u32[]{:S(2)}, u32[]{:S(2)}) async-start(bf16[4,1,576,256]{3,2,1,0:T(8,128)(2,1)} %get-tuple-element.94), calls=%async_computation.10 | async-start | bytes 2359296 | tf_op jit(solution)/shard_map/all_to_all | solution.py:317
  161.6 26.8 %all-to-all-start = ((bf16[4,1,576,256]{3,2,1,0:T(8,128)(2,1)}), bf16[4,1,576,256]{3,2,1,0:T(8,128)(2,1)S(1)}, u32[]{:S(2)}, u32[]{:S(2)}) async-start(bf16[4,1,576,256]{3,2,1,0:T(8,128)(2,1)} %get-tuple-element.87), calls=%async_computation.1 | async-start | bytes 2359296 | tf_op jit(solution)/shard_map/all_to_all | solution.py:317
  188.4 19.7 %all-to-all-start.9 = ((bf16[4,1,192,256]{3,2,1,0:T(8,128)(2,1)}), bf16[4,1,192,256]{3,2,1,0:T(8,128)(2,1)S(1)}, u32[]{:S(2)}, u32[]{:S(2)}) async-start(bf16[4,1,192,256]{3,2,1,0:T(8,128)(2,1)} %get-tuple-element.95), calls=%async_computation.11 | async-start | bytes 786432 | tf_op jit(solution)/shard_map/all_to_all | solution.py:317
  234.0 32.5 %all-to-all-start.10 = ((bf16[4,1,96,768]{3,2,1,0:T(8,128)(2,1)}), bf16[4,1,96,768]{3,2,1,0:T(8,128)(2,1)S(1)}, u32[]{:S(2)}, u32[]{:S(2)}) async-start(bf16[4,1,96,768]{3,2,1,0:T(8,128)(2,1)} %bitcast.592), calls=%async_computation.12 | async-start | bytes 1179648 | tf_op jit(solution)/shard_map/all_to_all | solution.py:317
  266.5 17.5 %all-to-all-start.3 = ((bf16[4,1,96,768]{3,2,1,0:T(8,128)(2,1)}), bf16[4,1,96,768]{3,2,1,0:T(8,128)(2,1)S(1)}, u32[]{:S(2)}, u32[]{:S(2)}) async-start(bf16[4,1,96,768]{3,2,1,0:T(8,128)(2,1)} %bitcast.28), calls=%async_computation.4 | async-start | bytes 1179648 | tf_op jit(solution)/shard_map/all_to_all | solution.py:317
  284.1 34.5 %all-to-all-start.11 = ((bf16[4,1,96,768]{3,2,1,0:T(8,128)(2,1)}), bf16[4,1,96,768]{3,2,1,0:T(8,128)(2,1)S(1)}, u32[]{:S(2)}, u32[]{:S(2)}) async-start(bf16[4,1,96,768]{3,2,1,0:T(8,128)(2,1)} %bitcast.623), calls=%async_computation.13 | async-start | bytes 1179648 | tf_op jit(solution)/shard_map/all_to_all | solution.py:317
  318.6 47.7 %all-to-all-start.4 = ((bf16[4,1,576,256]{3,2,1,0:T(8,128)(2,1)}), bf16[4,1,576,256]{3,2,1,0:T(8,128)(2,1)S(1)}, u32[]{:S(2)}, u32[]{:S(2)}) async-start(bf16[4,1,576,256]{3,2,1,0:T(8,128)(2,1)} %get-tuple-element.91), calls=%async_computation.5 | async-start | bytes 2359296 | tf_op jit(solution)/shard_map/all_to_all | solution.py:317
  366.3 26.0 %all-to-all-start.12 = ((bf16[4,1,576,256]{3,2,1,0:T(8,128)(2,1)}), bf16[4,1,576,256]{3,2,1,0:T(8,128)(2,1)}, u32[]{:S(2)}, u32[]{:S(2)}) async-start(bf16[4,1,576,256]{3,2,1,0:T(8,128)(2,1)} %copy-done.6), calls=%async_computation.14 | async-start | bytes 2359296 | tf_op jit(solution)/shard_map/all_to_all | solution.py:317
  392.3 20.9 %all-to-all-start.5 = ((bf16[4,1,192,256]{3,2,1,0:T(8,128)(2,1)}), bf16[4,1,192,256]{3,2,1,0:T(8,128)(2,1)}, u32[]{:S(2)}, u32[]{:S(2)}) async-start(bf16[4,1,192,256]{3,2,1,0:T(8,128)(2,1)} %get-tuple-element.92), calls=%async_computation.6 | async-start | bytes 786432 | tf_op jit(solution)/shard_map/all_to_all | solution.py:317
  424.6 12.5 all-to-all-start.6
  437.1 18.4 %all-to-all-start.14 = ((bf16[4,1,96,768]{3,2,1,0:T(8,128)(2,1)}), bf16[4,1,96,768]{3,2,1,0:T(8,128)(2,1)}, u32[]{:S(2)}, u32[]{:S(2)}) async-start(bf16[4,1,96,768]{3,2,1,0:T(8,128)(2,1)} %bitcast.593), calls=%async_computation.16 | async-start | bytes 1179648 | tf_op jit(solution)/shard_map/all_to_all | solution.py:317
  455.5 18.5 %all-to-all-start.7 = ((bf16[4,1,96,768]{3,2,1,0:T(8,128)(2,1)}), bf16[4,1,96,768]{3,2,1,0:T(8,128)(2,1)}, u32[]{:S(2)}, u32[]{:S(2)}) async-start(bf16[4,1,96,768]{3,2,1,0:T(8,128)(2,1)} %bitcast.626), calls=%async_computation.8 | async-start | bytes 1179648 | tf_op jit(solution)/shard_map/all_to_all | solution.py:317
  478.2 102.7 %reduce-scatter.14.cloned.1.call-start = ((), (), s32[]{:S(2)}) async-start(), calls=%async_computation.59 | async-start | bytes 1769472 | tf_op jit(solution)/shard_map/reduce_scatter | solution.py:658
  599.1 13.8 all-to-all-start.16
  603.3 251.4 %reduce-scatter.16.cloned.1.call-start = ((), (), s32[]{:S(2)}) async-start(), calls=%async_computation.60 | async-start | bytes 5308416 | tf_op jit(solution)/shard_map/reduce_scatter | solution.py:465
  666.9 28.2 %all-to-all-start.17 = ((bf16[4,1,96,768]{3,2,1,0:T(8,128)(2,1)}), bf16[4,1,96,768]{3,2,1,0:T(8,128)(2,1)}, u32[]{:S(2)}, u32[]{:S(2)}) async-start(bf16[4,1,96,768]{3,2,1,0:T(8,128)(2,1)} %bitcast.624), calls=%async_computation.20 | async-start | bytes 1179648 | tf_op jit(solution)/shard_map/all_to_all | solution.py:317
  695.1 14.7 all-to-all-start.23
  751.0 14.6 all-to-all-start.19
  755.4 108.3 %reduce-scatter.20.cloned.1.call-start = ((), (), s32[]{:S(2)}) async-start(), calls=%async_computation.62 | async-start | bytes 5308416 | tf_op jit(solution)/shard_map/reduce_scatter | solution.py:465
  772.3 120.3 %reduce-scatter.18.cloned.1.call-start = ((), (), s32[]{:S(2)}) async-start(), calls=%async_computation.61 | async-start | bytes 5308416 | tf_op jit(solution)/shard_map/reduce_scatter | solution.py:465
  783.4 14.1 all-to-all-start.28
  797.5 13.5 all-to-all-start.24
  801.0 164.0 %reduce-scatter.22.cloned.1.call-start = ((), (), s32[]{:S(2)}) async-start(), calls=%async_computation.63 | async-start | bytes 5308416 | tf_op jit(solution)/shard_map/reduce_scatter | solution.py:465
  850.3 13.5 all-to-all-start.29
  879.1 35.7 %all-to-all-start.30 = ((bf16[4,1,192,256]{3,2,1,0:T(8,128)(2,1)}), bf16[4,1,192,256]{3,2,1,0:T(8,128)(2,1)S(1)}, u32[]{:S(2)}, u32[]{:S(2)}) async-start(bf16[4,1,192,256]{3,2,1,0:T(8,128)(2,1)} %bitcast.123), calls=%async_computation.36 | async-start | bytes 786432 | tf_op jit(solution)/shard_map/all_to_all | solution.py:317
  914.9 26.8 %all-to-all-start.27 = ((bf16[4,1,576,256]{3,2,1,0:T(8,128)(2,1)}), bf16[4,1,576,256]{3,2,1,0:T(8,128)(2,1)}, u32[]{:S(2)}, u32[]{:S(2)}) async-start(bf16[4,1,576,256]{3,2,1,0:T(8,128)(2,1)} %get-tuple-element.111), calls=%async_computation.32 | async-start | bytes 2359296 | tf_op jit(solution)/shard_map/all_to_all | solution.py:317
  941.7 16.9 %all-to-all-start.31 = ((bf16[4,1,576,256]{3,2,1,0:T(8,128)(2,1)}), bf16[4,1,576,256]{3,2,1,0:T(8,128)(2,1)S(1)}, u32[]{:S(2)}, u32[]{:S(2)}) async-start(bf16[4,1,576,256]{3,2,1,0:T(8,128)(2,1)} %get-tuple-element.116), calls=%async_computation.37 | async-start | bytes 2359296 | tf_op jit(solution)/shard_map/all_to_all | solution.py:317
  946.0 67.2 %all-gather.32.cloned.1.call-start = ((), (), s32[]{:S(2)}) async-start(), calls=%async_computation.70 | async-start | bytes 3538944 | tf_op jit(solution)/shard_map/all_gather | solution.py:731
  974.9 150.7 %reduce-scatter.24.cloned.1.call-start = ((), (), s32[]{:S(2)}) async-start(), calls=%async_computation.64 | async-start | bytes 5308416 | tf_op jit(solution)/shard_map/reduce_scatter | solution.py:465
  983.7 235.1 %reduce-scatter.26.cloned.1.call-start = ((), (), s32[]{:S(2)}) async-start(), calls=%async_computation.65 | async-start | bytes 5308416 | tf_op jit(solution)/shard_map/reduce_scatter | solution.py:465
  1042.2 76.0 %all-to-all-start.33 = ((bf16[4,192,4016]{2,1,0:T(8,128)(2,1)}), bf16[4,192,4016]{2,1,0:T(8,128)(2,1)}, u32[]{:S(2)}, u32[]{:S(2)}) async-start(bf16[4,192,4016]{2,1,0:T(8,128)(2,1)} %bitcast.581), calls=%async_computation.39 | async-start | bytes 12582912 | tf_op jit(solution)/shard_map/all_to_all | solution.py:317
  1142.3 30.3 %all-to-all-start.36 = ((bf16[4,96,3072]{2,1,0:T(8,128)(2,1)}), bf16[4,96,3072]{2,1,0:T(8,128)(2,1)}, u32[]{:S(2)}, u32[]{:S(2)}) async-start(bf16[4,96,3072]{2,1,0:T(8,128)(2,1)} %broadcast_in_dim.34), calls=%async_computation.44 | async-start | bytes 4718592 | tf_op jit(solution)/shard_map/all_to_all | solution.py:317
  1146.8 120.6 %all-gather.34.cloned.1.call-start = ((), (), s32[]{:S(2)}) async-start(), calls=%async_computation.71 | async-start | bytes 3538944 | tf_op jit(solution)/shard_map/all_gather | solution.py:731
  1185.2 13.0 all-to-all-start.32
  1200.8 32.1 %all-to-all-start.37 = ((bf16[4,384,768]{2,1,0:T(8,128)(2,1)}), bf16[4,384,768]{2,1,0:T(8,128)(2,1)S(1)}, u32[]{:S(2)}, u32[]{:S(2)}) async-start(bf16[4,384,768]{2,1,0:T(8,128)(2,1)} %broadcast_in_dim.35), calls=%async_computation.45 | async-start | bytes 4718592 | tf_op jit(solution)/shard_map/all_to_all | solution.py:317
  1232.9 42.8 %all-to-all-start.38 = ((bf16[4,96,768]{2,1,0:T(8,128)(2,1)}), bf16[4,96,768]{2,1,0:T(8,128)(2,1)}, u32[]{:S(2)}, u32[]{:S(2)}) async-start(bf16[4,96,768]{2,1,0:T(8,128)(2,1)} %maximum_bitcast_fusion), calls=%async_computation.47 | async-start | bytes 1179648 | tf_op jit(solution)/shard_map/all_to_all | solution.py:317
  1278.5 41.6 %all-to-all-start.44 = ((bf16[4,96,3072]{2,1,0:T(8,128)(2,1)}), bf16[4,96,3072]{2,1,0:T(8,128)(2,1)S(1)}, u32[]{:S(2)}, u32[]{:S(2)}) async-start(bf16[4,96,3072]{2,1,0:T(8,128)(2,1)} %broadcast_in_dim.39), calls=%async_computation.53 | async-start | bytes 4718592 | tf_op jit(solution)/shard_map/all_to_all | solution.py:317
  1334.8 33.4 %all-to-all-start.45 = ((bf16[4,384,768]{2,1,0:T(8,128)(2,1)}), bf16[4,384,768]{2,1,0:T(8,128)(2,1)}, u32[]{:S(2)}, u32[]{:S(2)}) async-start(bf16[4,384,768]{2,1,0:T(8,128)(2,1)} %broadcast_in_dim.40), calls=%async_computation.54 | async-start | bytes 4718592 | tf_op jit(solution)/shard_map/all_to_all | solution.py:317
  1373.1 75.1 %all-to-all-start.41 = ((bf16[4,192,4016]{2,1,0:T(8,128)(2,1)}), bf16[4,192,4016]{2,1,0:T(8,128)(2,1)}, u32[]{:S(2)}, u32[]{:S(2)}) async-start(bf16[4,192,4016]{2,1,0:T(8,128)(2,1)} %broadcast_in_dim.36), calls=%async_computation.50 | async-start | bytes 12582912 | tf_op jit(solution)/shard_map/all_to_all | solution.py:317
  1449.1 39.0 %all-to-all-start.42 = ((bf16[4,96,768]{2,1,0:T(8,128)(2,1)}), bf16[4,96,768]{2,1,0:T(8,128)(2,1)S(1)}, u32[]{:S(2)}, u32[]{:S(2)}) async-start(bf16[4,96,768]{2,1,0:T(8,128)(2,1)} %broadcast_in_dim.37), calls=%async_computation.51 | async-start | bytes 1179648 | tf_op jit(solution)/shard_map/all_to_all | solution.py:317
  (214 other events, 5239.5 us)
Sparse Core Ops, SparseCore 0:
  14.0 54.5 all-gather.19
  71.4 41.6 reduce-scatter.11
  116.0 39.1 reduce-scatter.9
  157.3 50.7 all-gather.23
  210.1 50.5 all-gather.25
  262.7 50.5 all-gather.21
  315.5 50.5 all-gather.27
  367.7 50.5 all-gather.29
  548.9 31.9 reduce-scatter.13
  629.5 55.3 reduce-scatter.15
  772.4 64.0 reduce-scatter.19
  839.2 53.3 reduce-scatter.17
  895.5 53.3 reduce-scatter.21
  975.0 38.1 all-gather.31
  1015.9 53.8 reduce-scatter.23
  1072.5 53.3 reduce-scatter.25
  1150.7 37.8 all-gather.33

commit v2 on v1

--- a/solution.py
+++ b/solution.py
@@ -131,7 +131,7 @@
         ],
         compiler_params=pltpu.CompilerParams(vmem_limit_bytes=VMEM_LIMIT),
         cost_estimate=pl.CostEstimate(
-            flops=4 * count * heads * total * total * HD,
+            flops=80 * count * heads * total * total * HD,
             bytes_accessed=2 * qkv.size + 4 * tile.size,
             transcendentals=count * heads * total * total,
         ),
@@ -228,7 +228,7 @@
         ],
         compiler_params=pltpu.CompilerParams(vmem_limit_bytes=VMEM_LIMIT),
         cost_estimate=pl.CostEstimate(
-            flops=10 * count * heads * total * total * HD,
+            flops=125 * count * heads * total * total * HD,
             bytes_accessed=4 * qkv.size + 4 * tile.size,
             transcendentals=count * heads * total * total,
         ),
@@ -279,30 +279,33 @@
     )(hidden, gain[None], dense)
 
 
-def embed_adam_kernel(rate, clip_ref, grad_ref, weight_ref, first_ref, second_ref, *out_refs):
-    grad = jnp.concatenate([grad_ref[way].T for way in range(grad_ref.shape[0])], 1).astype(F32)
+def embed_adam_kernel(rate, clip_ref, seq_ref, weight_ref, first_ref, second_ref, *refs):
+    ways = len(refs) - 3
+    held = [ref[...] for ref in refs[:ways]]
+    ordered = []
+    for source in range(ways):
+        part = held[0]
+        for distance in range(1, ways):
+            part = jnp.where(seq_ref[0] == source ^ distance, held[distance], part)
+        ordered.append(part.astype(F32).T)
+    grad = jnp.concatenate(ordered, 1)
     updated = adam_update(
         weight_ref[...], grad * clip_ref[0], first_ref[...], second_ref[...], rate
     )
-    for ref, value in zip(out_refs, updated):
+    for ref, value in zip(refs[ways:], updated):
         ref[...] = value
 
 
-def embed_adam(weight, grad, first, second, clip, rate):
+def embed_adam(weight, grads, first, second, clip, rate):
     rows, width = weight.shape
-    ways, part, _ = grad.shape
     block = min(256, rows)
     state = pl.BlockSpec((block, width), lambda i: (i, 0))
     return pl.pallas_call(
         functools.partial(embed_adam_kernel, rate),
         grid=(pl.cdiv(rows, block),),
-        in_specs=[
-            pl.BlockSpec(memory_space=pltpu.SMEM),
-            pl.BlockSpec((ways, part, block), lambda i: (0, 0, i)),
-            state,
-            state,
-            state,
-        ],
+        in_specs=[pl.BlockSpec(memory_space=pltpu.SMEM)] * 2
+        + [state] * 3
+        + [pl.BlockSpec((grads[0].shape[0], block), lambda i: (0, i))] * len(grads),
         out_specs=[state, state, state],
         out_shape=[jax.ShapeDtypeStruct((rows, width), F32)] * 3,
         compiler_params=pltpu.CompilerParams(vmem_limit_bytes=VMEM_LIMIT),
@@ -310,20 +313,83 @@
             flops=20 * rows * width, bytes_accessed=26 * rows * width, transcendentals=rows * width
         ),
         name="embed_adam",
-    )(clip.reshape(1), grad, weight, first, second)
+    )(clip.reshape(1), lax.axis_index("seq").reshape(1), weight, first, second, *grads)
+
+
+def token_grad_kernel(ids_ref, *refs):
+    *moved_refs, head_ref, out_ref, sums_ref = refs
+    block = sums_ref.shape[0]
+
+    @pl.when(pl.program_id(1) == 0)
+    def _():
+        sums_ref[...] = jnp.zeros_like(sums_ref)
+
+    first = pl.program_id(0) * block
+    for batch, moved_ref in enumerate(moved_refs):
+        ids = ids_ref[0, batch : batch + 1, :]
+        vocab = lax.broadcasted_iota(jnp.int32, (block, ids.shape[1]), 0) + first
+        chosen = jnp.where(vocab == ids, 1.0, 0.0).astype(BF16)
+        moved = jnp.concatenate([moved_ref[0, way] for way in range(moved_ref.shape[1])], 1)
+        sums_ref[...] += contract(chosen, moved, 1, 1)
+
+    @pl.when(pl.program_id(1) == pl.num_programs(1) - 1)
+    def _():
+        out_ref[...] = (sums_ref[...].T + head_ref[...]).astype(BF16)
+
+
+def token_grad(ids, moved, head_grad):
+    owners, count, tokens = ids.shape
+    part, vocab_rows = head_grad.shape
+    block = min(1024, -(-vocab_rows // 128) * 128)
+    return pl.pallas_call(
+        token_grad_kernel,
+        grid=(pl.cdiv(vocab_rows, block), owners),
+        in_specs=[pl.BlockSpec((1, count, tokens), lambda i, j: (j, 0, 0))]
+        + [pl.BlockSpec((1,) + item.shape[1:], lambda i, j: (j, 0, 0, 0)) for item in moved]
+        + [pl.BlockSpec((part, block), lambda i, j: (0, i))],
+        out_specs=pl.BlockSpec((part, block), lambda i, j: (0, i)),
+        out_shape=jax.ShapeDtypeStruct((part, vocab_rows), BF16),
+        scratch_shapes=[pltpu.VMEM((block, part), F32)],
+        compiler_params=pltpu.CompilerParams(vmem_limit_bytes=VMEM_LIMIT),
+        cost_estimate=pl.CostEstimate(
+            flops=4 * vocab_rows * owners * count * tokens * part,
+            bytes_accessed=8 * owners * count * tokens * part,
+            transcendentals=0,
+        ),
+        name="token_grad",
+    )(ids, *moved, head_grad)
 
 
 def exchange(parts):
     return lax.all_to_all(parts, "seq", split_axis=0, concat_axis=0, tiled=True)
 
 
+def to_relative(part, distance):
+    ways = lax.axis_size("seq")
+    return lax.ppermute(part, "seq", [(way, way ^ distance) for way in range(ways)])
+
+
 def share(part):
-    ways = lax.axis_size("seq")
-    return exchange(jnp.broadcast_to(part[None], (ways,) + part.shape))
+    return [part] + [to_relative(part, k) for k in range(1, lax.axis_size("seq"))]
+
+
+def by_source(parts):
+    seq_index = lax.axis_index("seq")
+    first = parts[0]
+    whole = jnp.zeros(first.shape[:1] + (len(parts),) + first.shape[1:], first.dtype)
+    for distance, part in enumerate(parts):
+        at = (0, seq_index ^ distance) + (0,) * (first.ndim - 1)
+        whole = lax.dynamic_update_slice(whole, part[:, None], at)
+    return whole
 
 
 def sum_over_seq(parts):
-    return jnp.sum(exchange(parts).astype(F32), 0)
+    seq_index = lax.axis_index("seq")
+    mine = lax.dynamic_index_in_dim(parts, seq_index, 0, False).astype(F32)
+    for k in range(1, lax.axis_size("seq")):
+        part = lax.dynamic_index_in_dim(parts, seq_index ^ k, 0, False)
+        mine = mine + to_relative(part, k).astype(F32)
+    return mine
 
 
 def as_rows(flat):
@@ -379,6 +445,7 @@
         lse=lse,
         mixed_t=mixed_t,
         after_attn=after_attn,
+        mixed=mixed,
         scale_two=scale_two,
         normed_two=normed_two,
         router_probs=router_probs,
@@ -391,17 +458,12 @@
     return (result, kept)
 
 
-def layer_backward(
-    grad_out, kept, weights, gain_one, gain_two, router_w, tile, moe, lengths, gates
-):
-    dense, upward_w, downward_w = weights
+def experts_backward(grad_out, kept, weights, moe):
+    _, upward_w, downward_w = weights
     count, rows, width = grad_out.shape
-    attend_w, output_w = dense[:, : 3 * width], dense[:, 3 * width :]
     ways = lax.axis_size("seq")
-    dispatch, onehot = moe
+    dispatch, _ = moe
     slots = dispatch.shape[1]
-    flat = (count * rows, width)
-    grad_gate = jnp.sum(grad_out * kept["token_out"], -1, keepdims=True)
     grad_token = (kept["gate"] * grad_out).astype(BF16)
     sent = jnp.einsum("nst,ntd->nsd", dispatch, grad_token, preferred_element_type=F32).astype(BF16)
     sent = sent.reshape(count, ways, slots // ways, width).transpose(1, 0, 2, 3)
@@ -410,7 +472,18 @@
     grad_upward = jax.vjp(jax.nn.gelu, kept["upward"])[1](grad_activated)[0].astype(BF16)
     grad_rows = contract(grad_upward, upward_w, 1, 1).astype(BF16)
     back = exchange(grad_rows.reshape(ways, count, slots // ways, width))
-    back, *first_gate = after(back, *gates[0])
+    return (back, ((kept["expert_rows"], grad_upward), (kept["activated"], grad_expert)))
+
+
+def mixed_backward(grad_out, back, kept, weights, gain_two, router_w, moe):
+    dense, _, _ = weights
+    count, rows, width = grad_out.shape
+    output_w = dense[:, 3 * width :]
+    ways = lax.axis_size("seq")
+    dispatch, onehot = moe
+    slots = dispatch.shape[1]
+    flat = (count * rows, width)
+    grad_gate = jnp.sum(grad_out * kept["token_out"], -1, keepdims=True)
     back = back.transpose(1, 0, 2, 3).reshape(count, slots, width)
     grad_normed = jnp.einsum("nst,nsd->ntd", dispatch, back, preferred_element_type=F32)
     grad_probs = onehot * grad_gate
@@ -428,8 +501,17 @@
     grad_attn = grad_mid.astype(BF16)
     grad_mixed_t = contract(output_w, grad_attn, 1, 1).astype(BF16)
     grad_mixed_t = exchange(grad_mixed_t.reshape(ways, 1, width // ways, rows))
-    grad_mixed_t, *second_gate = after(grad_mixed_t, *gates[1])
+    return (grad_mixed_t, grad_mid, (kept["mixed_t"], grad_attn), (grad_gain_two, grad_router))
+
+
+def attention_backward(grad_mixed_t, grad_mid, kept, weights, gain_one, tile, lengths, piece):
+    dense, _, _ = weights
+    count, rows, width = kept["hidden"].shape
+    attend_w = dense[:, : 3 * width]
+    flat = (count * rows, width)
+    grad_mixed_t, piece = after(grad_mixed_t, piece)
     grad_qkv, grad_relative = attend_back(kept["qkv"], grad_mixed_t, kept["lse"], tile, lengths)
+    grad_qkv, piece = after(grad_qkv, sum_over_seq(piece))
     grad_projected_t = exchange(grad_qkv).reshape(3 * width, rows)
     grad_first, grad_gain_one = rms_back(
         kept["hidden"].reshape(flat),
@@ -438,16 +520,20 @@
         contract(grad_projected_t, attend_w, 0, 1),
     )
     return (
-        (grad_mid + grad_first).reshape(grad_out.shape),
-        (
-            (kept["expert_rows"], grad_upward),
-            (kept["activated"], grad_expert),
-            (kept["normed_one"].reshape(flat), grad_projected_t),
-            (kept["mixed_t"], grad_attn),
-        ),
-        (grad_gain_one, grad_gain_two, grad_router, grad_relative),
-        (first_gate, second_gate),
-    )
+        (grad_mid + grad_first).reshape(count, rows, width),
+        (kept["normed_one"].reshape(flat), grad_projected_t),
+        (grad_gain_one, grad_relative),
+        piece,
+    )
+
+
+def weight_grad(pairs, left_dim, right_dim):
+    return contract(
+        jnp.concatenate([item[0] for item in pairs], left_dim),
+        jnp.concatenate([item[1] for item in pairs], right_dim),
+        left_dim,
+        right_dim,
+    ).astype(BF16)
 
 
 def adam_update(weight, grad, first, second, rate):
@@ -533,16 +619,28 @@
     own_ids, first_dense = after(token_ids[:, 0], first_dense)
     first_dense = gather_owners(first_dense)
     group_ids = lax.all_gather(own_ids, "fsdp", axis=0, tiled=False)
+    valid_own = (seq_index * rows + positions[:, 0] < lengths[:, None]).astype(F32)
+    teacher_own = teacher_weight[:, 0] / jnp.sum(teacher_weight[:, 0], -1, keepdims=True)
+    small = jnp.concatenate(
+        [
+            lax.optimization_barrier(item.astype(BF16)).astype(F32).reshape(-1)
+            for item in (gains_weight, bias_weight, router_weight)
+        ]
+        + [item.astype(F32).reshape(-1) for item in (valid_own, targets, teacher_index, teacher_own)]
+    )
+    small = lax.all_gather(as_rows(small), "fsdp", axis=0, tiled=False)
     embed_low = embed_weight.astype(BF16)
     vocab_ids = jnp.arange(vocab_rows)
     founds = []
     for batch in range(count):
         local_ids = group_ids[:, batch].reshape(-1) - owner_index * vocab_rows
+        if batch == count - 1:
+            local_ids, small = after(local_ids, small)
         founds.append(
             matmul((local_ids[:, None] == vocab_ids[None, :]).astype(BF16), embed_low).astype(BF16)
         )
-        if batch == 0:
-            founds[0], first_dense = after(founds[0], first_dense)
+        if batch == count - 1:
+            founds[-1], first_dense = after(founds[-1], first_dense)
     later = (attend_weight, output_weight, upward_weight, downward_weight)
     founds[-1], *later = after(founds[-1], *later)
     hiddens = [
@@ -563,16 +661,7 @@
             )
         )
 
-    valid_own = (seq_index * rows + positions[:, 0] < lengths[:, None]).astype(F32)
-    teacher_own = teacher_weight[:, 0] / jnp.sum(teacher_weight[:, 0], -1, keepdims=True)
-    small = jnp.concatenate(
-        [
-            lax.optimization_barrier(item.astype(BF16)).astype(F32).reshape(-1)
-            for item in (gains_weight, bias_weight, router_weight)
-        ]
-        + [item.astype(F32).reshape(-1) for item in (valid_own, targets, teacher_index, teacher_own)]
-    )
-    small = lax.all_gather(as_rows(small), "fsdp", axis=0, tiled=False).reshape(owners, -1)
+    small = small.reshape(owners, -1)
     pieces, at = [], 0
     for item in (gains_weight, bias_weight, router_weight, valid_own, targets, teacher_index, teacher_own):
         pieces.append(small[:, at : at + item.size])
@@ -621,6 +710,8 @@
     used = [lengths[batch : batch + 1] for batch in range(count)]
     for layer in range(layers):
         for batch in range(count):
+            if layer == 0 and batch:
+                hiddens[batch], wanted, _ = after(hiddens[batch], wanted, kept_all[0][batch - 1]["mixed"])
             hiddens[batch], kept_all[layer][batch] = layer_forward(
                 hiddens[batch],
                 weights[layer],
@@ -632,7 +723,9 @@
                 used[batch],
             )
         if layer == 0:
-            hiddens[-1], wanted = after(hiddens[-1], wanted)
+            every_id = lax.all_gather(group_ids, "seq", axis=0, tiled=False) - owner_index * vocab_rows
+            every_id = every_id.transpose(1, 2, 0, 3).reshape(owners, count, -1)
+            hiddens[-1], every_id = after(hiddens[-1], every_id)
     hidden = jnp.concatenate(hiddens, 0)
 
     final, scale_final = rms_norm(hidden, gains_full[2 * layers])
@@ -659,8 +752,12 @@
         matmul(grad_logits, embed_low), "fsdp", scatter_dimension=0, tiled=True
     )
     grad_picked = (grad_picked * factor).reshape(count, picks, width)
-    head_grad = (contract(picked, grad_logits, 0, 0) * factor).astype(BF16)
-    head_grad = sum_over_seq(head_grad.reshape(ways, part, vocab_rows))
+    head_grad = (matmul(lax.optimization_barrier(picked.T), grad_logits) * factor).astype(BF16)
+    head_grad = head_grad.reshape(ways, part, vocab_rows)
+    run = -(-vocab_rows // (128 * layers * count)) * 128
+    pieces = [head_grad[:, :, at : at + run] for at in range(0, vocab_rows, run)]
+    pieces += [None] * (layers * count - len(pieces))
+    summed = []
     grad_final = jnp.einsum(
         "npt,npd->ntd", chosen.astype(F32), grad_picked, precision=HIGHEST_PRECISION
     )
@@ -677,82 +774,84 @@
     gain_grads[2 * layers] = grad_gain_final
     router_grads, table_grads = [None] * layers, [None] * layers
     grad_parts = [None] * layers
-    gates = []
     for layer in reversed(range(layers)):
-        sides, small_grads = [None] * count, [None] * count
-        passed = []
+        one, two = 2 * layer, 2 * layer + 1
+        stages, passed = [None] * count, grad_parts[layer + 1] if layer + 1 < layers else None
         for batch in range(count):
-            held = gates[2 * batch : 2 * batch + 2]
-            held = [held[at : at + 1] for at in range(2)]
-            grad_hiddens[batch], sides[batch], small_grads[batch], held = layer_backward(
+            back, pairs = experts_backward(
+                grad_hiddens[batch], kept_all[layer][batch], weights[layer], moes[batch]
+            )
+            if passed and batch < 2:
+                back, passed[batch] = after(back, passed[batch])
+            stages[batch] = (back, pairs)
+        up_down = [
+            weight_grad([pairs[which] for _, pairs in stages], 0, 0) for which in range(2)
+        ]
+        grad_parts[layer] = [scatter_owners(item) for item in up_down]
+        outer, smalls = [], []
+        for batch in range(count):
+            grad_mixed_t, grad_mid, pair, small_two = mixed_backward(
                 grad_hiddens[batch],
+                stages[batch][0],
                 kept_all[layer][batch],
                 weights[layer],
-                gains_full[2 * layer],
-                gains_full[2 * layer + 1],
+                gains_full[two],
                 router_full[layer],
+                moes[batch],
+            )
+            if batch == count - 1:
+                grad_mixed_t, *up_down = after(grad_mixed_t, *up_down)
+                if passed:
+                    grad_mixed_t, passed[2] = after(grad_mixed_t, passed[2])
+                if layer == 0:
+                    grad_mixed_t, grad_parts[0][0] = after(grad_mixed_t, grad_parts[0][0])
+            grad_hiddens[batch], attend_pair, small_one, piece = attention_backward(
+                grad_mixed_t,
+                grad_mid,
+                kept_all[layer][batch],
+                weights[layer],
+                gains_full[one],
                 tiles[layer],
-                moes[batch],
                 used[batch],
-                held,
+                pieces[len(summed)],
             )
-            passed.extend(held[0] + held[1])
-        if passed:
-            grad_parts[layer + 1] = passed
-        gain_grads[2 * layer], gain_grads[2 * layer + 1], router_grads[layer], grad_relative = (
-            sum(items) for items in zip(*small_grads)
+            summed.append(piece)
+            outer.append((attend_pair, pair))
+            smalls.append(small_one + small_two)
+        gain_grads[one], grad_relative, gain_grads[two], router_grads[layer] = (
+            sum(items) for items in zip(*smalls)
         )
         table_grads[layer] = jnp.dot(onehot_buckets.T, grad_relative.T, precision=HIGHEST_PRECISION)
-        weight_grads = [
-            contract(
-                jnp.concatenate([item[0] for item in pairs], left_dim),
-                jnp.concatenate([item[1] for item in pairs], right_dim),
-                left_dim,
-                right_dim,
-            ).astype(BF16)
-            for pairs, left_dim, right_dim in zip(zip(*sides), (0, 0, 0, 1), (0, 0, 1, 0))
-        ]
-        grad_parts[layer] = [scatter_owners(item) for item in weight_grads[:2]]
-        dense_grad = jnp.concatenate(weight_grads[2:], 1)
-        if layer:
-            grad_parts[layer].append(scatter_owners(dense_grad))
-        gates = grad_parts[layer]
+        dense_grad = jnp.concatenate(
+            [weight_grad([item[0] for item in outer], 0, 1), weight_grad([item[1] for item in outer], 1, 0)],
+            1,
+        )
         if layer:
             grad_hiddens[0], dense_grad = after(grad_hiddens[0], dense_grad)
+            grad_parts[layer].append(scatter_owners(dense_grad))
 
     moved = []
     for batch in range(count):
-        if batch < 2:
-            grad_hiddens[batch], grad_parts[0][batch] = after(
-                grad_hiddens[batch], grad_parts[0][batch]
-            )
         columns = grad_hiddens[batch].reshape(rows, width).astype(BF16).T
-        columns = exchange(columns.reshape(ways, part, rows))
-        columns = lax.all_gather(columns, "fsdp", axis=0, tiled=False)
-        moved.append(columns.transpose(2, 0, 1, 3).reshape(part, -1))
+        moved.append(exchange(columns.reshape(ways, part, rows)))
+    moved[-1], grad_parts[0][1] = after(moved[-1], grad_parts[0][1])
+    stacks = [jnp.stack([parts[which] for parts in grad_parts]) for which in range(2)]
+    moved[-1], dense_grad, *stacks = after(moved[-1], dense_grad, *stacks)
     moved[0], dense_grad = after(moved[0], dense_grad)
+    moved = [lax.all_gather(item, "fsdp", axis=0, tiled=False) for item in moved]
     grad_parts[0].append(scatter_owners(dense_grad))
-    shared = [[None] * 3 for layer in range(layers)]
-    shared[-1] = [share(item) for item in grad_parts[-1][:2]]
-    moved[-1], *shared[-1] = after(moved[-1], *shared[-1])
-    every_id = lax.all_gather(group_ids, "seq", axis=0, tiled=False) - owner_index * vocab_rows
-    every_id = every_id.transpose(2, 1, 0, 3).reshape(count, -1)
-    embed_part = head_grad
-    for batch in range(count):
-        embed_part = embed_part + matmul(
-            moved[batch], (every_id[batch][:, None] == vocab_ids[None, :]).astype(BF16)
-        )
-    embed_part = embed_part.astype(BF16)
-    for layer in range(layers):
-        dense = grad_parts[layer][2]
-        dense = jnp.concatenate(
-            [
-                dense[:, : 3 * width].reshape(shard, ways, 3 * part),
-                dense[:, 3 * width :].reshape(shard, ways, part),
-            ],
-            2,
-        )
-        grad_parts[layer][2] = sum_over_seq(dense.transpose(1, 0, 2)).astype(BF16)
+    head_grad = jnp.concatenate([piece for piece in summed if piece is not None], 1)
+    wholes = [share(item) for item in stacks]
+    embed_part = token_grad(every_id, moved, head_grad)
+    dense = jnp.stack([parts[2] for parts in grad_parts])
+    dense = jnp.concatenate(
+        [
+            dense[:, :, : 3 * width].reshape(layers, shard, ways, 3 * part),
+            dense[:, :, 3 * width :].reshape(layers, shard, ways, part),
+        ],
+        3,
+    )
+    dense_part = sum_over_seq(dense.transpose(2, 0, 1, 3)).astype(BF16)
 
     tables = lax.dynamic_update_slice(
         jnp.zeros(bias_full.shape, F32), jnp.stack(table_grads), (0, 0, seq_index * head_local)
@@ -778,7 +877,7 @@
     loss_value, loss_count = tiny[-2], tiny[-1]
 
     squares_part = (
-        sum_squares(embed_part, *(item for parts in grad_parts for item in parts))
+        sum_squares(embed_part, dense_part, *stacks)
         + sum_squares(gains_grad, bias_grad, router_grad) / ways
     )
     grad_norm = jnp.sqrt(
@@ -786,28 +885,14 @@
     )
     clip_factor = jnp.minimum(1.0, CLIP_NORM / (grad_norm + 1e-06))
 
-    embed_grad = share(embed_part)
-    for layer in range(layers):
-        shared[layer] = [
-            share(item) if done is None else done for item, done in zip(grad_parts[layer], (shared[layer] + [None])[:3])
-        ]
-    upward_grad = jnp.stack([items[0] for items in shared])
-    downward_grad = jnp.stack([items[1] for items in shared])
-    dense_grads = [items[2] for items in shared]
-    attend_grad = jnp.stack(
-        [
-            item[:, :, : 3 * part]
-            .reshape(ways, shard, 3, part)
-            .transpose(1, 2, 0, 3)
-            .reshape(shard, 3 * width)
-            for item in dense_grads
-        ]
-    )
-    output_grad = jnp.stack(
-        [item[:, :, 3 * part :].transpose(1, 0, 2).reshape(shard, width) for item in dense_grads]
-    )
+    embed_grads = share(embed_part)
+    upward_grad, downward_grad = (by_source(items) for items in wholes)
+    dense_grad = by_source(share(dense_part)).transpose(0, 2, 1, 3)
+    attend_grad = dense_grad[..., : 3 * part].reshape(layers, shard, ways, 3, part)
+    attend_grad = attend_grad.transpose(0, 1, 3, 2, 4).reshape(layers, shard, 3 * width)
+    output_grad = dense_grad[..., 3 * part :].reshape(layers, shard, width)
     grads = (
-        embed_grad,
+        None,
         attend_grad,
         output_grad,
         upward_grad,
@@ -848,7 +933,7 @@
     )
     results = [loss_value, loss_count, grad_norm]
     results.extend(
-        embed_adam(embed_weight, embed_grad, embed_mean, embed_square, clip_factor, STEP_RATES[0])
+        embed_adam(embed_weight, embed_grads, embed_mean, embed_square, clip_factor, STEP_RATES[0])
     )
     for weight, grad, first, second, rate in list(
         zip(params, grads, means, squares, STEP_RATES)

time: 1520 us -> 1370 us (0.901)
  waiting for transfers between devices: 356 us -> 208 us
  matrix products: 370 us -> 308 us
  Pallas kernels: 202 us -> 252 us
    all_to_all x42 -> x33, waiting for transfers between devices: 228 us -> 72.3 us  [exchange(): return lax.all_to_all(parts, 'seq', split_axis=0, concat_axis=0, tiled=True)]
    ppermute x0 -> x27, waiting for transfers between devices: none -> 90.6 us  [to_relative(): lax.ppermute(part, 'seq', [(way, way ^ distance) for way in range(ways)])]
    dot_general x17 -> x16, matrix products: 159 us -> 107 us  [matmul(): return jnp.dot(left_side, right_side, preferred_element_type=F32)]
    pallas_call x0 -> x1, Pallas kernels: none -> 47.8 us  [token_grad(): pl.pallas_call(token_grad_kernel, grid=(pl.cdiv(vocab_rows, block), owner...]
    all_to_all x42 -> x33, starting transfers between devices: 174 us -> 131 us  [exchange(): return lax.all_to_all(parts, 'seq', split_axis=0, concat_axis=0, tiled=True)]
    ppermute x0 -> x27, starting transfers between devices: none -> 34.1 us  [to_relative(): lax.ppermute(part, 'seq', [(way, way ^ distance) for way in range(ways)])]
    reduce_scatter x2, waiting for transfers between devices: 26.4 us -> 0.02 us  [per_device(): lax.psum_scatter(found.reshape(owners, rows, width), 'fsdp', scatter_dime...]
    all_gather x6, waiting for transfers between devices: 37.1 us -> 12.7 us  [gather_owners(): return lax.all_gather(item, 'fsdp', axis=0, tiled=True)]
  transfers between devices with their start and end apart: 60 -> 79, of which waited for: 29 -> 24; matrix products, arithmetic and copies ran while one was open for 35% -> 36% of each run, Pallas kernels for 13% -> 19%
where the time goes in v2:
time: 1370 us; the launch traced here: 1350 us
  matrix products  308 us (22%)
  Pallas kernels  252 us (18%)
  waiting for transfers between devices  208 us (15%)
  starting transfers between devices  180 us (13%)
  local copies, waits for them, and re-layouts  146 us (11%)
  other arithmetic  142 us (10%)
  blocking collectives  93 us (7%)
  between operations  24.6 us (2%)
    dot_general x37, matrix products, contract(): lax.dot_general(left_side, right_side, (((left_dim,), (right_dim,)), ((),...  146 us
    all_to_all x33, starting transfers between devices, exchange(): return lax.all_to_all(parts, 'seq', split_axis=0, concat_axis=0, tiled=True)  131 us
    dot_general x16, matrix products, matmul(): return jnp.dot(left_side, right_side, preferred_element_type=F32)  107 us
    ppermute x27, waiting for transfers between devices, to_relative(): lax.ppermute(part, 'seq', [(way, way ^ distance) for way in range(ways)])  90.6 us
    pallas_call x4, Pallas kernels, attend_back(): pl.pallas_call(attend_back_kernel, grid=(count,), in_specs=[pl.BlockSpec(...  89.6 us
    all_to_all x33, waiting for transfers between devices, exchange(): return lax.all_to_all(parts, 'seq', split_axis=0, concat_axis=0, tiled=True)  72.3 us
    pallas_call x4, Pallas kernels, attend(): pl.pallas_call(attend_kernel, grid=(count,), in_specs=[pl.BlockSpec(memor...  59.1 us
    sub x7, other arithmetic, adam_update(): weight - rate * (mean_hat / (jnp.sqrt(square_hat) + ADAM_EPSILON) + WEIGH...  56.5 us
  transfers between devices with their start and end apart: 79, of which 24 were waited for; matrix products, arithmetic and copies ran while one was open for 36% of the time, Pallas kernels for 19%

profile of v2, /device:TPU:0, one launch (start us, length us, event | category | flops | bytes accessed | tf_op | source)
XLA Modules:
  0.0 1353.1 jit_solution(6629690074559588494)
XLA Ops:
  13.9 7.8 convert_element_type.439
  21.7 14.7 %all-gather.9 = s32[8,2,256]{2,1,0:T(2,128)S(1)} all-gather(s32[1,2,256]{2,1,0:T(2,128)S(1)} %bitcast.738), channel_id=2, replica_groups=mesh['seq'=4,'fsdp'=8] {'fsdp'}, dimensions={0}, use_global_device_ids=true | all-gather | bytes 18432 | tf_op jit(solution)/shard_map/all_gather | solution.py:621
  37.0 18.5 %fusion.85 = bf16[2048,768]{1,0:T(8,128)(2,1)} fusion(bf16[4016,768]{1,0:T(8,128)(2,1)} %convert_element_type.439, s32[2048]{0:T(1024)S(1)} %bitcast.741), kind=kOutput, calls=%fused_computation.122 | convolution fusion | flops 12643041280 | bytes 9322496 | tf_op jit(solution)/shard_map/dot_general | solution.py:28
  57.3 16.8 %all_gather.56 = f32[8,80,128]{2,1,0:T(8,128)} all-gather(f32[1,80,128]{2,1,0:T(8,128)S(1)} %pad_bitcast_fusion.1), channel_id=1, replica_groups=mesh['seq'=4,'fsdp'=8] {'fsdp'}, dimensions={0}, use_global_device_ids=true | all-gather | bytes 368640 | tf_op jit(solution)/shard_map/all_gather | solution.py:631
  74.1 18.4 %fusion.84 = bf16[2048,768]{1,0:T(8,128)(2,1)} fusion(bf16[4016,768]{1,0:T(8,128)(2,1)} %convert_element_type.439, s32[2048]{0:T(1024)S(1)} %bitcast.740), kind=kOutput, calls=%fused_computation.121 | convolution fusion | flops 12643041280 | bytes 9322496 | tf_op jit(solution)/shard_map/dot_general | solution.py:28
  111.6 17.2 %fusion.2 = f32[512,32,128]{2,1,0:T(8,128)} fusion(s32[512,65]{1,0:T(8,128)S(1)} %get-tuple-element.393, f32[512,65]{1,0:T(8,128)S(1)} %concatenate.100, s32[512,65]{1,0:T(8,128)S(1)} %get-tuple-element.392), kind=kOutput, calls=%fused_computation.5 | convolution fusion | flops 1642168320 | bytes 8787968 | tf_op jit(solution)/shard_map/rkh,rkl->rhl/dot_general | solution.py:704
  128.8 10.0 copy.412
  138.8 7.7 slice.329
  167.2 18.9 %all-gather.5 = s32[32,2,256]{2,1,0:T(2,128)S(1)} all-gather(s32[8,2,256]{2,1,0:T(2,128)S(1)} %copy-done.107), channel_id=7, replica_groups=mesh['seq'=4,'fsdp'=8] {'seq'}, dimensions={0}, use_global_device_ids=true | all-gather | bytes 81920 | tf_op jit(solution)/shard_map/all_gather | solution.py:726
  186.9 14.7 %attend.4 = (bf16[4,1,192,256]{3,2,1,0:T(8,128)(2,1)}, f32[1,12,256]{2,1,0:T(8,128)S(1)}) custom-call(s32[1]{0:T(128)} %bitcast.length_ref, bf16[4,1,576,256]{3,2,1,0:T(8,128)(2,1)S(1)} %all-to-all-done.qkv_ref, f32[3,1792,256]{2,1,0:T(8,128)} %copy-done.6), custom_call_target="tpu_custom_call" | custom-call | flops 16106127360 | bytes 6684672 | tf_op jit(solution)/shard_map/attend/pallas_call | solution.py:116
  221.9 8.7 all-to-all-done.8.qkv_ref
  230.6 14.6 %attend.6 = (bf16[4,1,192,256]{3,2,1,0:T(8,128)(2,1)}, f32[1,12,256]{2,1,0:T(8,128)S(1)}) custom-call(s32[1]{0:T(128)} %bitcast.49.length_ref, bf16[4,1,576,256]{3,2,1,0:T(8,128)(2,1)S(1)} %all-to-all-done.8.qkv_ref, f32[3,1792,256]{2,1,0:T(8,128)} %copy-done.6), custom_call_target="tpu_custom_call" | custom-call | flops 16106127360 | bytes 6684672 | tf_op jit(solution)/shard_map/attend/pallas_call | solution.py:116
  269.3 8.2 multiply_convert_fusion.5
  288.0 7.4 multiply_convert_fusion.3
  341.0 14.7 %attend.5 = (bf16[4,1,192,256]{3,2,1,0:T(8,128)(2,1)}, f32[1,12,256]{2,1,0:T(8,128)S(1)}) custom-call(s32[1]{0:T(128)} %bitcast.length_ref, bf16[4,1,576,256]{3,2,1,0:T(8,128)(2,1)S(1)} %all-to-all-done.4.qkv_ref, f32[3,1792,256]{2,1,0:T(8,128)} %copy-done.7), custom_call_target="tpu_custom_call" | custom-call | flops 16106127360 | bytes 6684672 | tf_op jit(solution)/shard_map/attend/pallas_call | solution.py:116
  360.0 15.0 %attend.7 = (bf16[4,1,192,256]{3,2,1,0:T(8,128)(2,1)}, f32[1,12,256]{2,1,0:T(8,128)S(1)}) custom-call(s32[1]{0:T(128)} %bitcast.49.length_ref, bf16[4,1,576,256]{3,2,1,0:T(8,128)(2,1)} %all-to-all-done.12.qkv_ref, f32[3,1792,256]{2,1,0:T(8,128)} %copy-done.7), custom_call_target="tpu_custom_call" | custom-call | flops 16106127360 | bytes 6684672 | tf_op jit(solution)/shard_map/attend/pallas_call | solution.py:116
  400.7 8.4 multiply_convert_fusion.4
  409.1 8.9 all-gather.30.cloned.1.call-done
  428.2 7.4 multiply_convert_fusion.2
  449.1 6.9 all-to-all-done.15
  460.6 15.8 %all_gather.65 = bf16[512,768]{1,0:T(8,128)(2,1)S(1)} all-gather(bf16[64,768]{1,0:T(8,128)(2,1)S(1)} %bitcast.715), channel_id=1, replica_groups=mesh['seq'=4,'fsdp'=8] {'fsdp'}, dimensions={0}, use_global_device_ids=true | all-gather | bytes 884736 | tf_op jit(solution)/shard_map/all_gather | solution.py:734
  487.5 14.3 %all-gather.10 = f32[8,2,512]{2,1,0:T(2,128)S(1)} all-gather(f32[1,2,512]{2,1,0:T(2,128)S(1)} %maximum_bitcast_fusion.1), channel_id=8, replica_groups=mesh['seq'=4,'fsdp'=8] {'fsdp'}, dimensions={0}, use_global_device_ids=true | all-gather | bytes 36864 | tf_op jit(solution)/shard_map/all_gather | solution.py:740
  501.9 6.8 multiply_convert_fusion.1
  510.7 6.8 fusion.305
  517.6 31.4 %reduce-scatter.14.cloned.1.call-done = f32[64,768]{1,0:T(8,128)} async-done(((f32[512,768]{1,0:T(8,128)}), f32[64,768]{1,0:T(8,128)}) %reduce-scatter.14.cloned.1.call-update) | async-done | bytes 196624 | tf_op jit(solution)/shard_map/reduce_scatter | solution.py:751
  569.5 9.5 fusion.36
  579.0 8.2 fusion.22
  595.4 8.4 multiply_convert_fusion
  603.8 8.6 copy.374
  646.1 8.8 convolution_convert_fusion.4
  659.9 22.7 %attend_back.5 = (bf16[4,1,576,256]{3,2,1,0:T(8,128)(2,1)}, f32[3,1,2048]{2,1,0:T(1,128)S(1)}) custom-call(s32[1]{0:T(128)} %bitcast.49.length_ref, bf16[4,1,576,256]{3,2,1,0:T(8,128)(2,1)} %all-to-all-done.12.qkv_ref, bf16[4,1,192,256]{3,2,1,0:T(8,128)(2,1)S(1)} %all-to-all-done.22.out_grad_ref, f32[1,12,256]{2,1,0:T(8,128)S(1)} %get-tuple-element.137.lse_ref, ...), custom_call_target="tpu_custom_call" | custom-call | flops 25165824000 | bytes 7864320 | tf_op jit(solution)/shard_map/attend_back/pallas_call | solution.py:206
  717.5 12.5 all_to_all.180.out_grad_ref
  733.7 22.2 %attend_back.4 = (bf16[4,1,576,256]{3,2,1,0:T(8,128)(2,1)}, f32[3,1,2048]{2,1,0:T(1,128)S(1)}) custom-call(s32[1]{0:T(128)} %bitcast.length_ref, bf16[4,1,576,256]{3,2,1,0:T(8,128)(2,1)S(1)} %all-to-all-done.4.qkv_ref, bf16[4,1,192,256]{3,2,1,0:T(8,128)(2,1)S(1)} %all_to_all.180.out_grad_ref, f32[1,12,256]{2,1,0:T(8,128)S(1)} %get-tuple-element.129.lse_ref, ...), custom_call_target="tpu_custom_call" | custom-call | flops 25165824000 | bytes 7864320 | tf_op jit(solution)/shard_map/attend_back/pallas_call | solution.py:206
  764.7 6.8 all-to-all-done.19
  798.5 8.9 fusion.29
  807.4 8.2 fusion.15
  844.0 9.2 convolution_convert_fusion.1
  893.6 22.3 %attend_back.6 = (bf16[4,1,576,256]{3,2,1,0:T(8,128)(2,1)}, f32[3,1,2048]{2,1,0:T(1,128)S(1)}) custom-call(s32[1]{0:T(128)} %bitcast.length_ref, bf16[4,1,576,256]{3,2,1,0:T(8,128)(2,1)S(1)} %copy-done.11, bf16[4,1,192,256]{3,2,1,0:T(8,128)(2,1)S(1)} %all-to-all-done.26.out_grad_ref, f32[1,12,256]{2,1,0:T(8,128)S(1)} %get-tuple-element.144.lse_ref, ...), custom_call_target="tpu_custom_call" | custom-call | flops 25165824000 | bytes 7864320 | tf_op jit(solution)/shard_map/attend_back/pallas_call | solution.py:206
  928.0 22.3 %attend_back.7 = (bf16[4,1,576,256]{3,2,1,0:T(8,128)(2,1)}, f32[3,1,2048]{2,1,0:T(1,128)S(1)}) custom-call(s32[1]{0:T(128)} %bitcast.49.length_ref, bf16[4,1,576,256]{3,2,1,0:T(8,128)(2,1)S(1)} %copy-done.9, bf16[4,1,192,256]{3,2,1,0:T(8,128)(2,1)S(1)} %all-to-all-done.30.out_grad_ref, f32[1,12,256]{2,1,0:T(8,128)S(1)} %get-tuple-element.156.lse_ref, ...), custom_call_target="tpu_custom_call" | custom-call | flops 25165824000 | bytes 7864320 | tf_op jit(solution)/shard_map/attend_back/pallas_call | solution.py:206
  1012.8 7.4 all-to-all-start.32
  1041.4 10.4 collective-permute-done.21
  1056.2 46.2 %collective-permute-done.24 = bf16[2,384,768]{2,1,0:T(8,128)(2,1)} collective-permute-done((bf16[2,384,768]{2,1,0:T(8,128)(2,1)S(1)}, bf16[2,384,768]{2,1,0:T(8,128)(2,1)}, u32[]{:S(2)}, u32[]{:S(2)}) %collective-permute-start.24) | collective-permute-done | bytes 1179680 | tf_op jit(solution)/shard_map/ppermute | solution.py:369
  1104.7 25.4 %collective-permute-done.25 = bf16[2,384,768]{2,1,0:T(8,128)(2,1)} collective-permute-done((bf16[2,384,768]{2,1,0:T(8,128)(2,1)S(1)}, bf16[2,384,768]{2,1,0:T(8,128)(2,1)}, u32[]{:S(2)}, u32[]{:S(2)}) %collective-permute-start.25) | collective-permute-done | bytes 1179680 | tf_op jit(solution)/shard_map/ppermute | solution.py:369
  1151.1 47.8 %token_grad.1.refs_0_ = bf16[192,4016]{1,0:T(8,128)(2,1)S(1)} custom-call(s32[8,2,1024]{2,1,0:T(2,128)S(1)} %reshape.1118.ids_ref, bf16[8,4,192,256]{3,2,1,0:T(8,128)(2,1)S(1)} %bitcast.651, bf16[8,4,192,256]{3,2,1,0:T(8,128)(2,1)} %bitcast.745, f32[192,4016]{1,0:T(8,128)} %pad_maximum_fusion.2.refs_2_), custom_call_target="tpu_custom_call" | custom-call | flops 50532974592 | bytes 25165824 | tf_op jit(solution)/shard_map/token_grad/pallas_call | solution.py:344
  1226.8 23.9 %multiply_subtract_fusion = (f32[2,4,384,768]{3,2,1,0:T(8,128)}, f32[2,4,384,768]{3,2,1,0:T(8,128)}, f32[2,4,384,768]{3,2,1,0:T(8,128)}) fusion(f32[2,4,384,768]{3,2,1,0:T(8,128)} %param.52, f32[]{:T(128)} %min.3, bf16[2,4,384,768]{3,2,1,0:T(8,128)(2,1)} %bitcast_dynamic-update-slice_fusion, f32[2,4,384,768]{3,2,1,0:T(8,128)} %param.53, ...), kind=kLoop, calls=%fused_computation.13 | loop fusion | flops 40108032 | bytes 61341700 | tf_op jit(solution)/shard_map/sub | solution.py:544
  1250.7 23.9 %multiply_subtract_fusion.1 = (f32[2,4,96,3072]{3,2,1,0:T(8,128)}, f32[2,4,96,3072]{3,2,1,0:T(8,128)}, f32[2,4,96,3072]{3,2,1,0:T(8,128)}) fusion(f32[2,4,96,3072]{3,2,1,0:T(8,128)} %param.49, f32[]{:T(128)} %min.3, bf16[2,4,96,3072]{3,2,1,0:T(8,128)(2,1)} %bitcast_dynamic-update-slice_fusion.4, f32[2,4,96,3072]{3,2,1,0:T(8,128)} %param.50, ...), kind=kLoop, calls=%fused_computation.16 | loop fusion | flops 40108032 | bytes 61341700 | tf_op jit(solution)/shard_map/sub | solution.py:544
  1278.1 8.6 collective-permute-done.16.refs_2_
  1286.6 34.0 %embed_adam.1 = (f32[4016,768]{1,0:T(8,128)}, f32[4016,768]{1,0:T(8,128)}, f32[4016,768]{1,0:T(8,128)}) custom-call(f32[1]{0:T(128)} %bitcast.183.clip_ref, s32[1]{0:T(128)} %bitcast.184.seq_ref, f32[4016,768]{1,0:T(8,128)} %weight_ref.1, f32[4016,768]{1,0:T(8,128)} %first_ref.1, f32[4016,768]{1,0:T(8,128)} %second_ref.1, ...), custom_call_target="tpu_custom_call" | custom-call | flops 61685760 | bytes 80191488 | tf_op jit(solution)/shard_map/embed_adam/pallas_call | solution.py:303
  (871 shorter events, 602.1 us)
Async XLA Ops:
  7.2 85.3 %all-gather.20.cloned.1.call-start = ((), (), s32[]{:S(2)}) async-start(), calls=%async_computation.46 | async-start | bytes 5308416 | tf_op jit(solution)/shard_map/all_gather | solution.py:612
  13.9 143.1 %reduce-scatter.10.cloned.1.call-start = ((), (), s32[]{:S(2)}) async-start(), calls=%async_computation.45 | async-start | bytes 3538944 | tf_op jit(solution)/shard_map/reduce_scatter | solution.py:647
  55.5 149.6 %reduce-scatter.12.cloned.1.call-start = ((), (), s32[]{:S(2)}) async-start(), calls=%async_computation.48 | async-start | bytes 3538944 | tf_op jit(solution)/shard_map/reduce_scatter | solution.py:647
  92.5 176.8 %all-gather.24.cloned.1.call-start = ((), (), s32[]{:S(2)}) async-start(), calls=%async_computation.56 | async-start | bytes 5308416 | tf_op jit(solution)/shard_map/all_gather | solution.py:612
  98.0 179.6 %all-gather.26.cloned.1.call-start = ((), (), s32[]{:S(2)}) async-start(), calls=%async_computation.57 | async-start | bytes 5308416 | tf_op jit(solution)/shard_map/all_gather | solution.py:612
  104.7 207.9 %all-gather.22.cloned.1.call-start = ((), (), s32[]{:S(2)}) async-start(), calls=%async_computation.47 | async-start | bytes 5308416 | tf_op jit(solution)/shard_map/all_gather | solution.py:612
  108.2 292.5 %all-gather.28.cloned.1.call-start = ((), (), s32[]{:S(2)}) async-start(), calls=%async_computation.58 | async-start | bytes 5308416 | tf_op jit(solution)/shard_map/all_gather | solution.py:612
  163.4 23.5 %all-to-all-start = ((bf16[4,1,576,256]{3,2,1,0:T(8,128)(2,1)}), bf16[4,1,576,256]{3,2,1,0:T(8,128)(2,1)S(1)}, u32[]{:S(2)}, u32[]{:S(2)}) async-start(bf16[4,1,576,256]{3,2,1,0:T(8,128)(2,1)} %get-tuple-element.112), calls=%async_computation.1 | async-start | bytes 2359296 | tf_op jit(solution)/shard_map/all_to_all | solution.py:364
  216.7 201.3 %all-gather.30.cloned.1.call-start = ((), (), s32[]{:S(2)}) async-start(), calls=%async_computation.59 | async-start | bytes 5308416 | tf_op jit(solution)/shard_map/all_gather | solution.py:612
  397.1 26.7 %all-to-all-start.14 = ((bf16[4,1,96,768]{3,2,1,0:T(8,128)(2,1)}), bf16[4,1,96,768]{3,2,1,0:T(8,128)(2,1)S(1)}, u32[]{:S(2)}, u32[]{:S(2)}) async-start(bf16[4,1,96,768]{3,2,1,0:T(8,128)(2,1)} %bitcast.69), calls=%async_computation.16 | async-start | bytes 1179648 | tf_op jit(solution)/shard_map/all_to_all | solution.py:364
  446.5 102.5 %reduce-scatter.14.cloned.1.call-start = ((), (), s32[]{:S(2)}) async-start(), calls=%async_computation.49 | async-start | bytes 1769472 | tf_op jit(solution)/shard_map/reduce_scatter | solution.py:751
  569.0 288.5 %reduce-scatter.16.cloned.1.call-start = ((), (), s32[]{:S(2)}) async-start(), calls=%async_computation.50 | async-start | bytes 5308416 | tf_op jit(solution)/shard_map/reduce_scatter | solution.py:551
  645.9 220.8 %reduce-scatter.18.cloned.1.call-start = ((), (), s32[]{:S(2)}) async-start(), calls=%async_computation.51 | async-start | bytes 5308416 | tf_op jit(solution)/shard_map/reduce_scatter | solution.py:551
  656.3 26.3 %collective-permute-start.5 = (bf16[192,1024]{1,0:T(8,128)(2,1)S(1)}, bf16[192,1024]{1,0:T(8,128)(2,1)S(1)}, u32[]{:S(2)}, u32[]{:S(2)}) collective-permute-start(bf16[192,1024]{1,0:T(8,128)(2,1)S(1)} %get-tuple-element.384), channel_id=1, source_target_pairs={{0,24},{8,16},{16,8},{24,0},{1,25},{9,17},{17,9},{25,1},{2,26},{10... | collective-permute-start | bytes 1179656 | tf_op jit(solution)/shard_map/ppermute | solution.py:369
  659.2 23.3 %collective-permute-start.4 = (bf16[192,1024]{1,0:T(8,128)(2,1)S(1)}, bf16[192,1024]{1,0:T(8,128)(2,1)S(1)}, u32[]{:S(2)}, u32[]{:S(2)}) collective-permute-start(bf16[192,1024]{1,0:T(8,128)(2,1)S(1)} %get-tuple-element.385), channel_id=1, source_target_pairs={{0,16},{8,24},{16,0},{24,8},{1,17},{9,25},{17,1},{25,9},{2,18},{10... | collective-permute-start | bytes 1179656 | tf_op jit(solution)/shard_map/ppermute | solution.py:369
  659.8 22.8 %collective-permute-start.3 = (bf16[192,1024]{1,0:T(8,128)(2,1)S(1)}, bf16[192,1024]{1,0:T(8,128)(2,1)S(1)}, u32[]{:S(2)}, u32[]{:S(2)}) collective-permute-start(bf16[192,1024]{1,0:T(8,128)(2,1)S(1)} %get-tuple-element.383), channel_id=1, source_target_pairs={{0,8},{8,0},{16,24},{24,16},{1,9},{9,1},{17,25},{25,17},{2,10},{10... | collective-permute-start | bytes 1179656 | tf_op jit(solution)/shard_map/ppermute | solution.py:369
  730.1 25.8 %collective-permute-start.2 = (bf16[192,1024]{1,0:T(8,128)(2,1)S(1)}, bf16[192,1024]{1,0:T(8,128)(2,1)S(1)}, u32[]{:S(2)}, u32[]{:S(2)}) collective-permute-start(bf16[192,1024]{1,0:T(8,128)(2,1)S(1)} %get-tuple-element.381), channel_id=1, source_target_pairs={{0,24},{8,16},{16,8},{24,0},{1,25},{9,17},{17,9},{25,1},{2,26},{10... | collective-permute-start | bytes 1179656 | tf_op jit(solution)/shard_map/ppermute | solution.py:369
  731.2 24.7 %collective-permute-start.1 = (bf16[192,1024]{1,0:T(8,128)(2,1)S(1)}, bf16[192,1024]{1,0:T(8,128)(2,1)S(1)}, u32[]{:S(2)}, u32[]{:S(2)}) collective-permute-start(bf16[192,1024]{1,0:T(8,128)(2,1)S(1)} %get-tuple-element.382), channel_id=1, source_target_pairs={{0,16},{8,24},{16,0},{24,8},{1,17},{9,25},{17,1},{25,9},{2,18},{10... | collective-permute-start | bytes 1179656 | tf_op jit(solution)/shard_map/ppermute | solution.py:369
  732.5 23.4 %collective-permute-start = (bf16[192,1024]{1,0:T(8,128)(2,1)S(1)}, bf16[192,1024]{1,0:T(8,128)(2,1)S(1)}, u32[]{:S(2)}, u32[]{:S(2)}) collective-permute-start(bf16[192,1024]{1,0:T(8,128)(2,1)S(1)} %get-tuple-element.380), channel_id=1, source_target_pairs={{0,8},{8,0},{16,24},{24,16},{1,9},{9,1},{17,25},{25,17},{2,10},{10... | collective-permute-start | bytes 1179656 | tf_op jit(solution)/shard_map/ppermute | solution.py:369
  761.3 161.6 %reduce-scatter.20.cloned.1.call-start = ((), (), s32[]{:S(2)}) async-start(), calls=%async_computation.52 | async-start | bytes 5308416 | tf_op jit(solution)/shard_map/reduce_scatter | solution.py:551
  798.4 124.6 %reduce-scatter.22.cloned.1.call-start = ((), (), s32[]{:S(2)}) async-start(), calls=%async_computation.53 | async-start | bytes 5308416 | tf_op jit(solution)/shard_map/reduce_scatter | solution.py:551
  843.5 154.3 %reduce-scatter.24.cloned.1.call-start = ((), (), s32[]{:S(2)}) async-start(), calls=%async_computation.54 | async-start | bytes 5308416 | tf_op jit(solution)/shard_map/reduce_scatter | solution.py:551
  884.3 31.7 %all-to-all-start.30 = ((bf16[4,1,192,256]{3,2,1,0:T(8,128)(2,1)}), bf16[4,1,192,256]{3,2,1,0:T(8,128)(2,1)S(1)}, u32[]{:S(2)}, u32[]{:S(2)}) async-start(bf16[4,1,192,256]{3,2,1,0:T(8,128)(2,1)} %bitcast.141), calls=%async_computation.35 | async-start | bytes 786432 | tf_op jit(solution)/shard_map/all_to_all | solution.py:364
  890.1 25.8 %collective-permute-start.8 = (bf16[192,1024]{1,0:T(8,128)(2,1)}, bf16[192,1024]{1,0:T(8,128)(2,1)S(1)}, u32[]{:S(2)}, u32[]{:S(2)}) collective-permute-start(bf16[192,1024]{1,0:T(8,128)(2,1)} %get-tuple-element.375), channel_id=1, source_target_pairs={{0,24},{8,16},{16,8},{24,0},{1,25},{9,17},{17,9},{25,1},{2,26},{10... | collective-permute-start | bytes 1179656 | tf_op jit(solution)/shard_map/ppermute | solution.py:369
  893.0 22.9 %collective-permute-start.7 = (bf16[192,1024]{1,0:T(8,128)(2,1)}, bf16[192,1024]{1,0:T(8,128)(2,1)}, u32[]{:S(2)}, u32[]{:S(2)}) collective-permute-start(bf16[192,1024]{1,0:T(8,128)(2,1)} %get-tuple-element.376), channel_id=1, source_target_pairs={{0,16},{8,24},{16,0},{24,8},{1,17},{9,25},{17,1},{25,9},{2,18},{10... | collective-permute-start | bytes 1179656 | tf_op jit(solution)/shard_map/ppermute | solution.py:369
  918.4 34.1 %all-to-all-start.27 = ((bf16[4,1,576,256]{3,2,1,0:T(8,128)(2,1)}), bf16[4,1,576,256]{3,2,1,0:T(8,128)(2,1)}, u32[]{:S(2)}, u32[]{:S(2)}) async-start(bf16[4,1,576,256]{3,2,1,0:T(8,128)(2,1)} %get-tuple-element.147), calls=%async_computation.31 | async-start | bytes 2359296 | tf_op jit(solution)/shard_map/all_to_all | solution.py:364
  924.3 26.0 %collective-permute-start.11 = (bf16[192,944]{1,0:T(8,128)(2,1)S(1)}, bf16[192,944]{1,0:T(8,128)(2,1)S(1)}, u32[]{:S(2)}, u32[]{:S(2)}) collective-permute-start(bf16[192,944]{1,0:T(8,128)(2,1)S(1)} %get-tuple-element.378), channel_id=1, source_target_pairs={{0,24},{8,16},{16,8},{24,0},{1,25},{9,17},{17,9},{25,1},{2,26},{10... | collective-permute-start | bytes 1087496 | tf_op jit(solution)/shard_map/ppermute | solution.py:369
  927.3 23.0 %collective-permute-start.10 = (bf16[192,944]{1,0:T(8,128)(2,1)S(1)}, bf16[192,944]{1,0:T(8,128)(2,1)S(1)}, u32[]{:S(2)}, u32[]{:S(2)}) collective-permute-start(bf16[192,944]{1,0:T(8,128)(2,1)S(1)} %get-tuple-element.379), channel_id=1, source_target_pairs={{0,16},{8,24},{16,0},{24,8},{1,17},{9,25},{17,1},{25,9},{2,18},{10... | collective-permute-start | bytes 1087496 | tf_op jit(solution)/shard_map/ppermute | solution.py:369
  927.8 22.5 %collective-permute-start.9 = (bf16[192,944]{1,0:T(8,128)(2,1)S(1)}, bf16[192,944]{1,0:T(8,128)(2,1)S(1)}, u32[]{:S(2)}, u32[]{:S(2)}) collective-permute-start(bf16[192,944]{1,0:T(8,128)(2,1)S(1)} %get-tuple-element.377), channel_id=1, source_target_pairs={{0,8},{8,0},{16,24},{24,16},{1,9},{9,1},{17,25},{25,17},{2,10},{10... | collective-permute-start | bytes 1087496 | tf_op jit(solution)/shard_map/ppermute | solution.py:369
  992.7 144.6 %reduce-scatter.26.cloned.1.call-start = ((), (), s32[]{:S(2)}) async-start(), calls=%async_computation.55 | async-start | bytes 5308416 | tf_op jit(solution)/shard_map/reduce_scatter | solution.py:551
  999.3 149.8 %all-gather.32.cloned.1.call-start = ((), (), s32[]{:S(2)}) async-start(), calls=%async_computation.60 | async-start | bytes 3538944 | tf_op jit(solution)/shard_map/all_gather | solution.py:841
  999.9 149.3 %all-gather.34.cloned.1.call-start = ((), (), s32[]{:S(2)}) async-start(), calls=%async_computation.61 | async-start | bytes 3538944 | tf_op jit(solution)/shard_map/all_gather | solution.py:841
  1012.8 24.1 %all-to-all-start.32 = ((f32[32,16,128]{2,1,0:T(8,128)}), f32[32,16,128]{2,1,0:T(8,128)S(1)}, u32[]{:S(2)}, u32[]{:S(2)}) async-start(f32[32,16,128]{2,1,0:T(8,128)} %bitcast.265), calls=%async_computation.39 | async-start | bytes 524288 | tf_op jit(solution)/shard_map/all_to_all | solution.py:404
  1020.3 31.5 %collective-permute-start.21 = (bf16[2,96,3072]{2,1,0:T(8,128)(2,1)S(1)}, bf16[2,96,3072]{2,1,0:T(8,128)(2,1)}, u32[]{:S(2)}, u32[]{:S(2)}) collective-permute-start(bf16[2,96,3072]{2,1,0:T(8,128)(2,1)S(1)} %copy-done.37), channel_id=1, source_target_pairs={{0,8},{8,0},{16,24},{24,16},{1,9},{9,1},{17,25},{25,17},{2,10},{10... | collective-permute-start | bytes 3538952 | tf_op jit(solution)/shard_map/ppermute | solution.py:369
  1022.1 110.5 %collective-permute-start.22 = (bf16[2,96,3072]{2,1,0:T(8,128)(2,1)S(1)}, bf16[2,96,3072]{2,1,0:T(8,128)(2,1)}, u32[]{:S(2)}, u32[]{:S(2)}) collective-permute-start(bf16[2,96,3072]{2,1,0:T(8,128)(2,1)S(1)} %copy-done.37), channel_id=1, source_target_pairs={{0,16},{8,24},{16,0},{24,8},{1,17},{9,25},{17,1},{25,9},{2,18},{10... | collective-permute-start | bytes 3538952 | tf_op jit(solution)/shard_map/ppermute | solution.py:369
  1023.6 111.4 %collective-permute-start.23 = (bf16[2,96,3072]{2,1,0:T(8,128)(2,1)S(1)}, bf16[2,96,3072]{2,1,0:T(8,128)(2,1)}, u32[]{:S(2)}, u32[]{:S(2)}) collective-permute-start(bf16[2,96,3072]{2,1,0:T(8,128)(2,1)S(1)} %copy-done.37), channel_id=1, source_target_pairs={{0,24},{8,16},{16,8},{24,0},{1,25},{9,17},{17,9},{25,1},{2,26},{10... | collective-permute-start | bytes 3538952 | tf_op jit(solution)/shard_map/ppermute | solution.py:369
  1023.8 78.6 %collective-permute-start.24 = (bf16[2,384,768]{2,1,0:T(8,128)(2,1)S(1)}, bf16[2,384,768]{2,1,0:T(8,128)(2,1)}, u32[]{:S(2)}, u32[]{:S(2)}) collective-permute-start(bf16[2,384,768]{2,1,0:T(8,128)(2,1)S(1)} %pad_maximum_fusion.5), channel_id=1, source_target_pairs={{0,8},{8,0},{16,24},{24,16},{1,9},{9,1},{17,25},{25,17},{2,10},{10... | collective-permute-start | bytes 3538952 | tf_op jit(solution)/shard_map/ppermute | solution.py:369
  1025.6 104.6 %collective-permute-start.25 = (bf16[2,384,768]{2,1,0:T(8,128)(2,1)S(1)}, bf16[2,384,768]{2,1,0:T(8,128)(2,1)}, u32[]{:S(2)}, u32[]{:S(2)}) collective-permute-start(bf16[2,384,768]{2,1,0:T(8,128)(2,1)S(1)} %pad_maximum_fusion.5), channel_id=1, source_target_pairs={{0,16},{8,24},{16,0},{24,8},{1,17},{9,25},{17,1},{25,9},{2,18},{10... | collective-permute-start | bytes 3538952 | tf_op jit(solution)/shard_map/ppermute | solution.py:369
  1051.8 159.4 %collective-permute-start.26 = (bf16[2,384,768]{2,1,0:T(8,128)(2,1)S(1)}, bf16[2,384,768]{2,1,0:T(8,128)(2,1)}, u32[]{:S(2)}, u32[]{:S(2)}) collective-permute-start(bf16[2,384,768]{2,1,0:T(8,128)(2,1)S(1)} %pad_maximum_fusion.5), channel_id=1, source_target_pairs={{0,24},{8,16},{16,8},{24,0},{1,25},{9,17},{17,9},{25,1},{2,26},{10... | collective-permute-start | bytes 3538952 | tf_op jit(solution)/shard_map/ppermute | solution.py:369
  1145.2 55.1 %collective-permute-start.14 = (bf16[2,96,768]{2,1,0:T(8,128)(2,1)}, bf16[2,96,768]{2,1,0:T(8,128)(2,1)}, u32[]{:S(2)}, u32[]{:S(2)}) collective-permute-start(bf16[2,96,768]{2,1,0:T(8,128)(2,1)} %get-tuple-element.389), channel_id=1, source_target_pairs={{0,24},{8,16},{16,8},{24,0},{1,25},{9,17},{17,9},{25,1},{2,26},{10... | collective-permute-start | bytes 884744 | tf_op jit(solution)/shard_map/ppermute | solution.py:369
  1147.6 52.7 %collective-permute-start.13 = (bf16[2,96,768]{2,1,0:T(8,128)(2,1)}, bf16[2,96,768]{2,1,0:T(8,128)(2,1)}, u32[]{:S(2)}, u32[]{:S(2)}) collective-permute-start(bf16[2,96,768]{2,1,0:T(8,128)(2,1)} %get-tuple-element.388), channel_id=1, source_target_pairs={{0,16},{8,24},{16,0},{24,8},{1,17},{9,25},{17,1},{25,9},{2,18},{10... | collective-permute-start | bytes 884744 | tf_op jit(solution)/shard_map/ppermute | solution.py:369
  1147.7 52.5 %collective-permute-start.12 = (bf16[2,96,768]{2,1,0:T(8,128)(2,1)}, bf16[2,96,768]{2,1,0:T(8,128)(2,1)}, u32[]{:S(2)}, u32[]{:S(2)}) collective-permute-start(bf16[2,96,768]{2,1,0:T(8,128)(2,1)} %get-tuple-element.387), channel_id=1, source_target_pairs={{0,8},{8,0},{16,24},{24,16},{1,9},{9,1},{17,25},{25,17},{2,10},{10... | collective-permute-start | bytes 884744 | tf_op jit(solution)/shard_map/ppermute | solution.py:369
  1213.6 64.3 %collective-permute-start.15 = (bf16[192,4016]{1,0:T(8,128)(2,1)S(1)}, bf16[192,4016]{1,0:T(8,128)(2,1)S(1)}, u32[]{:S(2)}, u32[]{:S(2)}) collective-permute-start(bf16[192,4016]{1,0:T(8,128)(2,1)S(1)} %token_grad.1.refs_0_), channel_id=1, source_target_pairs={{0,8},{8,0},{16,24},{24,16},{1,9},{9,1},{17,25},{25,17},{2,10},{10... | collective-permute-start | bytes 4626440 | tf_op jit(solution)/shard_map/ppermute | solution.py:369
  1215.5 71.2 %collective-permute-start.16 = (bf16[192,4016]{1,0:T(8,128)(2,1)S(1)}, bf16[192,4016]{1,0:T(8,128)(2,1)}, u32[]{:S(2)}, u32[]{:S(2)}) collective-permute-start(bf16[192,4016]{1,0:T(8,128)(2,1)S(1)} %token_grad.1.refs_0_), channel_id=1, source_target_pairs={{0,16},{8,24},{16,0},{24,8},{1,17},{9,25},{17,1},{25,9},{2,18},{10... | collective-permute-start | bytes 4626440 | tf_op jit(solution)/shard_map/ppermute | solution.py:369
  1216.9 69.7 %collective-permute-start.17 = (bf16[192,4016]{1,0:T(8,128)(2,1)S(1)}, bf16[192,4016]{1,0:T(8,128)(2,1)}, u32[]{:S(2)}, u32[]{:S(2)}) collective-permute-start(bf16[192,4016]{1,0:T(8,128)(2,1)S(1)} %token_grad.1.refs_0_), channel_id=1, source_target_pairs={{0,24},{8,16},{16,8},{24,0},{1,25},{9,17},{17,9},{25,1},{2,26},{10... | collective-permute-start | bytes 4626440 | tf_op jit(solution)/shard_map/ppermute | solution.py:369
  1217.1 104.2 %collective-permute-start.18 = (bf16[2,96,768]{2,1,0:T(8,128)(2,1)}, bf16[2,96,768]{2,1,0:T(8,128)(2,1)}, u32[]{:S(2)}, u32[]{:S(2)}) collective-permute-start(bf16[2,96,768]{2,1,0:T(8,128)(2,1)} %get-tuple-element.356), channel_id=1, source_target_pairs={{0,8},{8,0},{16,24},{24,16},{1,9},{9,1},{17,25},{25,17},{2,10},{10... | collective-permute-start | bytes 884744 | tf_op jit(solution)/shard_map/ppermute | solution.py:369
  1218.9 103.6 %collective-permute-start.19 = (bf16[2,96,768]{2,1,0:T(8,128)(2,1)}, bf16[2,96,768]{2,1,0:T(8,128)(2,1)}, u32[]{:S(2)}, u32[]{:S(2)}) collective-permute-start(bf16[2,96,768]{2,1,0:T(8,128)(2,1)} %get-tuple-element.356), channel_id=1, source_target_pairs={{0,16},{8,24},{16,0},{24,8},{1,17},{9,25},{17,1},{25,9},{2,18},{10... | collective-permute-start | bytes 884744 | tf_op jit(solution)/shard_map/ppermute | solution.py:369
  1277.8 45.9 %collective-permute-start.20 = (bf16[2,96,768]{2,1,0:T(8,128)(2,1)S(1)}, bf16[2,96,768]{2,1,0:T(8,128)(2,1)}, u32[]{:S(2)}, u32[]{:S(2)}) collective-permute-start(bf16[2,96,768]{2,1,0:T(8,128)(2,1)S(1)} %copy-done.77), channel_id=1, source_target_pairs={{0,24},{8,16},{16,8},{24,0},{1,25},{9,17},{17,9},{25,1},{2,26},{10... | collective-permute-start | bytes 884744 | tf_op jit(solution)/shard_map/ppermute | solution.py:369
  (220 other events, 4192.0 us)
Sparse Core Ops, SparseCore 0:
  14.0 56.2 all-gather.19
  73.1 38.9 reduce-scatter.9
  115.0 39.4 reduce-scatter.11
  156.5 50.7 all-gather.23
  209.4 50.5 all-gather.25
  262.0 50.5 all-gather.21
  314.8 50.5 all-gather.27
  367.5 50.3 all-gather.29
  517.7 31.2 reduce-scatter.13
  595.5 55.2 reduce-scatter.15
  655.1 57.6 reduce-scatter.17
  782.3 59.6 reduce-scatter.19
  844.8 53.2 reduce-scatter.21
  900.9 53.3 reduce-scatter.23
  999.5 62.0 reduce-scatter.25
  1063.0 37.3 all-gather.31
  1102.5 37.1 all-gather.33

commit v3 on v2

--- a/solution.py
+++ b/solution.py
@@ -381,6 +381,13 @@
         at = (0, seq_index ^ distance) + (0,) * (first.ndim - 1)
         whole = lax.dynamic_update_slice(whole, part[:, None], at)
     return whole
+
+
+def sum_of_pairs(parts):
+    parts = [part.astype(F32) for part in parts]
+    while len(parts) > 1:
+        parts = [one + two for one, two in zip(parts[::2], parts[1::2])]
+    return parts[0]
 
 
 def sum_over_seq(parts):
@@ -835,23 +842,19 @@
         columns = grad_hiddens[batch].reshape(rows, width).astype(BF16).T
         moved.append(exchange(columns.reshape(ways, part, rows)))
     moved[-1], grad_parts[0][1] = after(moved[-1], grad_parts[0][1])
-    stacks = [jnp.stack([parts[which] for parts in grad_parts]) for which in range(2)]
-    moved[-1], dense_grad, *stacks = after(moved[-1], dense_grad, *stacks)
-    moved[0], dense_grad = after(moved[0], dense_grad)
+    up_parts = jnp.stack([parts[0] for parts in grad_parts])
+    down_parts = [parts[1] for parts in grad_parts]
+    dense_parts = [parts[2] for parts in grad_parts[1:]]
+    moved[-1], up_parts, *dense_parts = after(moved[-1], up_parts, *dense_parts)
     moved = [lax.all_gather(item, "fsdp", axis=0, tiled=False) for item in moved]
+    moved[-1], dense_grad, *down_parts = after(moved[-1], dense_grad, *down_parts)
     grad_parts[0].append(scatter_owners(dense_grad))
     head_grad = jnp.concatenate([piece for piece in summed if piece is not None], 1)
-    wholes = [share(item) for item in stacks]
+    up_whole = share(up_parts)
+    down_whole = [lax.all_gather(item, "seq", axis=0, tiled=False) for item in down_parts]
     embed_part = token_grad(every_id, moved, head_grad)
-    dense = jnp.stack([parts[2] for parts in grad_parts])
-    dense = jnp.concatenate(
-        [
-            dense[:, :, : 3 * width].reshape(layers, shard, ways, 3 * part),
-            dense[:, :, 3 * width :].reshape(layers, shard, ways, part),
-        ],
-        3,
-    )
-    dense_part = sum_over_seq(dense.transpose(2, 0, 1, 3)).astype(BF16)
+    dense_sum = [sum_of_pairs(share(item)) for item in [grad_parts[0][2]] + dense_parts]
+    dense_sum = jnp.stack(dense_sum)
 
     tables = lax.dynamic_update_slice(
         jnp.zeros(bias_full.shape, F32), jnp.stack(table_grads), (0, 0, seq_index * head_local)
@@ -877,8 +880,8 @@
     loss_value, loss_count = tiny[-2], tiny[-1]
 
     squares_part = (
-        sum_squares(embed_part, dense_part, *stacks)
-        + sum_squares(gains_grad, bias_grad, router_grad) / ways
+        sum_squares(embed_part, up_parts, *down_parts)
+        + sum_squares(dense_sum, gains_grad, bias_grad, router_grad) / ways
     )
     grad_norm = jnp.sqrt(
         sum_everywhere(jnp.broadcast_to(squares_part, (ways, owners, 1)))[0]
@@ -886,17 +889,16 @@
     clip_factor = jnp.minimum(1.0, CLIP_NORM / (grad_norm + 1e-06))
 
     embed_grads = share(embed_part)
-    upward_grad, downward_grad = (by_source(items) for items in wholes)
-    dense_grad = by_source(share(dense_part)).transpose(0, 2, 1, 3)
-    attend_grad = dense_grad[..., : 3 * part].reshape(layers, shard, ways, 3, part)
+    upward_grad = by_source(up_whole)
+    attend_grad = dense_sum[:, :, : 3 * width].reshape(layers, shard, ways, 3, part)
     attend_grad = attend_grad.transpose(0, 1, 3, 2, 4).reshape(layers, shard, 3 * width)
-    output_grad = dense_grad[..., 3 * part :].reshape(layers, shard, width)
+    output_grad = dense_sum[:, :, 3 * width :]
     grads = (
         None,
         attend_grad,
         output_grad,
         upward_grad,
-        downward_grad,
+        None,
         router_grad,
         gains_grad,
         bias_grad,
@@ -932,13 +934,23 @@
         bias_square,
     )
     results = [loss_value, loss_count, grad_norm]
-    results.extend(
-        embed_adam(embed_weight, embed_grads, embed_mean, embed_square, clip_factor, STEP_RATES[0])
-    )
-    for weight, grad, first, second, rate in list(
-        zip(params, grads, means, squares, STEP_RATES)
-    )[1:]:
-        results.extend(adam_update(weight, grad.astype(F32) * clip_factor, first, second, rate))
+    states = [None] * len(params)
+    states[0] = embed_adam(
+        embed_weight, embed_grads, embed_mean, embed_square, clip_factor, STEP_RATES[0]
+    )
+    for index in (3, 4, 1, 2, 5, 6, 7):
+        grad = grads[index]
+        if index == 4:
+            grad = jnp.stack(after(states[3][0], *down_whole)[1:])
+        states[index] = adam_update(
+            params[index],
+            grad.astype(F32) * clip_factor,
+            means[index],
+            squares[index],
+            STEP_RATES[index],
+        )
+    for state in states:
+        results.extend(state)
     return tuple(results)
 
 

time: 1370 us -> 1340 us (0.978)
  local copies, waits for them, and re-layouts: 146 us -> 128 us
    ppermute x27 -> x24, waiting for transfers between devices: 90.6 us -> 41.7 us  [to_relative(): lax.ppermute(part, 'seq', [(way, way ^ distance) for way in range(ways)])]
    all_gather x2, waiting for transfers between devices: 0.01 us -> 40 us  [per_device(): lax.all_gather(item, 'fsdp', axis=0, tiled=False)]
    ppermute x27 -> x24, starting transfers between devices: 34.1 us -> 30.2 us  [to_relative(): lax.ppermute(part, 'seq', [(way, way ^ distance) for way in range(ways)])]
    unnamed x385 -> x389, local copies, waits for them, and re-layouts: 29.5 us -> 32.8 us
  transfers between devices with their start and end apart: 79 -> 78, of which waited for: 24 -> 31; matrix products, arithmetic and copies ran while one was open for 36% -> 37% of each run, Pallas kernels for 19% -> 16%
where the time goes in v3:
time: 1340 us; the launch traced here: 1320 us
  matrix products  308 us (23%)
  Pallas kernels  252 us (19%)
  waiting for transfers between devices  212 us (16%)
  starting transfers between devices  170 us (13%)
  other arithmetic  137 us (10%)
  local copies, waits for them, and re-layouts  128 us (10%)
  blocking collectives  91.3 us (7%)
  between operations  25.6 us (2%)
    dot_general x37, matrix products, contract(): lax.dot_general(left_side, right_side, (((left_dim,), (right_dim,)), ((),...  145 us
    all_to_all x33, starting transfers between devices, exchange(): return lax.all_to_all(parts, 'seq', split_axis=0, concat_axis=0, tiled=True)  130 us
    dot_general x16, matrix products, matmul(): return jnp.dot(left_side, right_side, preferred_element_type=F32)  107 us
    pallas_call x4, Pallas kernels, attend_back(): pl.pallas_call(attend_back_kernel, grid=(count,), in_specs=[pl.BlockSpec(...  89.5 us
    all_to_all x33, waiting for transfers between devices, exchange(): return lax.all_to_all(parts, 'seq', split_axis=0, concat_axis=0, tiled=True)  82.3 us
    pallas_call x4, Pallas kernels, attend(): pl.pallas_call(attend_kernel, grid=(count,), in_specs=[pl.BlockSpec(memor...  59.3 us
    sub x7, other arithmetic, adam_update(): weight - rate * (mean_hat / (jnp.sqrt(square_hat) + ADAM_EPSILON) + WEIGH...  55.3 us
    pallas_call x1, Pallas kernels, token_grad(): pl.pallas_call(token_grad_kernel, grid=(pl.cdiv(vocab_rows, block), owner...  47.7 us
  transfers between devices with their start and end apart: 78, of which 31 were waited for; matrix products, arithmetic and copies ran while one was open for 37% of the time, Pallas kernels for 16%

profile of v3, /device:TPU:0, one launch (start us, length us, event | category | flops | bytes accessed | tf_op | source)
XLA Modules:
  0.0 1323.2 jit_solution(5841772274096414280)
XLA Ops:
  14.0 7.8 convert_element_type.435
  21.8 14.7 %all-gather.11 = s32[8,2,256]{2,1,0:T(2,128)S(1)} all-gather(s32[1,2,256]{2,1,0:T(2,128)S(1)} %bitcast.704), channel_id=2, replica_groups=mesh['seq'=4,'fsdp'=8] {'fsdp'}, dimensions={0}, use_global_device_ids=true | all-gather | bytes 18432 | tf_op jit(solution)/shard_map/all_gather | solution.py:628
  36.6 18.5 %fusion.85 = bf16[2048,768]{1,0:T(8,128)(2,1)} fusion(bf16[4016,768]{1,0:T(8,128)(2,1)} %convert_element_type.435, s32[2048]{0:T(1024)S(1)} %bitcast.707), kind=kOutput, calls=%fused_computation.123 | convolution fusion | flops 12643041280 | bytes 9322496 | tf_op jit(solution)/shard_map/dot_general | solution.py:28
  56.9 15.5 %all_gather.68 = f32[8,80,128]{2,1,0:T(8,128)S(1)} all-gather(f32[1,80,128]{2,1,0:T(8,128)S(1)} %pad_bitcast_fusion.1), channel_id=1, replica_groups=mesh['seq'=4,'fsdp'=8] {'fsdp'}, dimensions={0}, use_global_device_ids=true | all-gather | bytes 368640 | tf_op jit(solution)/shard_map/all_gather | solution.py:638
  72.3 18.4 %fusion.84 = bf16[2048,768]{1,0:T(8,128)(2,1)} fusion(bf16[4016,768]{1,0:T(8,128)(2,1)} %convert_element_type.435, s32[2048]{0:T(1024)S(1)} %bitcast.706), kind=kOutput, calls=%fused_computation.122 | convolution fusion | flops 12643041280 | bytes 9322496 | tf_op jit(solution)/shard_map/dot_general | solution.py:28
  110.7 17.2 %fusion.2 = f32[512,32,128]{2,1,0:T(8,128)} fusion(s32[512,65]{1,0:T(8,128)S(1)} %get-tuple-element.394, f32[512,65]{1,0:T(8,128)S(1)} %concatenate.97, s32[512,65]{1,0:T(8,128)S(1)} %get-tuple-element.393), kind=kOutput, calls=%fused_computation.5 | convolution fusion | flops 1642168320 | bytes 8787968 | tf_op jit(solution)/shard_map/rkh,rkl->rhl/dot_general | solution.py:711
  127.9 9.9 copy.344
  137.8 7.7 slice.321
  167.0 18.9 %all-gather.5 = s32[32,2,256]{2,1,0:T(2,128)S(1)} all-gather(s32[8,2,256]{2,1,0:T(2,128)S(1)} %all-gather.11), channel_id=7, replica_groups=mesh['seq'=4,'fsdp'=8] {'seq'}, dimensions={0}, use_global_device_ids=true | all-gather | bytes 81920 | tf_op jit(solution)/shard_map/all_gather | solution.py:733
  186.6 14.7 %attend.4 = (bf16[4,1,192,256]{3,2,1,0:T(8,128)(2,1)}, f32[1,12,256]{2,1,0:T(8,128)S(1)}) custom-call(s32[1]{0:T(128)} %bitcast.length_ref, bf16[4,1,576,256]{3,2,1,0:T(8,128)(2,1)S(1)} %all-to-all-done.qkv_ref, f32[3,1792,256]{2,1,0:T(8,128)} %copy-done.6), custom_call_target="tpu_custom_call" | custom-call | flops 16106127360 | bytes 6684672 | tf_op jit(solution)/shard_map/attend/pallas_call | solution.py:116
  221.7 8.6 all-to-all-done.8.qkv_ref
  230.3 14.7 %attend.6 = (bf16[4,1,192,256]{3,2,1,0:T(8,128)(2,1)}, f32[1,12,256]{2,1,0:T(8,128)S(1)}) custom-call(s32[1]{0:T(128)} %bitcast.49.length_ref, bf16[4,1,576,256]{3,2,1,0:T(8,128)(2,1)S(1)} %all-to-all-done.8.qkv_ref, f32[3,1792,256]{2,1,0:T(8,128)} %copy-done.6), custom_call_target="tpu_custom_call" | custom-call | flops 16106127360 | bytes 6684672 | tf_op jit(solution)/shard_map/attend/pallas_call | solution.py:116
  269.0 8.5 multiply_convert_fusion.5
  287.8 7.3 multiply_convert_fusion.3
  341.8 14.7 %attend.5 = (bf16[4,1,192,256]{3,2,1,0:T(8,128)(2,1)}, f32[1,12,256]{2,1,0:T(8,128)S(1)}) custom-call(s32[1]{0:T(128)} %bitcast.length_ref, bf16[4,1,576,256]{3,2,1,0:T(8,128)(2,1)S(1)} %all-to-all-done.4.qkv_ref, f32[3,1792,256]{2,1,0:T(8,128)} %copy-done.7), custom_call_target="tpu_custom_call" | custom-call | flops 16106127360 | bytes 6684672 | tf_op jit(solution)/shard_map/attend/pallas_call | solution.py:116
  360.8 15.0 %attend.7 = (bf16[4,1,192,256]{3,2,1,0:T(8,128)(2,1)}, f32[1,12,256]{2,1,0:T(8,128)S(1)}) custom-call(s32[1]{0:T(128)} %bitcast.49.length_ref, bf16[4,1,576,256]{3,2,1,0:T(8,128)(2,1)} %all-to-all-done.12.qkv_ref, f32[3,1792,256]{2,1,0:T(8,128)} %copy-done.7), custom_call_target="tpu_custom_call" | custom-call | flops 16106127360 | bytes 6684672 | tf_op jit(solution)/shard_map/attend/pallas_call | solution.py:116
  401.5 8.4 multiply_convert_fusion.4
  410.0 8.8 all-gather.34.cloned.1.call-done
  429.0 7.4 multiply_convert_fusion.2
  449.9 6.9 all-to-all-done.15
  461.4 15.9 %all_gather.77 = bf16[512,768]{1,0:T(8,128)(2,1)S(1)} all-gather(bf16[64,768]{1,0:T(8,128)(2,1)S(1)} %bitcast.681), channel_id=1, replica_groups=mesh['seq'=4,'fsdp'=8] {'fsdp'}, dimensions={0}, use_global_device_ids=true | all-gather | bytes 884736 | tf_op jit(solution)/shard_map/all_gather | solution.py:741
  488.3 14.2 %all-gather.12 = f32[8,2,512]{2,1,0:T(2,128)S(1)} all-gather(f32[1,2,512]{2,1,0:T(2,128)S(1)} %maximum_bitcast_fusion.1), channel_id=8, replica_groups=mesh['seq'=4,'fsdp'=8] {'fsdp'}, dimensions={0}, use_global_device_ids=true | all-gather | bytes 36864 | tf_op jit(solution)/shard_map/all_gather | solution.py:747
  502.7 6.8 multiply_convert_fusion.1
  511.5 6.8 fusion.298
  518.3 31.5 %reduce-scatter.14.cloned.1.call-done = f32[64,768]{1,0:T(8,128)} async-done(((f32[512,768]{1,0:T(8,128)}), f32[64,768]{1,0:T(8,128)}) %reduce-scatter.14.cloned.1.call-update) | async-done | bytes 196624 | tf_op jit(solution)/shard_map/reduce_scatter | solution.py:758
  570.1 9.5 fusion.36
  579.6 8.2 fusion.22
  589.1 7.1 convolution_convert_fusion.5
  596.3 8.4 multiply_convert_fusion
  604.7 8.6 copy.318
  647.0 8.8 convolution_convert_fusion.4
  660.7 22.7 %attend_back.5 = (bf16[4,1,576,256]{3,2,1,0:T(8,128)(2,1)}, f32[3,1,2048]{2,1,0:T(1,128)S(1)}) custom-call(s32[1]{0:T(128)} %bitcast.49.length_ref, bf16[4,1,576,256]{3,2,1,0:T(8,128)(2,1)} %all-to-all-done.12.qkv_ref, bf16[4,1,192,256]{3,2,1,0:T(8,128)(2,1)S(1)} %all-to-all-done.22.out_grad_ref, f32[1,12,256]{2,1,0:T(8,128)S(1)} %get-tuple-element.140.lse_ref, ...), custom_call_target="tpu_custom_call" | custom-call | flops 25165824000 | bytes 7864320 | tf_op jit(solution)/shard_map/attend_back/pallas_call | solution.py:206
  718.4 12.1 all_to_all.180.out_grad_ref
  734.2 22.2 %attend_back.4 = (bf16[4,1,576,256]{3,2,1,0:T(8,128)(2,1)}, f32[3,1,2048]{2,1,0:T(1,128)S(1)}) custom-call(s32[1]{0:T(128)} %bitcast.length_ref, bf16[4,1,576,256]{3,2,1,0:T(8,128)(2,1)S(1)} %all-to-all-done.4.qkv_ref, bf16[4,1,192,256]{3,2,1,0:T(8,128)(2,1)S(1)} %all_to_all.180.out_grad_ref, f32[1,12,256]{2,1,0:T(8,128)S(1)} %get-tuple-element.132.lse_ref, ...), custom_call_target="tpu_custom_call" | custom-call | flops 25165824000 | bytes 7864320 | tf_op jit(solution)/shard_map/attend_back/pallas_call | solution.py:206
  799.0 8.9 fusion.29
  807.9 8.2 fusion.15
  844.5 9.2 convolution_convert_fusion.1
  894.0 22.3 %attend_back.6 = (bf16[4,1,576,256]{3,2,1,0:T(8,128)(2,1)}, f32[3,1,2048]{2,1,0:T(1,128)S(1)}) custom-call(s32[1]{0:T(128)} %bitcast.length_ref, bf16[4,1,576,256]{3,2,1,0:T(8,128)(2,1)S(1)} %copy-done.11, bf16[4,1,192,256]{3,2,1,0:T(8,128)(2,1)S(1)} %all-to-all-done.26.out_grad_ref, f32[1,12,256]{2,1,0:T(8,128)S(1)} %get-tuple-element.147.lse_ref, ...), custom_call_target="tpu_custom_call" | custom-call | flops 25165824000 | bytes 7864320 | tf_op jit(solution)/shard_map/attend_back/pallas_call | solution.py:206
  928.4 22.3 %attend_back.7 = (bf16[4,1,576,256]{3,2,1,0:T(8,128)(2,1)}, f32[3,1,2048]{2,1,0:T(1,128)S(1)}) custom-call(s32[1]{0:T(128)} %bitcast.49.length_ref, bf16[4,1,576,256]{3,2,1,0:T(8,128)(2,1)S(1)} %copy-done.9, bf16[4,1,192,256]{3,2,1,0:T(8,128)(2,1)S(1)} %all-to-all-done.30.out_grad_ref, f32[1,12,256]{2,1,0:T(8,128)S(1)} %get-tuple-element.159.lse_ref, ...), custom_call_target="tpu_custom_call" | custom-call | flops 25165824000 | bytes 7864320 | tf_op jit(solution)/shard_map/attend_back/pallas_call | solution.py:206
  961.8 7.0 all-to-all-done.31
  993.6 31.5 %all-gather.38.cloned.1.call-done = bf16[32,192,256]{2,1,0:T(8,128)(2,1)} async-done(((bf16[4,192,256]{2,1,0:T(8,128)(2,1)}), bf16[32,192,256]{2,1,0:T(8,128)(2,1)}) %all-gather.38.cloned.1.call-update) | async-done | bytes 3145744 | tf_op jit(solution)/shard_map/all_gather | solution.py:849
  1073.9 9.9 collective-permute-done.16
  1086.6 23.0 %collective-permute-done.21 = bf16[2,96,3072]{2,1,0:T(8,128)(2,1)} collective-permute-done((bf16[2,96,3072]{2,1,0:T(8,128)(2,1)}, bf16[2,96,3072]{2,1,0:T(8,128)(2,1)}, u32[]{:S(2)}, u32[]{:S(2)}) %collective-permute-start.21) | collective-permute-done | bytes 1179680 | tf_op jit(solution)/shard_map/ppermute | solution.py:369
  1116.7 8.5 all-gather.36.cloned.1.call-done
  1127.1 47.7 %token_grad.1.refs_0_ = bf16[192,4016]{1,0:T(8,128)(2,1)S(1)} custom-call(s32[8,2,1024]{2,1,0:T(2,128)S(1)} %reshape.1096.ids_ref, bf16[8,4,192,256]{3,2,1,0:T(8,128)(2,1)S(1)} %bitcast.621, bf16[8,4,192,256]{3,2,1,0:T(8,128)(2,1)} %bitcast.711, f32[192,4016]{1,0:T(8,128)} %pad_maximum_fusion.4.refs_2_), custom_call_target="tpu_custom_call" | custom-call | flops 50532974592 | bytes 25165824 | tf_op jit(solution)/shard_map/token_grad/pallas_call | solution.py:344
  1217.5 23.9 %multiply_subtract_fusion.1 = (f32[2,4,96,3072]{3,2,1,0:T(8,128)}, f32[2,4,96,3072]{3,2,1,0:T(8,128)}, f32[2,4,96,3072]{3,2,1,0:T(8,128)}) fusion(f32[2,4,96,3072]{3,2,1,0:T(8,128)} %param.49, f32[]{:T(128)} %min.3, bf16[2,4,96,3072]{3,2,1,0:T(8,128)(2,1)} %bitcast_dynamic-update-slice_fusion, f32[2,4,96,3072]{3,2,1,0:T(8,128)} %param.50, ...), kind=kLoop, calls=%fused_computation.16 | loop fusion | flops 40108032 | bytes 61341700 | tf_op jit(solution)/shard_map/sub | solution.py:551
  1243.1 24.8 %multiply_subtract_fusion = (f32[2,4,384,768]{3,2,1,0:T(8,128)}, f32[2,4,384,768]{3,2,1,0:T(8,128)}, f32[2,4,384,768]{3,2,1,0:T(8,128)}) fusion(f32[2,4,384,768]{3,2,1,0:T(8,128)} %param.52, f32[]{:T(128)} %min.3, bf16[1,4,384,768]{3,2,1,0:T(8,128)(2,1)} %bitcast.635, bf16[1,4,384,768]{3,2,1,0:T(8,128)(2,1)} %bitcast.634, f32[2,4,384,768]{3,2,1,0:T(8,128)} %param.53, ...), kind=kLoop, calls=%fused_computation.13 | loop fusion | flops 42467328 | bytes 61341700 | tf_op jit(solution)/shard_map/sub | solution.py:551
  1281.2 34.0 %embed_adam.1 = (f32[4016,768]{1,0:T(8,128)}, f32[4016,768]{1,0:T(8,128)}, f32[4016,768]{1,0:T(8,128)}) custom-call(f32[1]{0:T(128)} %bitcast.177.clip_ref, s32[1]{0:T(128)} %bitcast.178.seq_ref, f32[4016,768]{1,0:T(8,128)} %weight_ref.1, f32[4016,768]{1,0:T(8,128)} %first_ref.1, f32[4016,768]{1,0:T(8,128)} %second_ref.1, ...), custom_call_target="tpu_custom_call" | custom-call | flops 61685760 | bytes 80191488 | tf_op jit(solution)/shard_map/embed_adam/pallas_call | solution.py:303
  (855 shorter events, 589.9 us)
Async XLA Ops:
  7.2 83.5 %all-gather.24.cloned.1.call-start = ((), (), s32[]{:S(2)}) async-start(), calls=%async_computation.46 | async-start | bytes 5308416 | tf_op jit(solution)/shard_map/all_gather | solution.py:619
  14.0 142.7 %reduce-scatter.10.cloned.1.call-start = ((), (), s32[]{:S(2)}) async-start(), calls=%async_computation.45 | async-start | bytes 3538944 | tf_op jit(solution)/shard_map/reduce_scatter | solution.py:654
  55.1 149.8 %reduce-scatter.12.cloned.1.call-start = ((), (), s32[]{:S(2)}) async-start(), calls=%async_computation.48 | async-start | bytes 3538944 | tf_op jit(solution)/shard_map/reduce_scatter | solution.py:654
  90.7 178.3 %all-gather.28.cloned.1.call-start = ((), (), s32[]{:S(2)}) async-start(), calls=%async_computation.56 | async-start | bytes 5308416 | tf_op jit(solution)/shard_map/all_gather | solution.py:619
  96.2 181.4 %all-gather.30.cloned.1.call-start = ((), (), s32[]{:S(2)}) async-start(), calls=%async_computation.57 | async-start | bytes 5308416 | tf_op jit(solution)/shard_map/all_gather | solution.py:619
  102.9 210.2 %all-gather.26.cloned.1.call-start = ((), (), s32[]{:S(2)}) async-start(), calls=%async_computation.47 | async-start | bytes 5308416 | tf_op jit(solution)/shard_map/all_gather | solution.py:619
  108.1 293.4 %all-gather.32.cloned.1.call-start = ((), (), s32[]{:S(2)}) async-start(), calls=%async_computation.58 | async-start | bytes 5308416 | tf_op jit(solution)/shard_map/all_gather | solution.py:619
  163.1 23.5 %all-to-all-start = ((bf16[4,1,576,256]{3,2,1,0:T(8,128)(2,1)}), bf16[4,1,576,256]{3,2,1,0:T(8,128)(2,1)S(1)}, u32[]{:S(2)}, u32[]{:S(2)}) async-start(bf16[4,1,576,256]{3,2,1,0:T(8,128)(2,1)} %get-tuple-element.115), calls=%async_computation.1 | async-start | bytes 2359296 | tf_op jit(solution)/shard_map/all_to_all | solution.py:364
  216.4 202.4 %all-gather.34.cloned.1.call-start = ((), (), s32[]{:S(2)}) async-start(), calls=%async_computation.59 | async-start | bytes 5308416 | tf_op jit(solution)/shard_map/all_gather | solution.py:619
  337.1 19.6 %all-to-all-start.12 = ((bf16[4,1,576,256]{3,2,1,0:T(8,128)(2,1)}), bf16[4,1,576,256]{3,2,1,0:T(8,128)(2,1)}, u32[]{:S(2)}, u32[]{:S(2)}) async-start(bf16[4,1,576,256]{3,2,1,0:T(8,128)(2,1)} %copy-done.12), calls=%async_computation.14 | async-start | bytes 2359296 | tf_op jit(solution)/shard_map/all_to_all | solution.py:364
  398.0 26.7 %all-to-all-start.14 = ((bf16[4,1,96,768]{3,2,1,0:T(8,128)(2,1)}), bf16[4,1,96,768]{3,2,1,0:T(8,128)(2,1)S(1)}, u32[]{:S(2)}, u32[]{:S(2)}) async-start(bf16[4,1,96,768]{3,2,1,0:T(8,128)(2,1)} %bitcast.69), calls=%async_computation.16 | async-start | bytes 1179648 | tf_op jit(solution)/shard_map/all_to_all | solution.py:364
  447.3 102.5 %reduce-scatter.14.cloned.1.call-start = ((), (), s32[]{:S(2)}) async-start(), calls=%async_computation.49 | async-start | bytes 1769472 | tf_op jit(solution)/shard_map/reduce_scatter | solution.py:758
  569.8 288.3 %reduce-scatter.16.cloned.1.call-start = ((), (), s32[]{:S(2)}) async-start(), calls=%async_computation.50 | async-start | bytes 5308416 | tf_op jit(solution)/shard_map/reduce_scatter | solution.py:558
  646.8 220.2 %reduce-scatter.18.cloned.1.call-start = ((), (), s32[]{:S(2)}) async-start(), calls=%async_computation.51 | async-start | bytes 5308416 | tf_op jit(solution)/shard_map/reduce_scatter | solution.py:558
  657.2 26.2 %collective-permute-start.5 = (bf16[192,1024]{1,0:T(8,128)(2,1)S(1)}, bf16[192,1024]{1,0:T(8,128)(2,1)S(1)}, u32[]{:S(2)}, u32[]{:S(2)}) collective-permute-start(bf16[192,1024]{1,0:T(8,128)(2,1)S(1)} %get-tuple-element.388), channel_id=1, source_target_pairs={{0,24},{8,16},{16,8},{24,0},{1,25},{9,17},{17,9},{25,1},{2,26},{10... | collective-permute-start | bytes 1179656 | tf_op jit(solution)/shard_map/ppermute | solution.py:369
  660.1 23.3 %collective-permute-start.4 = (bf16[192,1024]{1,0:T(8,128)(2,1)S(1)}, bf16[192,1024]{1,0:T(8,128)(2,1)S(1)}, u32[]{:S(2)}, u32[]{:S(2)}) collective-permute-start(bf16[192,1024]{1,0:T(8,128)(2,1)S(1)} %get-tuple-element.389), channel_id=1, source_target_pairs={{0,16},{8,24},{16,0},{24,8},{1,17},{9,25},{17,1},{25,9},{2,18},{10... | collective-permute-start | bytes 1179656 | tf_op jit(solution)/shard_map/ppermute | solution.py:369
  660.6 22.8 %collective-permute-start.3 = (bf16[192,1024]{1,0:T(8,128)(2,1)S(1)}, bf16[192,1024]{1,0:T(8,128)(2,1)S(1)}, u32[]{:S(2)}, u32[]{:S(2)}) collective-permute-start(bf16[192,1024]{1,0:T(8,128)(2,1)S(1)} %get-tuple-element.387), channel_id=1, source_target_pairs={{0,8},{8,0},{16,24},{24,16},{1,9},{9,1},{17,25},{25,17},{2,10},{10... | collective-permute-start | bytes 1179656 | tf_op jit(solution)/shard_map/ppermute | solution.py:369
  730.7 25.8 %collective-permute-start.2 = (bf16[192,1024]{1,0:T(8,128)(2,1)S(1)}, bf16[192,1024]{1,0:T(8,128)(2,1)S(1)}, u32[]{:S(2)}, u32[]{:S(2)}) collective-permute-start(bf16[192,1024]{1,0:T(8,128)(2,1)S(1)} %get-tuple-element.385), channel_id=1, source_target_pairs={{0,24},{8,16},{16,8},{24,0},{1,25},{9,17},{17,9},{25,1},{2,26},{10... | collective-permute-start | bytes 1179656 | tf_op jit(solution)/shard_map/ppermute | solution.py:369
  731.8 24.7 %collective-permute-start.1 = (bf16[192,1024]{1,0:T(8,128)(2,1)S(1)}, bf16[192,1024]{1,0:T(8,128)(2,1)S(1)}, u32[]{:S(2)}, u32[]{:S(2)}) collective-permute-start(bf16[192,1024]{1,0:T(8,128)(2,1)S(1)} %get-tuple-element.386), channel_id=1, source_target_pairs={{0,16},{8,24},{16,0},{24,8},{1,17},{9,25},{17,1},{25,9},{2,18},{10... | collective-permute-start | bytes 1179656 | tf_op jit(solution)/shard_map/ppermute | solution.py:369
  733.2 23.3 %collective-permute-start = (bf16[192,1024]{1,0:T(8,128)(2,1)S(1)}, bf16[192,1024]{1,0:T(8,128)(2,1)S(1)}, u32[]{:S(2)}, u32[]{:S(2)}) collective-permute-start(bf16[192,1024]{1,0:T(8,128)(2,1)S(1)} %get-tuple-element.384), channel_id=1, source_target_pairs={{0,8},{8,0},{16,24},{24,16},{1,9},{9,1},{17,25},{25,17},{2,10},{10... | collective-permute-start | bytes 1179656 | tf_op jit(solution)/shard_map/ppermute | solution.py:369
  761.9 161.5 %reduce-scatter.20.cloned.1.call-start = ((), (), s32[]{:S(2)}) async-start(), calls=%async_computation.52 | async-start | bytes 5308416 | tf_op jit(solution)/shard_map/reduce_scatter | solution.py:558
  798.9 124.4 %reduce-scatter.22.cloned.1.call-start = ((), (), s32[]{:S(2)}) async-start(), calls=%async_computation.53 | async-start | bytes 5308416 | tf_op jit(solution)/shard_map/reduce_scatter | solution.py:558
  844.1 136.3 %reduce-scatter.24.cloned.1.call-start = ((), (), s32[]{:S(2)}) async-start(), calls=%async_computation.54 | async-start | bytes 5308416 | tf_op jit(solution)/shard_map/reduce_scatter | solution.py:558
  884.7 31.6 %all-to-all-start.30 = ((bf16[4,1,192,256]{3,2,1,0:T(8,128)(2,1)}), bf16[4,1,192,256]{3,2,1,0:T(8,128)(2,1)S(1)}, u32[]{:S(2)}, u32[]{:S(2)}) async-start(bf16[4,1,192,256]{3,2,1,0:T(8,128)(2,1)} %bitcast.141), calls=%async_computation.35 | async-start | bytes 786432 | tf_op jit(solution)/shard_map/all_to_all | solution.py:364
  890.5 25.8 %collective-permute-start.8 = (bf16[192,1024]{1,0:T(8,128)(2,1)}, bf16[192,1024]{1,0:T(8,128)(2,1)S(1)}, u32[]{:S(2)}, u32[]{:S(2)}) collective-permute-start(bf16[192,1024]{1,0:T(8,128)(2,1)} %get-tuple-element.379), channel_id=1, source_target_pairs={{0,24},{8,16},{16,8},{24,0},{1,25},{9,17},{17,9},{25,1},{2,26},{10... | collective-permute-start | bytes 1179656 | tf_op jit(solution)/shard_map/ppermute | solution.py:369
  893.5 22.9 %collective-permute-start.7 = (bf16[192,1024]{1,0:T(8,128)(2,1)}, bf16[192,1024]{1,0:T(8,128)(2,1)}, u32[]{:S(2)}, u32[]{:S(2)}) collective-permute-start(bf16[192,1024]{1,0:T(8,128)(2,1)} %get-tuple-element.380), channel_id=1, source_target_pairs={{0,16},{8,24},{16,0},{24,8},{1,17},{9,25},{17,1},{25,9},{2,18},{10... | collective-permute-start | bytes 1179656 | tf_op jit(solution)/shard_map/ppermute | solution.py:369
  894.0 22.4 %collective-permute-start.6 = (bf16[192,1024]{1,0:T(8,128)(2,1)S(1)}, bf16[192,1024]{1,0:T(8,128)(2,1)}, u32[]{:S(2)}, u32[]{:S(2)}) collective-permute-start(bf16[192,1024]{1,0:T(8,128)(2,1)S(1)} %get-tuple-element.378), channel_id=1, source_target_pairs={{0,8},{8,0},{16,24},{24,16},{1,9},{9,1},{17,25},{25,17},{2,10},{10... | collective-permute-start | bytes 1179656 | tf_op jit(solution)/shard_map/ppermute | solution.py:369
  918.9 34.0 %all-to-all-start.27 = ((bf16[4,1,576,256]{3,2,1,0:T(8,128)(2,1)}), bf16[4,1,576,256]{3,2,1,0:T(8,128)(2,1)}, u32[]{:S(2)}, u32[]{:S(2)}) async-start(bf16[4,1,576,256]{3,2,1,0:T(8,128)(2,1)} %get-tuple-element.150), calls=%async_computation.31 | async-start | bytes 2359296 | tf_op jit(solution)/shard_map/all_to_all | solution.py:364
  924.7 26.0 %collective-permute-start.11 = (bf16[192,944]{1,0:T(8,128)(2,1)S(1)}, bf16[192,944]{1,0:T(8,128)(2,1)S(1)}, u32[]{:S(2)}, u32[]{:S(2)}) collective-permute-start(bf16[192,944]{1,0:T(8,128)(2,1)S(1)} %get-tuple-element.382), channel_id=1, source_target_pairs={{0,24},{8,16},{16,8},{24,0},{1,25},{9,17},{17,9},{25,1},{2,26},{10... | collective-permute-start | bytes 1087496 | tf_op jit(solution)/shard_map/ppermute | solution.py:369
  927.7 23.0 %collective-permute-start.10 = (bf16[192,944]{1,0:T(8,128)(2,1)S(1)}, bf16[192,944]{1,0:T(8,128)(2,1)S(1)}, u32[]{:S(2)}, u32[]{:S(2)}) collective-permute-start(bf16[192,944]{1,0:T(8,128)(2,1)S(1)} %get-tuple-element.383), channel_id=1, source_target_pairs={{0,16},{8,24},{16,0},{24,8},{1,17},{9,25},{17,1},{25,9},{2,18},{10... | collective-permute-start | bytes 1087496 | tf_op jit(solution)/shard_map/ppermute | solution.py:369
  928.2 22.5 %collective-permute-start.9 = (bf16[192,944]{1,0:T(8,128)(2,1)S(1)}, bf16[192,944]{1,0:T(8,128)(2,1)S(1)}, u32[]{:S(2)}, u32[]{:S(2)}) collective-permute-start(bf16[192,944]{1,0:T(8,128)(2,1)S(1)} %get-tuple-element.381), channel_id=1, source_target_pairs={{0,8},{8,0},{16,24},{24,16},{1,9},{9,1},{17,25},{25,17},{2,10},{10... | collective-permute-start | bytes 1087496 | tf_op jit(solution)/shard_map/ppermute | solution.py:369
  978.0 47.1 %all-gather.38.cloned.1.call-start = ((), (), s32[]{:S(2)}) async-start(), calls=%async_computation.61 | async-start | bytes 3538944 | tf_op jit(solution)/shard_map/all_gather | solution.py:849
  984.6 128.6 %reduce-scatter.26.cloned.1.call-start = ((), (), s32[]{:S(2)}) async-start(), calls=%async_computation.55 | async-start | bytes 5308416 | tf_op jit(solution)/shard_map/reduce_scatter | solution.py:558
  1034.3 91.0 %all-gather.36.cloned.1.call-start = ((), (), s32[]{:S(2)}) async-start(), calls=%async_computation.60 | async-start | bytes 3538944 | tf_op jit(solution)/shard_map/all_gather | solution.py:849
  1051.8 189.5 %all-gather.40.cloned.1.call-start = ((), (), s32[]{:S(2)}) async-start(), calls=%async_computation.62 | async-start | bytes 2949120 | tf_op jit(solution)/shard_map/all_gather | solution.py:854
  1051.9 19.9 %collective-permute-start.17 = (bf16[96,3072]{1,0:T(8,128)(2,1)S(1)}, bf16[96,3072]{1,0:T(8,128)(2,1)S(1)}, u32[]{:S(2)}, u32[]{:S(2)}) collective-permute-start(bf16[96,3072]{1,0:T(8,128)(2,1)S(1)} %copy-done.84), channel_id=1, source_target_pairs={{0,24},{8,16},{16,8},{24,0},{1,25},{9,17},{17,9},{25,1},{2,26},{10... | collective-permute-start | bytes 1769480 | tf_op jit(solution)/shard_map/ppermute | solution.py:369
  1054.6 29.1 %collective-permute-start.16 = (bf16[96,3072]{1,0:T(8,128)(2,1)S(1)}, bf16[96,3072]{1,0:T(8,128)(2,1)S(1)}, u32[]{:S(2)}, u32[]{:S(2)}) collective-permute-start(bf16[96,3072]{1,0:T(8,128)(2,1)S(1)} %copy-done.84), channel_id=1, source_target_pairs={{0,16},{8,24},{16,0},{24,8},{1,17},{9,25},{17,1},{25,9},{2,18},{10... | collective-permute-start | bytes 1769480 | tf_op jit(solution)/shard_map/ppermute | solution.py:369
  1055.2 29.4 %collective-permute-start.15 = (bf16[96,3072]{1,0:T(8,128)(2,1)S(1)}, bf16[96,3072]{1,0:T(8,128)(2,1)}, u32[]{:S(2)}, u32[]{:S(2)}) collective-permute-start(bf16[96,3072]{1,0:T(8,128)(2,1)S(1)} %copy-done.84), channel_id=1, source_target_pairs={{0,8},{8,0},{16,24},{24,16},{1,9},{9,1},{17,25},{25,17},{2,10},{10... | collective-permute-start | bytes 1769480 | tf_op jit(solution)/shard_map/ppermute | solution.py:369
  1055.5 54.1 %collective-permute-start.21 = (bf16[2,96,3072]{2,1,0:T(8,128)(2,1)}, bf16[2,96,3072]{2,1,0:T(8,128)(2,1)}, u32[]{:S(2)}, u32[]{:S(2)}) collective-permute-start(bf16[2,96,3072]{2,1,0:T(8,128)(2,1)} %pad_maximum_fusion.6), channel_id=1, source_target_pairs={{0,8},{8,0},{16,24},{24,16},{1,9},{9,1},{17,25},{25,17},{2,10},{10... | collective-permute-start | bytes 3538952 | tf_op jit(solution)/shard_map/ppermute | solution.py:369
  1057.2 54.7 %collective-permute-start.22 = (bf16[2,96,3072]{2,1,0:T(8,128)(2,1)}, bf16[2,96,3072]{2,1,0:T(8,128)(2,1)S(1)}, u32[]{:S(2)}, u32[]{:S(2)}) collective-permute-start(bf16[2,96,3072]{2,1,0:T(8,128)(2,1)} %pad_maximum_fusion.6), channel_id=1, source_target_pairs={{0,16},{8,24},{16,0},{24,8},{1,17},{9,25},{17,1},{25,9},{2,18},{10... | collective-permute-start | bytes 3538952 | tf_op jit(solution)/shard_map/ppermute | solution.py:369
  1071.9 122.1 %collective-permute-start.23 = (bf16[2,96,3072]{2,1,0:T(8,128)(2,1)}, bf16[2,96,3072]{2,1,0:T(8,128)(2,1)}, u32[]{:S(2)}, u32[]{:S(2)}) collective-permute-start(bf16[2,96,3072]{2,1,0:T(8,128)(2,1)} %pad_maximum_fusion.6), channel_id=1, source_target_pairs={{0,24},{8,16},{16,8},{24,0},{1,25},{9,17},{17,9},{25,1},{2,26},{10... | collective-permute-start | bytes 3538952 | tf_op jit(solution)/shard_map/ppermute | solution.py:369
  1113.1 128.3 %all-gather.42.cloned.1.call-start = ((), (), s32[]{:S(2)}) async-start(), calls=%async_computation.63 | async-start | bytes 2949120 | tf_op jit(solution)/shard_map/all_gather | solution.py:854
  1113.2 69.6 %collective-permute-start.14 = (bf16[96,3072]{1,0:T(8,128)(2,1)}, bf16[96,3072]{1,0:T(8,128)(2,1)}, u32[]{:S(2)}, u32[]{:S(2)}) collective-permute-start(bf16[96,3072]{1,0:T(8,128)(2,1)} %reduce-scatter.26.cloned.1.call-done), channel_id=1, source_target_pairs={{0,24},{8,16},{16,8},{24,0},{1,25},{9,17},{17,9},{25,1},{2,26},{10... | collective-permute-start | bytes 1769480 | tf_op jit(solution)/shard_map/ppermute | solution.py:369
  1114.7 68.1 %collective-permute-start.13 = (bf16[96,3072]{1,0:T(8,128)(2,1)}, bf16[96,3072]{1,0:T(8,128)(2,1)}, u32[]{:S(2)}, u32[]{:S(2)}) collective-permute-start(bf16[96,3072]{1,0:T(8,128)(2,1)} %reduce-scatter.26.cloned.1.call-done), channel_id=1, source_target_pairs={{0,16},{8,24},{16,0},{24,8},{1,17},{9,25},{17,1},{25,9},{2,18},{10... | collective-permute-start | bytes 1769480 | tf_op jit(solution)/shard_map/ppermute | solution.py:369
  1116.2 66.6 %collective-permute-start.12 = (bf16[96,3072]{1,0:T(8,128)(2,1)}, bf16[96,3072]{1,0:T(8,128)(2,1)}, u32[]{:S(2)}, u32[]{:S(2)}) collective-permute-start(bf16[96,3072]{1,0:T(8,128)(2,1)} %reduce-scatter.26.cloned.1.call-done), channel_id=1, source_target_pairs={{0,8},{8,0},{16,24},{24,16},{1,9},{9,1},{17,25},{25,17},{2,10},{10... | collective-permute-start | bytes 1769480 | tf_op jit(solution)/shard_map/ppermute | solution.py:369
  1196.3 78.0 %collective-permute-start.18 = (bf16[192,4016]{1,0:T(8,128)(2,1)S(1)}, bf16[192,4016]{1,0:T(8,128)(2,1)S(1)}, u32[]{:S(2)}, u32[]{:S(2)}) collective-permute-start(bf16[192,4016]{1,0:T(8,128)(2,1)S(1)} %token_grad.1.refs_0_), channel_id=1, source_target_pairs={{0,8},{8,0},{16,24},{24,16},{1,9},{9,1},{17,25},{25,17},{2,10},{10... | collective-permute-start | bytes 4626440 | tf_op jit(solution)/shard_map/ppermute | solution.py:369
  1198.2 81.6 %collective-permute-start.19 = (bf16[192,4016]{1,0:T(8,128)(2,1)S(1)}, bf16[192,4016]{1,0:T(8,128)(2,1)}, u32[]{:S(2)}, u32[]{:S(2)}) collective-permute-start(bf16[192,4016]{1,0:T(8,128)(2,1)S(1)} %token_grad.1.refs_0_), channel_id=1, source_target_pairs={{0,16},{8,24},{16,0},{24,8},{1,17},{9,25},{17,1},{25,9},{2,18},{10... | collective-permute-start | bytes 4626440 | tf_op jit(solution)/shard_map/ppermute | solution.py:369
  1199.7 81.5 %collective-permute-start.20 = (bf16[192,4016]{1,0:T(8,128)(2,1)S(1)}, bf16[192,4016]{1,0:T(8,128)(2,1)}, u32[]{:S(2)}, u32[]{:S(2)}) collective-permute-start(bf16[192,4016]{1,0:T(8,128)(2,1)S(1)} %token_grad.1.refs_0_), channel_id=1, source_target_pairs={{0,24},{8,16},{16,8},{24,0},{1,25},{9,17},{17,9},{25,1},{2,26},{10... | collective-permute-start | bytes 4626440 | tf_op jit(solution)/shard_map/ppermute | solution.py:369
  (221 other events, 4816.3 us)
Sparse Core Ops, SparseCore 0:
  14.1 56.7 all-gather.23
  73.7 38.8 reduce-scatter.9
  115.6 39.4 reduce-scatter.11
  157.1 50.7 all-gather.27
  210.0 50.5 all-gather.29
  262.6 50.5 all-gather.25
  315.3 50.5 all-gather.31
  368.1 50.6 all-gather.33
  518.4 31.3 reduce-scatter.13
  596.4 55.3 reduce-scatter.15
  655.9 57.6 reduce-scatter.17
  782.8 59.7 reduce-scatter.19
  845.5 53.3 reduce-scatter.21
  901.6 53.3 reduce-scatter.23
  984.7 40.2 all-gather.37
  1027.8 58.0 reduce-scatter.25
  1087.9 37.2 all-gather.35
  1126.9 53.2 all-gather.39
  1182.1 52.0 all-gather.41
